TPU v7x, 32 devices: a whole 2x2x4 slice. The times are simulated.
32 devices in a mesh: dp: 8 (over y, x, core), tensor: 4 (over z).
Axes of the slice: x: 2, y: 2, z: 4, core: 2. Of those that a mesh axis runs over, the one named last changes fastest.
Arguments:
- inputs: bfloat16 [1024, 16, 1024], P('tensor', 'dp'), may hold values from -6 to 6
- cotangent: bfloat16 [1024, 16, 1024], P('tensor', 'dp'), may hold values from -6 to 6
- lengths: int32 [16], replicated, may hold values from 128 to 1024, as said below
- dealing: int32 [16], replicated, may hold values from 0 to 15, as said below
- undealing: int32 [16], replicated, may hold values from 0 to 15, as said below
- query_weight: float32 [1024, 1024], P('dp', 'tensor'), may hold values from -0.1875 to 0.1875
- key_weight: float32 [1024, 1024], P('dp', 'tensor'), may hold values from -0.1875 to 0.1875
- value_weight: float32 [1024, 1024], P('dp', 'tensor'), may hold values from -0.1875 to 0.1875
- output_weight: float32 [1024, 1024], P('tensor', 'dp'), may hold values from -3 to 3
- up_weight: float32 [1024, 4096], P('dp', 'tensor'), may hold values from -0.1875 to 0.1875
- down_weight: float32 [4096, 1024], P('tensor', 'dp'), may hold values from -0.09375 to 0.09375
- query_bias: float32 [1024], P('tensor'), may hold values from -3 to 3
- value_bias: float32 [1024], P('tensor'), may hold values from -3 to 3
- output_bias: float32 [1024], replicated, may hold values from -3 to 3
- up_bias: float32 [4096], P('tensor'), may hold values from -3 to 3
- down_bias: float32 [1024], replicated, may hold values from -3 to 3
- first_gain: float32 [1024], replicated, may hold values from 0.25 to 1.75
- first_shift: float32 [1024], replicated, may hold values from -3 to 3
- second_gain: float32 [1024], replicated, may hold values from 0.25 to 1.75
- second_shift: float32 [1024], replicated, may hold values from -3 to 3
Outputs:
- layer_output: bfloat16 [1024, 16, 1024], P('tensor', 'dp')
- input_grad: bfloat16 [1024, 16, 1024], P('tensor', 'dp')
- query_weight_grad: float32 [1024, 1024], P('dp', 'tensor')
- key_weight_grad: float32 [1024, 1024], P('dp', 'tensor')
- value_weight_grad: float32 [1024, 1024], P('dp', 'tensor')
- output_weight_grad: float32 [1024, 1024], P('tensor', 'dp')
- up_weight_grad: float32 [1024, 4096], P('dp', 'tensor')
- down_weight_grad: float32 [4096, 1024], P('tensor', 'dp')
- query_bias_grad: float32 [1024], P('tensor')
- value_bias_grad: float32 [1024], P('tensor')
- output_bias_grad: float32 [1024], replicated
- up_bias_grad: float32 [4096], P('tensor')
- down_bias_grad: float32 [1024], replicated
- first_gain_grad: float32 [1024], replicated
- first_shift_grad: float32 [1024], replicated
- second_gain_grad: float32 [1024], replicated
- second_shift_grad: float32 [1024], replicated
Inputs may be any that keep to these rules, and one draw needn't show every extreme that they name: `lengths`: 8 or more sequences have exactly 1024 tokens. `dealing`: a permutation of the sequences; dealt slot s belongs to dp index s // 2, and every dp index is dealt a sequence of 1024 tokens. undealing[dealing[s]] = s for every slot s.
All inputs are finite; a program needn't handle non-finite values.
Results may differ from a plain program's by a relative error of at most 0.022.
Values may be sent and summed in bfloat16 or wider, within the bound.
A program may use at most 192 MiB of HBM per device.

v0:
```python
import jax
import jax.numpy as jnp
from jax import lax
from jax.sharding import PartitionSpec as P

HEAD_DIM = 64


def normalize(hidden, norm_gain, norm_shift):
    center = hidden - jnp.mean(hidden, axis=-1, keepdims=True)
    spread = jnp.mean(center * center, axis=-1, keepdims=True)
    return center * lax.rsqrt(spread + 1e-05) * norm_gain + norm_shift


def gelu_exact(values):
    return jax.nn.gelu(values, approximate=False)


def product(left_side, right_side):
    return jnp.dot(left_side, right_side, preferred_element_type=jnp.float32)


def against(left_side, right_side):
    return lax.dot_general(
        left_side, right_side, (((1,), (1,)), ((), ())), preferred_element_type=jnp.float32
    )


def weight_grad(left_side, right_side):
    return lax.dot_general(
        left_side, right_side, (((0,), (0,)), ((), ())), preferred_element_type=jnp.float32
    )


def masked_scores(query_seq, key_seq, length):
    scores = jnp.einsum("qhe,khe->hqk", query_seq, key_seq, preferred_element_type=jnp.float32)
    visible = jnp.arange(key_seq.shape[0]) < length
    return jnp.where(visible[None, None, :], scores, -1000000000.0)


def attend_forward(pieces):
    query_seq, key_seq, value_seq, length = pieces
    scores = masked_scores(query_seq, key_seq, length)
    summit = jnp.max(scores, axis=-1, keepdims=True)
    raised = jnp.exp(scores - summit)
    row_total = jnp.sum(raised, axis=-1, keepdims=True)
    prob_rows = (raised / row_total).astype(jnp.bfloat16)
    attended = jnp.einsum("hqk,khe->qhe", prob_rows, value_seq, preferred_element_type=jnp.float32)
    return (attended.astype(jnp.bfloat16), summit[..., 0] + jnp.log(row_total[..., 0]))


def attend_backward(pieces):
    query_seq, key_seq, value_seq, log_total, length, out_grad = pieces
    scores = masked_scores(query_seq, key_seq, length)
    prob_rows = jnp.exp(scores - log_total[..., None])
    prob_grad = jnp.einsum("qhe,khe->hqk", out_grad, value_seq, preferred_element_type=jnp.float32)
    value_grad = jnp.einsum(
        "hqk,qhe->khe", prob_rows.astype(jnp.bfloat16), out_grad, preferred_element_type=jnp.float32
    )
    inner_sum = jnp.sum(prob_rows * prob_grad, axis=-1, keepdims=True)
    score_grad = (prob_rows * (prob_grad - inner_sum)).astype(jnp.bfloat16)
    query_grad = jnp.einsum("hqk,khe->qhe", score_grad, key_seq, preferred_element_type=jnp.float32)
    key_grad = jnp.einsum("hqk,qhe->khe", score_grad, query_seq, preferred_element_type=jnp.float32)
    return (
        query_grad.astype(jnp.bfloat16),
        key_grad.astype(jnp.bfloat16),
        value_grad.astype(jnp.bfloat16),
    )


def reorder(stacked, new_order):
    pieces = lax.all_to_all(stacked, "dp", split_axis=1, concat_axis=2, tiled=True)
    moved = jnp.take(pieces, new_order, axis=2)
    return lax.all_to_all(moved, "dp", split_axis=2, concat_axis=1, tiled=True)


def spread_rows(values):
    return lax.all_gather(values, "tensor", axis=0, tiled=True)


def spread_grads(values):
    return lax.all_gather(values, "tensor", axis=0, tiled=True)


def fold_rows(row_term, row_count):
    return lax.psum_scatter(
        row_term(jnp.int32(0), lax.axis_size("tensor") * row_count).astype(jnp.bfloat16),
        "tensor",
        scatter_dimension=0,
        tiled=True,
    ).astype(jnp.float32)


def fold_grads(row_term, row_count):
    return lax.psum_scatter(
        row_term(jnp.int32(0), lax.axis_size("tensor") * row_count).astype(jnp.bfloat16),
        "tensor",
        scatter_dimension=0,
        tiled=True,
    ).astype(jnp.float32)


def shards(
    inputs,
    cotangent,
    lengths,
    dealing,
    undealing,
    query_weight,
    key_weight,
    value_weight,
    output_weight,
    up_weight,
    down_weight,
    query_bias,
    value_bias,
    output_bias,
    up_bias,
    down_bias,
    first_gain,
    first_shift,
    second_gain,
    second_shift,
):
    local_rows, slot_count, model_width = inputs.shape
    full_span = local_rows * lax.axis_size("tensor")
    inner_width = query_weight.shape[1]
    heads_here = inner_width // HEAD_DIM
    my_rows = local_rows * slot_count
    my_slots = lax.axis_index("dp") * slot_count + jnp.arange(slot_count, dtype=jnp.int32)
    seq_lengths = jnp.take(lengths, jnp.take(dealing, my_slots))
    positions = lax.axis_index("tensor") * local_rows + jnp.arange(local_rows, dtype=jnp.int32)
    rows_valid = (positions[:, None] < seq_lengths[None, :]).astype(jnp.float32)
    w_query, w_key, w_value, w_out, w_up, w_down = (
        lax.all_gather(query_weight.astype(jnp.bfloat16), "dp", axis=0, tiled=True),
        lax.all_gather(key_weight.astype(jnp.bfloat16), "dp", axis=0, tiled=True),
        lax.all_gather(value_weight.astype(jnp.bfloat16), "dp", axis=0, tiled=True),
        lax.all_gather(output_weight.astype(jnp.bfloat16), "dp", axis=1, tiled=True),
        lax.all_gather(up_weight.astype(jnp.bfloat16), "dp", axis=0, tiled=True),
        lax.all_gather(down_weight.astype(jnp.bfloat16), "dp", axis=1, tiled=True),
    )

    def heads_first(flat_rows):
        return jnp.transpose(
            flat_rows.reshape(full_span, slot_count, heads_here, HEAD_DIM), (1, 0, 2, 3)
        )

    def rows_last(head_rows):
        return jnp.transpose(head_rows, (1, 0, 2, 3)).reshape(full_span * slot_count, inner_width)

    dealt_rows = reorder(inputs[None], dealing)[0]
    full_in = spread_rows(dealt_rows).reshape(full_span * slot_count, model_width)
    query_rows = ((product(full_in, w_query) + query_bias) * 0.125).astype(jnp.bfloat16)
    key_rows = product(full_in, w_key).astype(jnp.bfloat16)
    value_rows = (product(full_in, w_value) + value_bias).astype(jnp.bfloat16)
    query_heads = heads_first(query_rows)
    key_heads = heads_first(key_rows)
    value_heads = heads_first(value_rows)
    attended, log_totals = lax.map(
        attend_forward, (query_heads, key_heads, value_heads, seq_lengths)
    )
    attn_mixed = rows_last(attended)

    def out_term(first_row, row_count):
        return product(attn_mixed, w_out)

    branch = fold_rows(out_term, my_rows).reshape(local_rows, slot_count, model_width) + output_bias
    residual = dealt_rows.astype(jnp.float32) + branch
    hidden_one, back_one = jax.vjp(normalize, residual, first_gain, first_shift)
    full_hidden = spread_rows(hidden_one.astype(jnp.bfloat16)).reshape(
        full_span * slot_count, model_width
    )
    expanded = product(full_hidden, w_up) + up_bias
    activated = gelu_exact(expanded).astype(jnp.bfloat16)

    def down_term(first_row, row_count):
        return product(activated, w_down)

    branch_two = (
        fold_rows(down_term, my_rows).reshape(local_rows, slot_count, model_width) + down_bias
    )
    result, back_two = jax.vjp(normalize, hidden_one + branch_two, second_gain, second_shift)
    w_query, w_key, w_value, w_out, w_up, w_down = (
        lax.all_gather(query_weight.astype(jnp.bfloat16), "dp", axis=0, tiled=True),
        lax.all_gather(key_weight.astype(jnp.bfloat16), "dp", axis=0, tiled=True),
        lax.all_gather(value_weight.astype(jnp.bfloat16), "dp", axis=0, tiled=True),
        lax.all_gather(output_weight.astype(jnp.bfloat16), "dp", axis=1, tiled=True),
        lax.all_gather(up_weight.astype(jnp.bfloat16), "dp", axis=0, tiled=True),
        lax.all_gather(down_weight.astype(jnp.bfloat16), "dp", axis=1, tiled=True),
    )
    seed_grad = cotangent.astype(jnp.float32) * rows_valid[:, :, None]
    grad_two, gain_two_grad, shift_two_grad = back_two(seed_grad)
    full_mlp_grad = spread_grads(grad_two.astype(jnp.bfloat16)).reshape(
        full_span * slot_count, model_width
    )
    down_bias_grad = jnp.sum(full_mlp_grad, axis=0, dtype=jnp.float32)
    down_grad = weight_grad(activated, full_mlp_grad)
    act_grad = against(full_mlp_grad, w_down)
    gelu_pull = jax.vjp(gelu_exact, expanded)[1]
    expand_grad = gelu_pull(act_grad)[0].astype(jnp.bfloat16)
    up_bias_grad = jnp.sum(expand_grad, axis=0, dtype=jnp.float32)
    up_grad = weight_grad(full_hidden, expand_grad)

    def up_back_term(first_row, row_count):
        return against(expand_grad, w_up)

    hidden_grad = grad_two + fold_grads(up_back_term, my_rows).reshape(
        local_rows, slot_count, model_width
    )
    grad_one, gain_one_grad, shift_one_grad = back_one(hidden_grad)
    full_attn_grad = spread_grads(grad_one.astype(jnp.bfloat16)).reshape(
        full_span * slot_count, model_width
    )
    output_bias_grad = jnp.sum(full_attn_grad, axis=0, dtype=jnp.float32)
    out_grad = weight_grad(attn_mixed, full_attn_grad)
    mixed_grad = against(full_attn_grad, w_out).astype(jnp.bfloat16)
    query_grad_heads, key_grad_heads, value_grad_heads = lax.map(
        attend_backward,
        (query_heads, key_heads, value_heads, log_totals, seq_lengths, heads_first(mixed_grad)),
    )
    query_grad = rows_last(query_grad_heads) * 0.125
    key_grad = rows_last(key_grad_heads)
    value_grad = rows_last(value_grad_heads)
    query_bias_grad = jnp.sum(query_grad, axis=0, dtype=jnp.float32)
    value_bias_grad = jnp.sum(value_grad, axis=0, dtype=jnp.float32)
    query_w_grad = weight_grad(full_in, query_grad)
    key_w_grad = weight_grad(full_in, key_grad)
    value_w_grad = weight_grad(full_in, value_grad)

    def input_term(first_row, row_count):
        total_term = against(query_grad, w_query)
        total_term = total_term + against(key_grad, w_key)
        return total_term + against(value_grad, w_value)

    dealt_grad = grad_one + fold_grads(input_term, my_rows).reshape(
        local_rows, slot_count, model_width
    )
    query_sum, key_sum, value_sum, out_sum, up_sum, down_sum = (
        lax.psum_scatter(query_w_grad, "dp", scatter_dimension=0, tiled=True),
        lax.psum_scatter(key_w_grad, "dp", scatter_dimension=0, tiled=True),
        lax.psum_scatter(value_w_grad, "dp", scatter_dimension=0, tiled=True),
        lax.psum_scatter(out_grad, "dp", scatter_dimension=1, tiled=True),
        lax.psum_scatter(up_grad, "dp", scatter_dimension=0, tiled=True),
        lax.psum_scatter(down_grad, "dp", scatter_dimension=1, tiled=True),
    )
    bias_sums = lax.psum(
        (query_bias_grad, value_bias_grad, output_bias_grad, up_bias_grad, down_bias_grad), "dp"
    )
    norm_sums = lax.psum(
        (gain_one_grad, shift_one_grad, gain_two_grad, shift_two_grad), ("dp", "tensor")
    )
    returned = reorder(
        jnp.stack([result.astype(jnp.bfloat16), dealt_grad.astype(jnp.bfloat16)]), undealing
    )
    return (
        returned[0],
        returned[1],
        query_sum,
        key_sum,
        value_sum,
        out_sum,
        up_sum,
        down_sum,
        bias_sums[0],
        bias_sums[1],
        bias_sums[2],
        bias_sums[3],
        bias_sums[4],
        norm_sums[0],
        norm_sums[1],
        norm_sums[2],
        norm_sums[3],
    )


def solution(mesh):
    placed = (
        P("tensor", "dp", None),
        P("tensor", "dp", None),
        P(),
        P(),
        P(),
        P("dp", "tensor"),
        P("dp", "tensor"),
        P("dp", "tensor"),
        P("tensor", "dp"),
        P("dp", "tensor"),
        P("tensor", "dp"),
        P("tensor"),
        P("tensor"),
        P(),
        P("tensor"),
        P(),
        P(),
        P(),
        P(),
        P(),
    )
    return jax.shard_map(
        shards,
        mesh=mesh,
        in_specs=placed,
        out_specs=(
            P("tensor", "dp", None),
            P("tensor", "dp", None),
            P("dp", "tensor"),
            P("dp", "tensor"),
            P("dp", "tensor"),
            P("tensor", "dp"),
            P("dp", "tensor"),
            P("tensor", "dp"),
            P("tensor"),
            P("tensor"),
            P(),
            P("tensor"),
            P(),
            P(),
            P(),
            P(),
            P(),
        ),
        check_vma=False,
    )
```

profile of v0, /device:TPU:0, one launch (start us, length us, event | category | flops | bytes accessed | tf_op | source)
XLA Modules:
  0.0 1335.6 jit_solution(13870563835975874723)
XLA Ops:
  7.2 5.2 all-to-all-start
  13.8 14.0 %all-to-all-done = bf16[1,256,2,1024]{3,2,0,1:T(2,128)(2,1)S(1)} async-done(((bf16[1,256,2,1024]{3,2,0,1:T(2,128)(2,1)}), bf16[1,256,2,1024]{3,2,0,1:T(2,128)(2,1)S(1)}, u32[]{:S(2)}, u32[]{:S(2)}) %all-to-all-start) | async-done | bytes 1048608 | tf_op jit(solution)/shard_map/all_to_all | solution.py:72
  29.0 17.9 %all_to_all.66 = bf16[1,32,16,1024]{3,1,0,2:T(8,128)(2,1)S(1)} all-to-all(bf16[1,32,16,1024]{3,1,0,2:T(8,128)(2,1)S(1)} %fusion.84), channel_id=1, replica_groups=mesh['dp'=8,'tensor'=4] {'dp'}, dimensions={2} | all-to-all | bytes 2097152 | tf_op jit(solution)/shard_map/all_to_all | solution.py:74
  49.7 10.0 all_gather.40
  59.7 9.8 all_gather.37
  69.5 8.9 all_gather.39
  78.4 9.9 all_gather.38
  88.3 40.1 %all-gather.7.cloned.1.call-done = bf16[1024,2,1024]{2,0,1:T(8,128)(2,1)} async-done(((bf16[256,2,1024]{2,0,1:T(8,128)(2,1)}), bf16[1024,2,1024]{2,0,1:T(8,128)(2,1)}) %all-gather.7.cloned.1.call-update) | async-done | bytes 4194320 | tf_op jit(solution)/shard_map/all_gather | solution.py:78
  128.4 8.5 copy.195
  137.0 7.2 reshape.385
  160.7 4.4 fusion.61
  165.1 4.5 reshape.386
  173.5 24.3 %while.26 = (s32[]{:T(128)}, bf16[2,1024,4,64]{1,3,2,0:T(8,128)(2,1)}, f32[2,4,1024]{2,1,0:T(4,128)S(1)}, bf16[2,1024,4,64]{1,3,2,0:T(8,128)(2,1)S(1)}, s32[2]{0...) while((s32[]{:T(128)}, ...), condition=%wide.region_3.5_spmd, body=%wide.region_0.4_spmd.sunk | while | flops 1111749632 | bytes 60954792 | solution.py:159
  197.8 4.3 copy.199
  202.1 4.3 reshape.389
  206.4 4.6 convolution_convert_fusion.2
  211.1 75.4 %reduce-scatter.11.cloned.1.call-done = bf16[512,1024]{1,0:T(8,128)(2,1)} async-done(((bf16[2048,1024]{1,0:T(8,128)(2,1)}), bf16[512,1024]{1,0:T(8,128)(2,1)}) %reduce-scatter.11.cloned.1.call-update) | async-done | bytes 1048592 | tf_op jit(solution)/shard_map/reduce_scatter | solution.py:86
  298.5 4.4 fusion.82
  306.6 77.7 %all-gather.9.cloned.1.call-done = bf16[1024,2,1024]{2,0,1:T(8,128)(2,1)} async-done(((bf16[256,2,1024]{2,0,1:T(8,128)(2,1)}), bf16[1024,2,1024]{2,0,1:T(8,128)(2,1)}) %all-gather.9.cloned.1.call-update) | async-done | bytes 4194320 | tf_op jit(solution)/shard_map/all_gather | solution.py:78
  384.3 8.5 copy.206
  392.8 7.4 reshape.393
  400.2 13.0 all-gather.11.cloned.1.call-done
  413.2 26.3 %multiply_convert_fusion.1 = (bf16[2048,1024]{1,0:T(8,128)(2,1)}, f32[2048,1024]{1,0:T(8,128)}, f32[2048,1024]{1,0:T(8,128)}) fusion(f32[1024]{0:T(1024)S(1)} %copy-done.68, bf16[2048,1024]{1,0:T(8,128)(2,1)} %reshape.393, bf16[1024,1024]{1,0:T(8,128)(2,1)} %all-gather.11.cloned.1.call-done), kind=kOutput, calls=%fused_computation.70 | convolution fusion | flops 4433379328 | bytes 27267072 | tf_op jit(solution)/shard_map/dot_general | solution.py:20
  443.3 9.4 convolution_convert_fusion.4
  452.9 76.8 %reduce-scatter.13.cloned.1.call-done = bf16[512,1024]{1,0:T(8,128)(2,1)} async-done(((bf16[2048,1024]{1,0:T(8,128)(2,1)}), bf16[512,1024]{1,0:T(8,128)(2,1)}) %reduce-scatter.13.cloned.1.call-update) | async-done | bytes 1048592 | tf_op jit(solution)/shard_map/reduce_scatter | solution.py:86
  533.2 3.8 fusion.90
  537.2 3.9 multiply_reduce_fusion.5
  544.5 4.0 multiply_reduce_fusion.4
  552.4 81.0 %all-gather.15.cloned.1.call-done = bf16[1024,2,1024]{2,0,1:T(8,128)(2,1)} async-done(((bf16[256,2,1024]{2,0,1:T(8,128)(2,1)}), bf16[1024,2,1024]{2,0,1:T(8,128)(2,1)}) %all-gather.15.cloned.1.call-update) | async-done | bytes 4194320 | tf_op jit(solution)/shard_map/all_gather | solution.py:82
  633.4 8.6 copy.215
  641.9 7.2 reshape.397
  649.1 14.0 %convert_reduce_fusion.1 = (f32[1024]{0:T(1024)}, bf16[2048,1024]{1,0:T(8,128)(2,1)S(1)}) fusion(f32[2048,1024]{1,0:T(8,128)} %get-tuple-element.325, f32[2048,1024]{1,0:T(8,128)} %get-tuple-element.338, f32[1024]{0:T(1024)S(1)} %copy-done.68, bf16[2048,1024]{1,0:T(8,128)(2,1)} %reshape.397, bf16[1024,1024]{1,0:T(8,128)(2,1)} %all-gather.13.cloned.1.call-done), kind=kOutput, calls=%fused_computation.66 | convolution fusion | flops 4330617856 | bytes 27271168 | tf_op jit(solution)/shard_map/dot_general | solution.py:24
  665.1 6.3 convolution_convert_fusion.3
  671.7 75.2 %reduce-scatter.15.cloned.1.call-done = bf16[512,1024]{1,0:T(8,128)(2,1)} async-done(((bf16[2048,1024]{1,0:T(8,128)(2,1)}), bf16[512,1024]{1,0:T(8,128)(2,1)}) %reduce-scatter.15.cloned.1.call-update) | async-done | bytes 1048592 | tf_op jit(solution)/shard_map/reduce_scatter | solution.py:95
  750.3 4.6 multiply_reduce_fusion.2
  758.1 81.4 %all-gather.17.cloned.1.call-done = bf16[1024,2,1024]{2,0,1:T(8,128)(2,1)} async-done(((bf16[256,2,1024]{2,0,1:T(8,128)(2,1)}), bf16[1024,2,1024]{2,0,1:T(8,128)(2,1)}) %all-gather.17.cloned.1.call-update) | async-done | bytes 4194320 | tf_op jit(solution)/shard_map/all_gather | solution.py:82
  839.5 8.5 copy.217
  848.0 7.2 reshape.400
  855.2 4.4 convolution_convert_fusion.5
  859.6 4.5 reshape.401
  864.1 4.1 copy.220
  871.5 67.3 %while.27 = (s32[]{:T(128)}, bf16[2,1024,4,64]{1,3,2,0:T(8,128)(2,1)}, bf16[2,1024,4,64]{1,3,2,0:T(8,128)(2,1)}, bf16[2,1024,4,64]{1,3,2,0:T(8,128)(2,1)}, bf16[...) while((s32[]{:T(128)}, ...), condition=%wide.region_17.19_spmd, body=%wide.region_15.18_spmd.sunk | while | flops 2735469568 | bytes 139584720 | solution.py:217
  875.4 5.8 fusion.171
  881.2 9.5 multiply_reduce_fusion.8
  890.7 8.5 multiply_convert_fusion.3
  908.9 5.9 fusion.171
  914.8 9.5 multiply_reduce_fusion.8
  924.2 8.5 multiply_convert_fusion.3
  942.8 3.9 mul.286
  966.7 10.0 fusion.102
  976.8 10.0 fusion.103
  988.0 4.4 fusion.101
  999.2 4.5 fusion.72
  1006.1 35.9 %reduce-scatter.17.cloned.1.call-done = bf16[512,1024]{1,0:T(8,128)(2,1)} async-done(((bf16[2048,1024]{1,0:T(8,128)(2,1)}), bf16[512,1024]{1,0:T(8,128)(2,1)}) %reduce-scatter.17.cloned.1.call-update) | async-done | bytes 1048592 | tf_op jit(solution)/shard_map/reduce_scatter | solution.py:95
  1055.0 4.9 fusion.99
  1060.0 31.8 %all-to-all-done.2 = bf16[2,256,2,1024]{3,2,0,1:T(2,128)(2,1)S(1)} async-done(((bf16[2,256,2,1024]{3,2,0,1:T(2,128)(2,1)}), bf16[2,256,2,1024]{3,2,0,1:T(2,128)(2,1)S(1)}, u32[]{:S(2)}, u32[]{:S(2)}) %all-to-all-start.2) | async-done | bytes 2097184 | tf_op jit(solution)/shard_map/all_to_all | solution.py:72
  1097.9 4.4 all-to-all-start.3
  1102.6 4.5 fusion.100
  1110.2 52.4 %all-reduce = (f32[1024]{0:T(1024)}, f32[1024]{0:T(1024)}, f32[1024]{0:T(1024)}, f32[1024]{0:T(1024)}) all-reduce(f32[1024]{0:T(1024)S(1)} %copy-done.61, f32[1024]{0:T(1024)S(1)} %copy-done.62, f32[1024]{0:T(1024)S(1)} %copy-done.63, f32[1024]{0:T(1024)S(1)} %copy-done.64), channel_id=1, replica_groups=mesh['dp'=8,'tensor'=4] {'dp','tensor'}, use_global_device_ids=true, to_apply=%region_36.38 | all-reduce | flops 4096 | bytes 32768 | tf_op jit(solution)/shard_map/psum | solution.py:249
  1166.1 24.3 %all-reduce.1 = (f32[256]{0:T(256)}, f32[256]{0:T(256)}, f32[1024]{0:T(1024)}, f32[1024]{0:T(1024)}, f32[1024]{0:T(1024)}) all-reduce(f32[256]{0:T(256)S(1)} %reduce_sum.216, f32[256]{0:T(256)S(1)} %reduce_sum.218, f32[1024]{0:T(1024)S(1)} %convert_reduce_fusion.2, ...), channel_id=1, replica_groups=mesh['dp'=8,'tensor'=4] {'dp'}, use_global_device_ids=true, to_apply=%region_26.28 | all-reduce | flops 3584 | bytes 28672 | tf_op jit(solution)/shard_map/psum | solution.py:246
  1196.8 13.1 reduce-scatter.25.cloned.1.call-done
  1209.9 39.6 %reduce-scatter.19.cloned.1.call-done = f32[128,256]{1,0:T(8,128)} async-done(((f32[1024,256]{1,0:T(8,128)}), f32[128,256]{1,0:T(8,128)}) %reduce-scatter.19.cloned.1.call-update) | async-done | bytes 131088 | tf_op jit(solution)/shard_map/reduce_scatter | solution.py:239
  1249.5 39.6 %reduce-scatter.21.cloned.1.call-done = f32[128,256]{1,0:T(8,128)} async-done(((f32[1024,256]{1,0:T(8,128)}), f32[128,256]{1,0:T(8,128)}) %reduce-scatter.21.cloned.1.call-update) | async-done | bytes 131088 | tf_op jit(solution)/shard_map/reduce_scatter | solution.py:240
  1289.1 39.6 %reduce-scatter.23.cloned.1.call-done = f32[128,256]{1,0:T(8,128)} async-done(((f32[1024,256]{1,0:T(8,128)}), f32[128,256]{1,0:T(8,128)}) %reduce-scatter.23.cloned.1.call-update) | async-done | bytes 131088 | tf_op jit(solution)/shard_map/reduce_scatter | solution.py:241
  (312 shorter events, 177.8 us)
Async XLA Ops:
  7.2 41.8 %copy-start = (s32[16]{0:T(128)S(1)}, s32[16]{0:T(128)}, u32[]{:S(2)}) copy-start(s32[16]{0:T(128)} %param.28) | copy-start | bytes 196
  7.2 20.6 %all-to-all-start = ((bf16[1,256,2,1024]{3,2,0,1:T(2,128)(2,1)}), bf16[1,256,2,1024]{3,2,0,1:T(2,128)(2,1)S(1)}, u32[]{:S(2)}, u32[]{:S(2)}) async-start(bf16[1,256,2,1024]{3,2,0,1:T(2,128)(2,1)} %bitcast.237), calls=%async_computation | async-start | bytes 2097152 | tf_op jit(solution)/shard_map/all_to_all | solution.py:72
  12.4 116.0 %all-gather.7.cloned.1.call-start = ((), (), s32[]{:S(2)}) async-start(), calls=%async_computation.14 | async-start | bytes 5242880 | tf_op jit(solution)/shard_map/all_gather | solution.py:78
  28.8 19.4 %copy-start.2 = (s32[16]{0:T(128)S(1)}, s32[16]{0:T(128)}, u32[]{:S(2)}) copy-start(s32[16]{0:T(128)} %param.29) | copy-start | bytes 196
  28.8 20.1 %copy-start.41 = (f32[128,256]{1,0:T(8,128)S(1)}, f32[128,256]{1,0:T(8,128)}, u32[]{:S(2)}) copy-start(f32[128,256]{1,0:T(8,128)} %param.31) | copy-start | bytes 393220
  28.8 20.1 %copy-start.42 = (f32[128,256]{1,0:T(8,128)S(1)}, f32[128,256]{1,0:T(8,128)}, u32[]{:S(2)}) copy-start(f32[128,256]{1,0:T(8,128)} %param.32) | copy-start | bytes 393220
  28.8 20.1 %copy-start.43 = (f32[128,256]{1,0:T(8,128)S(1)}, f32[128,256]{1,0:T(8,128)}, u32[]{:S(2)}) copy-start(f32[128,256]{1,0:T(8,128)} %param.33) | copy-start | bytes 393220
  28.8 20.1 %copy-start.44 = (f32[256,128]{1,0:T(8,128)S(1)}, f32[256,128]{1,0:T(8,128)}, u32[]{:S(2)}) copy-start(f32[256,128]{1,0:T(8,128)} %param.34) | copy-start | bytes 393220
  46.9 90.0 %copy-start.3 = (bf16[1,32,16,1024]{3,1,0,2:T(8,128)(2,1)}, bf16[1,32,16,1024]{3,1,0,2:T(8,128)(2,1)S(1)}, u32[]{:S(2)}) copy-start(bf16[1,32,16,1024]{3,1,0,2:T(8,128)(2,1)S(1)} %all_to_all.66) | copy-start | bytes 3145732
  48.1 238.3 %reduce-scatter.11.cloned.1.call-start = ((), (), s32[]{:S(2)}) async-start(), calls=%async_computation.15 | async-start | bytes 5242880 | tf_op jit(solution)/shard_map/reduce_scatter | solution.py:86
  69.5 91.2 %copy-start.31 = (bf16[1024,256]{1,0:T(8,128)(2,1)}, bf16[1024,256]{1,0:T(8,128)(2,1)S(1)}, u32[]{:S(2)}) copy-start(bf16[1024,256]{1,0:T(8,128)(2,1)S(1)} %all_gather.37) | copy-start | bytes 1572868
  78.4 65.8 %copy-start.33 = (bf16[1024,256]{1,0:T(8,128)(2,1)}, bf16[1024,256]{1,0:T(8,128)(2,1)S(1)}, u32[]{:S(2)}) copy-start(bf16[1024,256]{1,0:T(8,128)(2,1)S(1)} %all_gather.39) | copy-start | bytes 1572868
  88.3 64.1 %copy-start.34 = (bf16[1024,256]{1,0:T(8,128)(2,1)}, bf16[1024,256]{1,0:T(8,128)(2,1)S(1)}, u32[]{:S(2)}) copy-start(bf16[1024,256]{1,0:T(8,128)(2,1)S(1)} %all_gather.38) | copy-start | bytes 1572868
  197.8 8.6 copy-start.11
  211.0 79.2 %copy-start.4 = (bf16[1,32,16,1024]{3,1,0,2:T(8,128)(2,1)S(1)}, bf16[1,32,16,1024]{3,1,0,2:T(8,128)(2,1)}, u32[]{:S(2)}) copy-start(bf16[1,32,16,1024]{3,1,0,2:T(8,128)(2,1)} %copy-done.3) | copy-start | bytes 3145732
  211.0 79.2 %copy-start.39 = (f32[1024]{0:T(1024)S(1)}, f32[1024]{0:T(1024)}, u32[]{:S(2)}) copy-start(f32[1024]{0:T(1024)} %param.39) | copy-start | bytes 12292
  211.0 173.3 %all-gather.9.cloned.1.call-start = ((), (), s32[]{:S(2)}) async-start(), calls=%async_computation.16 | async-start | bytes 5242880 | tf_op jit(solution)/shard_map/all_gather | solution.py:78
  290.2 8.2 copy-start.37
  290.2 8.2 copy-start.47
  292.6 10.2 copy-start.55
  295.1 459.9 %copy-start.49 = (f32[256,2]{0,1:T(2,128)}, f32[256,2]{0,1:T(2,128)S(1)}, u32[]{:S(2)}) copy-start(f32[256,2]{0,1:T(2,128)S(1)} %rsqrt.23) | copy-start | bytes 6148
  302.8 110.4 %all-gather.11.cloned.1.call-start = ((), (), s32[]{:S(2)}) async-start(), calls=%async_computation.17 | async-start | bytes 2359296 | tf_op jit(solution)/shard_map/all_gather | solution.py:139
  304.7 138.6 %all-gather.13.cloned.1.call-start = ((), (), s32[]{:S(2)}) async-start(), calls=%async_computation.18 | async-start | bytes 2359296 | tf_op jit(solution)/shard_map/all_gather | solution.py:140
  306.5 223.1 %reduce-scatter.13.cloned.1.call-start = ((), (), s32[]{:S(2)}) async-start(), calls=%async_computation.19 | async-start | bytes 5242880 | tf_op jit(solution)/shard_map/reduce_scatter | solution.py:86
  392.8 20.4 %copy-start.68 = (f32[1024]{0:T(1024)S(1)}, f32[1024]{0:T(1024)}, u32[]{:S(2)}) copy-start(f32[1024]{0:T(1024)} %param.40) | copy-start | bytes 12292
  452.7 80.5 %copy-start.51 = (f32[1024]{0:T(1024)S(1)}, f32[1024]{0:T(1024)}, u32[]{:S(2)}) copy-start(f32[1024]{0:T(1024)} %param.41) | copy-start | bytes 12292
  452.8 180.6 %all-gather.15.cloned.1.call-start = ((), (), s32[]{:S(2)}) async-start(), calls=%async_computation.20 | async-start | bytes 5242880 | tf_op jit(solution)/shard_map/all_gather | solution.py:82
  537.2 7.3 copy-start.57
  537.2 7.3 copy-start.45
  548.6 201.7 %copy-start.53 = (f32[256,2]{0,1:T(2,128)}, f32[256,2]{0,1:T(2,128)S(1)}, u32[]{:S(2)}) copy-start(f32[256,2]{0,1:T(2,128)S(1)} %get-tuple-element.337) | copy-start | bytes 6148
  551.9 195.0 %reduce-scatter.15.cloned.1.call-start = ((), (), s32[]{:S(2)}) async-start(), calls=%async_computation.21 | async-start | bytes 5242880 | tf_op jit(solution)/shard_map/reduce_scatter | solution.py:95
  649.1 16.0 %copy-start.67 = (bf16[1024,1024]{1,0:T(8,128)(2,1)S(1)}, bf16[1024,1024]{1,0:T(8,128)(2,1)}, u32[]{:S(2)}) copy-start(bf16[1024,1024]{1,0:T(8,128)(2,1)} %all-gather.11.cloned.1.call-done) | copy-start | bytes 6291460
  671.5 168.0 %all-gather.17.cloned.1.call-start = ((), (), s32[]{:S(2)}) async-start(), calls=%async_computation.22 | async-start | bytes 5242880 | tf_op jit(solution)/shard_map/all_gather | solution.py:82
  758.1 283.9 %reduce-scatter.17.cloned.1.call-start = ((), (), s32[]{:S(2)}) async-start(), calls=%async_computation.23 | async-start | bytes 5242880 | tf_op jit(solution)/shard_map/reduce_scatter | solution.py:95
  848.0 7.2 copy-start.36
  938.8 7.9 copy-start.27
  942.8 10.0 copy-start.14
  946.7 15.0 %copy-start.23 = (bf16[2048,256]{1,0:T(8,128)(2,1)}, bf16[2048,256]{1,0:T(8,128)(2,1)S(1)}, u32[]{:S(2)}) copy-start(bf16[2048,256]{1,0:T(8,128)(2,1)S(1)} %mul.286) | copy-start | bytes 3145732
  952.8 8.9 copy-start.21
  966.5 230.2 %reduce-scatter.27.cloned.1.call-start = ((), (), s32[]{:S(2)}) async-start(), calls=%async_computation.28 | async-start | bytes 4718592 | tf_op jit(solution)/shard_map/reduce_scatter | solution.py:243
  976.8 220.0 %reduce-scatter.29.cloned.1.call-start = ((), (), s32[]{:S(2)}) async-start(), calls=%async_computation.29 | async-start | bytes 4718592 | tf_op jit(solution)/shard_map/reduce_scatter | solution.py:244
  986.9 7.6 copy-start.12
  986.9 223.0 %reduce-scatter.25.cloned.1.call-start = ((), (), s32[]{:S(2)}) async-start(), calls=%async_computation.27 | async-start | bytes 1179648 | tf_op jit(solution)/shard_map/reduce_scatter | solution.py:242
  992.5 6.6 copy-start.38
  992.5 6.6 copy-start.40
  992.5 6.6 copy-start.46
  992.5 6.6 copy-start.48
  992.6 6.6 copy-start.50
  992.6 6.6 copy-start.52
  992.6 6.6 copy-start.54
  992.6 6.6 copy-start.56
  992.6 6.6 copy-start.58
  992.6 256.9 %reduce-scatter.19.cloned.1.call-start = ((), (), s32[]{:S(2)}) async-start(), calls=%async_computation.24 | async-start | bytes 1179648 | tf_op jit(solution)/shard_map/reduce_scatter | solution.py:239
  1006.0 39.3 %copy-start.9 = (f32[256,2,1024]{2,0,1:T(8,128)S(1)}, f32[256,2,1024]{2,0,1:T(8,128)}, u32[]{:S(2)}) copy-start(f32[256,2,1024]{2,0,1:T(8,128)} %copy-done.8) | copy-start | bytes 6291460
  1006.0 39.3 %copy-start.60 = (f32[256,2]{0,1:T(2,128)S(1)}, f32[256,2]{0,1:T(2,128)}, u32[]{:S(2)}) copy-start(f32[256,2]{0,1:T(2,128)} %copy-done.59) | copy-start | bytes 6148
  1047.8 7.2 copy-start.22
  1051.3 40.5 %all-to-all-start.2 = ((bf16[2,256,2,1024]{3,2,0,1:T(2,128)(2,1)}), bf16[2,256,2,1024]{3,2,0,1:T(2,128)(2,1)S(1)}, u32[]{:S(2)}, u32[]{:S(2)}) async-start(bf16[2,256,2,1024]{3,2,0,1:T(2,128)(2,1)} %copy.226), calls=%async_computation.6 | async-start | bytes 4194304 | tf_op jit(solution)/shard_map/all_to_all | solution.py:72
  1054.9 234.2 %reduce-scatter.21.cloned.1.call-start = ((), (), s32[]{:S(2)}) async-start(), calls=%async_computation.25 | async-start | bytes 1179648 | tf_op jit(solution)/shard_map/reduce_scatter | solution.py:240
  1097.9 92.5 %all-to-all-start.3 = ((bf16[2,32,16,1024]{3,1,0,2:T(8,128)(2,1)}), bf16[2,32,16,1024]{3,1,0,2:T(8,128)(2,1)}, u32[]{:S(2)}, u32[]{:S(2)}) async-start(bf16[2,32,16,1024]{3,1,0,2:T(8,128)(2,1)} %select_bitcast_fusion), calls=%async_computation.7 | async-start | bytes 4194304 | tf_op jit(solution)/shard_map/all_to_all | solution.py:74
  1102.3 226.5 %reduce-scatter.23.cloned.1.call-start = ((), (), s32[]{:S(2)}) async-start(), calls=%async_computation.26 | async-start | bytes 1179648 | tf_op jit(solution)/shard_map/reduce_scatter | solution.py:241
  1107.1 55.5 %copy-start.15 = (bf16[2,1024,4,64]{1,3,2,0:T(8,128)(2,1)S(1)}, bf16[2,1024,4,64]{1,3,2,0:T(8,128)(2,1)}, u32[]{:S(2)}) copy-start(bf16[2,1024,4,64]{1,3,2,0:T(8,128)(2,1)} %get-tuple-element.114) | copy-start | bytes 3145732
  1107.1 55.5 %copy-start.18 = (bf16[2,1024,4,64]{1,3,2,0:T(8,128)(2,1)S(1)}, bf16[2,1024,4,64]{1,3,2,0:T(8,128)(2,1)}, u32[]{:S(2)}) copy-start(bf16[2,1024,4,64]{1,3,2,0:T(8,128)(2,1)} %get-tuple-element.112) | copy-start | bytes 3145732
  1110.2 55.9 %copy-start.66 = (f32[1024]{0:T(1024)S(1)}, f32[1024]{0:T(1024)}, u32[]{:S(2)}) copy-start(f32[1024]{0:T(1024)} %get-tuple-element.317) | copy-start | bytes 12292
  1192.5 136.3 %copy-start.1 = (s32[16]{0:T(128)S(1)}, s32[16]{0:T(128)}, u32[]{:S(2)}) copy-start(s32[16]{0:T(128)} %param.28) | copy-start | bytes 196
  (32 other events, 104.1 us)
Sparse Core Ops, SparseCore 0:
  48.3 80.1 all-gather.6
  211.1 75.2 reduce-scatter.10
  303.0 81.2 all-gather.8
  386.7 26.4 all-gather.10
  415.1 28.1 all-gather.12
  452.9 76.7 reduce-scatter.12
  552.0 81.2 all-gather.14
  671.6 75.2 reduce-scatter.14
  758.2 81.2 all-gather.16
  966.6 75.2 reduce-scatter.16
  1045.9 61.6 reduce-scatter.26
  1111.8 58.2 reduce-scatter.28
  1173.8 35.9 reduce-scatter.24
  1213.5 35.9 reduce-scatter.18
  1253.1 35.9 reduce-scatter.20
  1292.7 35.9 reduce-scatter.22
where the time goes:
time: 1340 us
  waiting for transfers between devices  738 us (55%)
  matrix products  178 us (13%)
  local copies, waits for them, and re-layouts  176 us (13%)
  blocking collectives  133 us (10%)
  other arithmetic  78.6 us (6%)
  between operations  15.2 us (1%)
  starting transfers between devices  15.1 us (1%)
    all_gather x2, waiting for transfers between devices, spread_grads(): return lax.all_gather(values, 'tensor', axis=0, tiled=True)  162 us
    reduce_scatter x2, waiting for transfers between devices, fold_rows(): lax.psum_scatter(row_term(jnp.int32(0), lax.axis_size('tensor') * row_cou...  152 us
    all_gather x2, waiting for transfers between devices, spread_rows(): return lax.all_gather(values, 'tensor', axis=0, tiled=True)  118 us
    reduce_scatter x2, waiting for transfers between devices, fold_grads(): lax.psum_scatter(row_term(jnp.int32(0), lax.axis_size('tensor') * row_cou...  111 us
    psum x1, blocking collectives, shards(): lax.psum((gain_one_grad, shift_one_grad, gain_two_grad, shift_two_grad),...  52.4 us
    dot_general x6, matrix products, product(): return jnp.dot(left_side, right_side, preferred_element_type=jnp.float32)  51.6 us
    all_to_all x2, waiting for transfers between devices, reorder(): lax.all_to_all(stacked, 'dp', split_axis=1, concat_axis=2, tiled=True)  45.9 us
    reduce_scatter x1, waiting for transfers between devices, shards(): lax.psum_scatter(query_w_grad, 'dp', scatter_dimension=0, tiled=True)  39.6 us
  transfers between devices with their start and end apart: 19, of which 16 were waited for; matrix products, arithmetic and copies ran while one was open for 9% of the time, Pallas kernels for 0%

commit v1 on v0

v1 whole, which is shorter than its diff:
```python
import functools

import jax
import jax.numpy as jnp
from jax import lax
from jax.experimental import pallas as pl
from jax.experimental.pallas import tpu as pltpu
from jax.sharding import PartitionSpec as P

HEAD_DIM = 64
KINDS = 3
MESH = pl.DeviceIdType.MESH
VMEM_LIMIT = 60 << 20
BF = jnp.bfloat16
F32 = jnp.float32


def flip(index, bit):
    unit = 1 << bit
    return index + unit * (1 - 2 * lax.rem(lax.div(index, unit), 2))


def orders(bits):
    return (tuple(range(bits)), tuple(reversed(range(bits))))


def relative(chip, order, code):
    for place, bit in enumerate(order):
        if code >> place & 1:
            chip = flip(chip, bit)
    return chip


def place():
    d, t = lax.axis_index("dp"), lax.axis_index("tensor")
    return d, t, lax.div(d, 2), lax.rem(d, 2)


def greet(n_dp, n_tensor):
    d, t, _, _ = place()
    barrier = pltpu.get_barrier_semaphore()
    me = d * n_tensor + t
    count = n_dp * n_tensor

    def one(step, carry):
        other = lax.rem(me + step, count)
        pl.semaphore_signal(
            barrier,
            inc=1,
            device_id=(lax.div(other, n_tensor), lax.rem(other, n_tensor)),
            device_id_type=MESH,
        )
        return carry

    lax.fori_loop(1, count, one, 0)
    pl.semaphore_wait(barrier, count - 1)


def remote(src, dst, ssem, rsem, device):
    return pltpu.make_async_remote_copy(
        src_ref=src,
        dst_ref=dst,
        send_sem=ssem,
        recv_sem=rsem,
        device_id=device,
        device_id_type=MESH,
    )


def landed(ref, sem):
    pltpu.make_async_copy(ref, ref, sem).wait()


def send_or_keep(mine, src, dst, ssem, rsem, device):
    @pl.when(mine)
    def _():
        pltpu.make_async_copy(src, dst, rsem).start()

    @pl.when(jnp.logical_not(mine))
    def _():
        remote(src, dst, ssem, rsem, device).start()


def sent(mine, src, ssem):
    @pl.when(jnp.logical_not(mine))
    def _():
        landed(src, ssem)


def gather_kernel(
    n_dp,
    n_tensor,
    undealing,
    x_ref,
    cot_ref,
    shard_ref,
    xl_ref,
    cl_ref,
    full_ref,
    c_one,
    c_two,
    x_s,
    x_r,
    c1_s,
    c1_r,
    c2_s,
    c2_r,
    own_sem,
    z_s,
    z_r,
    xy_s,
    xy_r,
    sib_s,
    sib_r,
):
    d, t, chip, core = place()
    chips = n_dp // 2
    bits = chips.bit_length() - 1
    half_t = n_tensor // 2
    rows, cols = shard_ref.shape[1:]
    half_cols = cols // 2
    prow, pcol = c_one.shape[2:]
    n_col = cot_ref.shape[2] // pcol
    greet(n_dp, n_tensor)

    def block(k, tt, who, half):
        return full_ref.at[k, tt, who, core, :, pl.ds(half * half_cols, half_cols)]

    for k in range(KINDS):
        pltpu.make_async_copy(shard_ref.at[k], full_ref.at[k, t, chip, core], own_sem.at[k]).start()
        for step in range(1, n_tensor):
            remote(
                shard_ref.at[k],
                full_ref.at[k, t, chip, core],
                z_s.at[k, step],
                z_r.at[k, t],
                (d, lax.rem(t + step, n_tensor)),
            ).start()
    for s in range(2):
        send_or_keep(
            (lax.div(t, half_t) == core) & (2 * core + s == t),
            x_ref.at[s],
            xl_ref.at[lax.rem(t, half_t)],
            x_s.at[s],
            x_r.at[lax.rem(t, half_t)],
            (2 * chip + lax.div(t, half_t), 2 * core + s),
        )

    def piece(who):
        return cot_ref.at[
            :,
            pl.ds(pl.multiple_of(lax.div(who, n_col) * prow, prow), prow),
            pl.ds(pl.multiple_of(lax.rem(who, n_col) * pcol, pcol), pcol),
        ]

    pltpu.make_async_copy(piece(d), c_one.at[d], c1_r.at[0]).start()
    for step in range(1, n_dp):
        who = lax.rem(d + step, n_dp)
        remote(piece(who), c_one.at[d], c1_s.at[step], c1_r.at[step], (who, t)).start()

    def forward(k, tt, half, code):
        order = orders(bits)[half]
        chip_here = relative(chip, order, code)
        ref = block(k, tt, chip_here, half)
        for s in range(code.bit_length(), bits):
            target = code | 1 << s
            remote(
                ref,
                ref,
                xy_s.at[k, tt, half, target],
                xy_r.at[k, tt, half, target],
                (2 * flip(chip, order[s]) + core, t),
            ).start()
        remote(
            ref, ref, sib_s.at[k, tt, half, code], sib_r.at[k, tt, half, code], (d + 1 - 2 * core, t)
        ).start()

    def cot_second():
        for step in range(n_dp):
            landed(c_one.at[0], c1_r.at[step])
        count = 2 * n_dp
        for step in range(count):
            seq = lax.rem(4 * chip + step, count)
            slot = undealing[seq]
            c_two[seq] = c_one[lax.div(slot, 2), lax.rem(slot, 2)]
            goal = 2 * lax.div(seq, 4) + lax.div(t, half_t)
            send_or_keep(
                (goal == d) & (lax.rem(seq, 4) == t),
                c_two.at[seq],
                cl_ref.at[lax.rem(t, half_t), d],
                c2_s.at[step],
                c2_r.at[lax.rem(t, half_t), d],
                (goal, lax.rem(seq, 4)),
            )

    for k in range(KINDS):
        landed(shard_ref.at[k], own_sem.at[k])
        for step in range(n_tensor):
            tt = lax.rem(t + step, n_tensor)
            if step:
                landed(shard_ref.at[k], z_r.at[k, tt])
            for half in range(2):
                forward(k, tt, half, 0)
        if k == 0:
            cot_second()
        for code in range(1, chips):
            for step in range(n_tensor):
                tt = lax.rem(t + step, n_tensor)
                for half in range(2):
                    landed(block(k, tt, chip, half), xy_r.at[k, tt, half, code])
                    forward(k, tt, half, code)

    for k in range(KINDS):
        for step in range(1, n_tensor):
            landed(shard_ref.at[k], z_s.at[k, step])
        for step in range(n_tensor):
            tt = lax.rem(t + step, n_tensor)
            for half in range(2):
                for code in range(chips):
                    ref = block(k, tt, chip, half)
                    landed(ref, sib_r.at[k, tt, half, code])
                    landed(ref, sib_s.at[k, tt, half, code])
                    if code:
                        landed(ref, xy_s.at[k, tt, half, code])
    for s in range(2):
        sent((lax.div(t, half_t) == core) & (2 * core + s == t), x_ref.at[s], x_s.at[s])
        landed(x_ref.at[s], x_r.at[s])
    for step in range(1, n_dp):
        landed(c_one.at[0], c1_s.at[step])
    for step in range(2 * n_dp):
        seq = lax.rem(4 * chip + step, 2 * n_dp)
        goal = 2 * lax.div(seq, 4) + lax.div(t, half_t)
        sent((goal == d) & (lax.rem(seq, 4) == t), c_two.at[0], c2_s.at[step])
    for q in range(half_t):
        for who in range(n_dp):
            landed(c_two.at[0], c2_r.at[q, who])


def gather(n_dp, n_tensor, undealing, x_in, cot_in, shard):
    slots, span, width = x_in.shape
    rows, cols = shard.shape[1:]
    chips = n_dp // 2
    n_pos = min(n_dp, span // 16)
    prow, pcol = span // n_pos, width // (n_dp // n_pos)
    dma = pltpu.SemaphoreType.DMA
    any_space = pl.BlockSpec(memory_space=pl.ANY)
    return pl.pallas_call(
        functools.partial(gather_kernel, n_dp, n_tensor),
        out_shape=(
            jax.ShapeDtypeStruct((2, span, width), BF),
            jax.ShapeDtypeStruct((2, n_dp, prow, pcol), BF),
            jax.ShapeDtypeStruct((KINDS, n_tensor, chips, 2, rows, cols), BF),
        ),
        in_specs=[pl.BlockSpec(memory_space=pltpu.SMEM), any_space, any_space, any_space],
        out_specs=(any_space, any_space, any_space),
        scratch_shapes=[
            pltpu.VMEM((n_dp, slots, prow, pcol), BF),
            pltpu.VMEM((2 * n_dp, prow, pcol), BF),
            dma((2,)),
            dma((2,)),
            dma((n_dp,)),
            dma((n_dp,)),
            dma((2 * n_dp,)),
            dma((n_tensor // 2, n_dp)),
            dma((KINDS,)),
            dma((KINDS, n_tensor)),
            dma((KINDS, n_tensor)),
            dma((KINDS, n_tensor, 2, chips)),
            dma((KINDS, n_tensor, 2, chips)),
            dma((KINDS, n_tensor, 2, chips)),
            dma((KINDS, n_tensor, 2, chips)),
        ],
        compiler_params=pltpu.CompilerParams(
            collective_id=0, has_side_effects=True, vmem_limit_bytes=VMEM_LIMIT
        ),
        name="gather_all",
    )(undealing, x_in, cot_in, shard)


def scatter_kernel(
    n_dp,
    n_tensor,
    grad_ref,
    bias_ref,
    y_ref,
    sum_ref,
    bias_out,
    y_out,
    from_core,
    held,
    from_chip,
    from_z,
    bias_in,
    y_s,
    y_r,
    b_s,
    b_r,
    bo_s,
    bo_r,
    own_sem,
    core_s,
    core_r,
    xy_s,
    xy_r,
    z_s,
    z_r,
    out_sem,
):
    d, t, chip, core = place()
    chips = n_dp // 2
    bits = chips.bit_length() - 1
    half_t = n_tensor // 2
    count = n_dp * n_tensor
    me = d * n_tensor + t
    rows, cols = grad_ref.shape[4:]
    half_cols = cols // 2
    pieces = KINDS * n_tensor
    greet(n_dp, n_tensor)

    def at(index):
        k = lax.div(index, n_tensor)
        return k, lax.rem(t + lax.rem(index, n_tensor), n_tensor)

    def begin(index, carry):
        k, tt = at(index)
        remote(
            grad_ref.at[k, tt, :, 1 - core],
            from_core.at[index],
            core_s.at[index],
            core_r.at[index],
            (d + 1 - 2 * core, t),
        ).start()
        pltpu.make_async_copy(grad_ref.at[k, tt, :, core], held.at[index], own_sem.at[index]).start()
        return carry

    lax.fori_loop(0, pieces, begin, 0)

    for a in range(y_ref.shape[0]):
        for q in range(2):
            send_or_keep(
                (lax.div(t, half_t) == core) & (2 * core + q == t),
                y_ref.at[a, q],
                y_out.at[a, lax.rem(t, half_t)],
                y_s.at[a, q],
                y_r.at[a, lax.rem(t, half_t)],
                (2 * chip + lax.div(t, half_t), 2 * core + q),
            )

    def device(index):
        return (lax.div(index, n_tensor), lax.rem(index, n_tensor))

    def bias_begin(step, carry):
        other = lax.rem(me + step, count)
        remote(
            bias_ref.at[other], bias_in.at[step], b_s.at[step], b_r.at[step], device(other)
        ).start()
        return carry

    lax.fori_loop(1, count, bias_begin, 0)
    pltpu.make_async_copy(bias_ref.at[me], bias_in.at[0], b_r.at[0]).start()

    def bias_middle():
        def arrive(step, total):
            landed(bias_in.at[0], b_r.at[step])
            return total + bias_in[step]

        total = lax.fori_loop(0, count, arrive, jnp.zeros(bias_in.shape[1:], F32))

        def leave(step, carry):
            landed(bias_in.at[0], b_s.at[step])
            return carry

        lax.fori_loop(1, count, leave, 0)
        bias_in[0] = total
        pltpu.make_async_copy(bias_in.at[0], bias_out.at[me], bo_r.at[0]).start()

        def spread(step, carry):
            other = lax.rem(me + step, count)
            remote(
                bias_in.at[0], bias_out.at[me], bo_s.at[step], bo_r.at[step], device(other)
            ).start()
            return carry

        lax.fori_loop(1, count, spread, 0)

    def bias_end():
        def last(step, carry):
            landed(bias_in.at[0], bo_r.at[step])
            return carry

        lax.fori_loop(0, count, last, 0)

        def gone(step, carry):
            landed(bias_in.at[0], bo_s.at[step])
            return carry

        lax.fori_loop(1, count, gone, 0)

    def pass_on(index, s):
        for half in range(2):
            order = orders(bits)[half]
            for code in range(1 << s, 2 << s):
                remote(
                    held.at[index, relative(chip, order, code), :, pl.ds(half * half_cols, half_cols)],
                    from_chip.at[index, half, code - 1],
                    xy_s.at[index, half, code],
                    xy_r.at[index, half, code],
                    (2 * flip(chip, order[s]) + core, t),
                ).start()

    def take_in(index, s):
        for half in range(2):
            order = orders(bits)[half]
            for code in range(1 << s, 2 << s):
                landed(from_chip.at[0, 0, 0], xy_r.at[index, half, code])
                spot = held.at[
                    index,
                    relative(chip, order, code - (1 << s)),
                    :,
                    pl.ds(half * half_cols, half_cols),
                ]
                spot[...] = (
                    spot[...].astype(F32) + from_chip[index, half, code - 1].astype(F32)
                ).astype(BF)

    def first(index):
        landed(held.at[0], own_sem.at[index])
        landed(held.at[0], core_r.at[index])

        def add(c, carry):
            held[index, c] = (held[index, c].astype(F32) + from_core[index, c].astype(F32)).astype(BF)
            return carry

        lax.fori_loop(0, chips, add, 0)
        if bits:
            pass_on(index, bits - 1)

    def finish(index):
        k, tt = at(index)
        step = lax.rem(index, n_tensor)

        @pl.when(step > 0)
        def _():
            remote(
                held.at[index, chip],
                from_z.at[k, step],
                z_s.at[k, step],
                z_r.at[k, step],
                (d, tt),
            ).start()

    def turn(it, carry):
        for stage in range(bits + 1):
            index = it - stage

            @pl.when((index >= 0) & (index < pieces))
            def _(stage=stage, index=index):
                if stage == 0:
                    first(index)
                else:
                    take_in(index, bits - stage)
                    if stage < bits:
                        pass_on(index, bits - stage - 1)
                if stage == bits:
                    finish(index)

        return carry

    lax.fori_loop(0, pieces + bits, turn, 0)
    bias_middle()

    for k in range(KINDS):
        total = held[k * n_tensor, chip].astype(F32)
        for step in range(1, n_tensor):
            landed(from_z.at[0, 0], z_r.at[k, step])
            total = total + from_z[k, step].astype(F32)
        sum_ref[k] = total

    def close(index, carry):
        landed(held.at[0], core_s.at[index])
        for half in range(2):
            for code in range(1, chips):
                landed(from_chip.at[0, 0, 0], xy_s.at[index, half, code])
        return carry

    lax.fori_loop(0, pieces, close, 0)
    for k in range(KINDS):
        for step in range(1, n_tensor):
            landed(from_z.at[0, 0], z_s.at[k, step])
    for a in range(y_ref.shape[0]):
        for q in range(2):
            sent((lax.div(t, half_t) == core) & (2 * core + q == t), y_ref.at[a, q], y_s.at[a, q])
            landed(y_ref.at[a, q], y_r.at[a, q])
    bias_end()


def scatter(n_dp, n_tensor, grads, bias, outs):
    rows, cols = grads.shape[4:]
    chips = n_dp // 2
    pieces = KINDS * n_tensor
    count = n_dp * n_tensor
    dma = pltpu.SemaphoreType.DMA
    any_space = pl.BlockSpec(memory_space=pl.ANY)
    return pl.pallas_call(
        functools.partial(scatter_kernel, n_dp, n_tensor),
        out_shape=(
            jax.ShapeDtypeStruct((KINDS, rows, cols), F32),
            jax.ShapeDtypeStruct(bias.shape, F32),
            jax.ShapeDtypeStruct(outs.shape, BF),
        ),
        in_specs=[any_space] * 3,
        out_specs=(pl.BlockSpec(memory_space=pltpu.VMEM), any_space, any_space),
        scratch_shapes=[
            pltpu.VMEM((pieces, chips, rows, cols), BF),
            pltpu.VMEM((pieces, chips, rows, cols), BF),
            pltpu.VMEM((pieces, 2, chips - 1, rows, cols // 2), BF),
            pltpu.VMEM((KINDS, n_tensor, rows, cols), BF),
            pltpu.VMEM(bias.shape, F32),
            dma((outs.shape[0], 2)),
            dma((outs.shape[0], 2)),
            dma((count,)),
            dma((count,)),
            dma((count,)),
            dma((count,)),
            dma((pieces,)),
            dma((pieces,)),
            dma((pieces,)),
            dma((pieces, 2, chips)),
            dma((pieces, 2, chips)),
            dma((KINDS, n_tensor)),
            dma((KINDS, n_tensor)),
            dma((1,)),
        ],
        compiler_params=pltpu.CompilerParams(
            collective_id=1, has_side_effects=True, vmem_limit_bytes=VMEM_LIMIT
        ),
        name="scatter_all",
    )(grads, bias, outs)


def normalize(hidden, norm_gain, norm_shift):
    center = hidden - jnp.mean(hidden, axis=-1, keepdims=True)
    spread = jnp.mean(center * center, axis=-1, keepdims=True)
    return center * lax.rsqrt(spread + 1e-05) * norm_gain + norm_shift


def gelu_exact(values):
    return jax.nn.gelu(values, approximate=False)


def mm(spec, left, right):
    return jnp.einsum(spec, left, right, preferred_element_type=F32)


def shards(
    n_dp,
    n_tensor,
    inputs,
    cotangent,
    lengths,
    dealing,
    undealing,
    query_weight,
    key_weight,
    value_weight,
    output_weight,
    up_weight,
    down_weight,
    query_bias,
    value_bias,
    output_bias,
    up_bias,
    down_bias,
    first_gain,
    first_shift,
    second_gain,
    second_shift,
):
    span, slots, width = inputs.shape
    group = query_weight.shape[1]
    units = up_weight.shape[1]
    half = span * n_tensor // 2
    d, t, chip, core = place()
    length = lengths[2 * slots * chip + t]
    positions = core * half + jnp.arange(half)
    valid = (positions < length).astype(F32)

    shard = jnp.stack(
        [
            jnp.concatenate([query_weight, key_weight, value_weight, output_weight.T], axis=1),
            up_weight,
            down_weight.T,
        ]
    ).astype(BF)
    x_loc, cot_loc, full = gather(
        n_dp,
        n_tensor,
        undealing,
        jnp.transpose(inputs, (1, 0, 2)),
        jnp.transpose(cotangent, (1, 0, 2)),
        shard,
    )
    n_col = width // cot_loc.shape[3]
    cot = cot_loc.reshape(2, n_dp // n_col, n_col, *cot_loc.shape[2:])
    cot = jnp.transpose(cot, (0, 1, 3, 2, 4)).reshape(half, width)
    x = x_loc.reshape(half, width)
    full = full.reshape(KINDS, n_tensor, width, 4 * group)
    w_qkv = full[0][:, :, : 3 * group].reshape(n_tensor, width, 3, group)
    w_out = full[0][:, :, 3 * group :]
    w_up, w_down = full[1], full[2]

    bias_q = lax.all_gather(query_bias, "tensor", axis=0)
    bias_v = lax.all_gather(value_bias, "tensor", axis=0)
    bias_u = lax.all_gather(up_bias, "tensor", axis=0)

    def swap(values):
        other = lax.ppermute(values, "dp", [(i, i ^ 1) for i in range(n_dp)])
        return other

    def whole(values):
        other = swap(values)
        return jnp.concatenate(
            [jnp.where(core == 0, values, other), jnp.where(core == 0, other, values)], axis=0
        )

    qkv = mm("nm,tmjc->jntc", x, w_qkv)
    query = ((qkv[0] + bias_q) * 0.125).astype(BF)
    key = qkv[1].astype(BF)
    value = (qkv[2] + bias_v).astype(BF)
    heads = n_tensor * group // HEAD_DIM

    def split(values):
        return jnp.transpose(values.reshape(-1, heads, HEAD_DIM), (1, 0, 2))

    def join(values):
        return jnp.transpose(values, (1, 0, 2)).reshape(-1, n_tensor, group)

    q_h, k_h, v_h = split(query), split(whole(key)), split(whole(value))
    visible = jnp.arange(2 * half) < length

    def attend(one):
        q_one, k_one, v_one = one
        scores = jnp.where(visible, mm("qe,ke->qk", q_one, k_one), -1000000000.0)
        summit = jnp.max(scores, axis=-1, keepdims=True)
        raised = jnp.exp(scores - summit)
        total = jnp.sum(raised, axis=-1, keepdims=True)
        out = mm("qk,ke->qe", (raised / total).astype(BF), v_one)
        return out.astype(BF), (summit + jnp.log(total))[:, 0]

    attended, log_total = lax.map(attend, (q_h, k_h, v_h))
    mixed = join(attended)
    branch = mm("ntc,tmc->nm", mixed, w_out) + output_bias
    residual = x.astype(F32) + branch
    hidden_one, back_one = jax.vjp(normalize, residual, first_gain, first_shift)
    hidden_low = hidden_one.astype(BF)
    expanded = mm("nm,tmf->ntf", hidden_low, w_up) + bias_u
    activated = gelu_exact(expanded).astype(BF)
    branch_two = mm("ntf,tmf->nm", activated, w_down) + down_bias
    result, back_two = jax.vjp(normalize, hidden_one + branch_two, second_gain, second_shift)

    seed = cot.astype(F32) * valid[:, None]
    grad_two, gain_two, shift_two = back_two(seed)
    mlp_grad = grad_two.astype(BF)
    down_bias_grad = jnp.sum(mlp_grad, axis=0, dtype=F32)
    down_grad = mm("nm,ntf->tmf", mlp_grad, activated).astype(BF)
    act_grad = mm("nm,tmf->ntf", mlp_grad, w_down)
    expand_grad = jax.vjp(gelu_exact, expanded)[1](act_grad)[0].astype(BF)
    up_bias_grad = jnp.sum(expand_grad, axis=0, dtype=F32)
    up_grad = mm("nm,ntf->tmf", hidden_low, expand_grad).astype(BF)
    hidden_grad = grad_two + mm("ntf,tmf->nm", expand_grad, w_up)
    grad_one, gain_one, shift_one = back_one(hidden_grad)
    attn_grad = grad_one.astype(BF)
    output_bias_grad = jnp.sum(attn_grad, axis=0, dtype=F32)
    out_grad = mm("nm,ntc->tmc", attn_grad, mixed).astype(BF)
    mixed_grad = split(mm("nm,tmc->ntc", attn_grad, w_out).astype(BF))

    def attend_back(one):
        q_one, k_one, v_one, total, o_one = one
        scores = jnp.where(visible, mm("qe,ke->qk", q_one, k_one), -1000000000.0)
        probs = jnp.exp(scores - total[:, None])
        prob_grad = mm("qe,ke->qk", o_one, v_one)
        value_g = mm("qk,qe->ke", probs.astype(BF), o_one)
        inner = jnp.sum(probs * prob_grad, axis=-1, keepdims=True)
        score_grad = (probs * (prob_grad - inner)).astype(BF)
        query_g = mm("qk,ke->qe", score_grad, k_one)
        key_g = mm("qk,qe->ke", score_grad, q_one)
        return query_g.astype(BF), key_g.astype(BF), value_g.astype(BF)

    query_g, key_g, value_g = lax.map(attend_back, (q_h, k_h, v_h, log_total, mixed_grad))

    def collect(values):
        parts = join(values).reshape(2, half, n_tensor, group)
        own = jnp.where(core == 0, parts[0], parts[1])
        other = jnp.where(core == 0, parts[1], parts[0])
        return (own.astype(F32) + swap(other).astype(F32)).astype(BF)

    query_grad = join(query_g) * jnp.asarray(0.125, BF)
    qkv_grad = jnp.stack([query_grad, collect(key_g), collect(value_g)])
    query_bias_grad = jnp.sum(qkv_grad[0], axis=0, dtype=F32)
    value_bias_grad = jnp.sum(qkv_grad[2], axis=0, dtype=F32)
    qkv_w_grad = mm("nm,jntc->tmjc", x, qkv_grad).astype(BF)
    dealt = grad_one + mm("jntc,tmjc->nm", qkv_grad, w_qkv)

    grads = jnp.stack(
        [
            jnp.concatenate([qkv_w_grad.reshape(n_tensor, width, 3 * group), out_grad], axis=2),
            up_grad,
            down_grad,
        ]
    ).reshape(KINDS, n_tensor, n_dp // 2, 2, width // n_dp, 4 * group)
    parts = (
        query_bias_grad,
        value_bias_grad,
        output_bias_grad,
        up_bias_grad,
        down_bias_grad,
        gain_one,
        shift_one,
        gain_two,
        shift_two,
    )
    count = n_dp * n_tensor
    flat = jnp.concatenate([part.reshape(-1) for part in parts])
    flat = jnp.pad(flat.reshape(count, -1), ((0, 0), (0, 1024 - flat.shape[0] // count)))
    outs = jnp.stack([result.astype(BF), dealt.astype(BF)]).reshape(2, 2, span, width)
    sums, bias_sum, returned = scatter(n_dp, n_tensor, grads, flat.reshape(count, 8, 128), outs)

    returned = jnp.transpose(returned, (0, 2, 1, 3))
    used = sum(part.size for part in parts) // count
    bias_sum = bias_sum.reshape(count, 1024)[:, :used].reshape(-1)
    sizes = [part.size for part in parts]
    ends = [sum(sizes[: i + 1]) for i in range(len(sizes))]
    pieces = [bias_sum[end - size : end] for end, size in zip(ends, sizes)]

    def mine(values, size):
        return lax.dynamic_slice(values, (t * size,), (size,))

    return (
        returned[0],
        returned[1],
        sums[0][:, :group],
        sums[0][:, group : 2 * group],
        sums[0][:, 2 * group : 3 * group],
        sums[0][:, 3 * group :].T,
        sums[1],
        sums[2].T,
        mine(pieces[0], group),
        mine(pieces[1], group),
        pieces[2],
        mine(pieces[3], units),
        pieces[4],
        pieces[5],
        pieces[6],
        pieces[7],
        pieces[8],
    )


def solution(mesh):
    tokens = P("tensor", "dp", None)
    rows, columns = P("dp", "tensor"), P("tensor", "dp")
    split, copied = P("tensor"), P()
    return jax.shard_map(
        functools.partial(shards, mesh.shape["dp"], mesh.shape["tensor"]),
        mesh=mesh,
        in_specs=(
            (tokens, tokens, copied, copied, copied)
            + (rows, rows, rows, columns, rows, columns)
            + (split, split, copied, split, copied, copied, copied, copied, copied)
        ),
        out_specs=(
            (tokens, tokens, rows, rows, rows, columns, rows, columns)
            + (split, split, copied, split, copied, copied, copied, copied, copied)
        ),
        check_vma=False,
    )
```

time: 1340 us -> 844 us (0.63)
  waiting for transfers between devices: 738 us -> 0.01 us
  Pallas kernels: 0 us -> 278 us
  matrix products: 178 us -> 269 us
  blocking collectives: 133 us -> 45.4 us
  local copies, waits for them, and re-layouts: 176 us -> 131 us
  other arithmetic: 78.6 us -> 103 us
  starting transfers between devices: 15.1 us -> 0.51 us
  between operations: 15.2 us -> 1.69 us
    reduce_scatter x10 -> x0, waiting for transfers between devices: 395 us -> none  [the longest x2 152 us: fold_rows(): lax.psum_scatter(row_term(jnp.int32(0), lax.axis_size('tensor') * row_cou...]
    all_gather x6 -> x0, waiting for transfers between devices: 297 us -> none  [the longest x2 162 us: spread_grads(): return lax.all_gather(values, 'tensor', axis=0, tiled=True)]
    pallas_call x0 -> x2, Pallas kernels: none -> 278 us  [the longest x1 144 us: gather(): pl.pallas_call(functools.partial(gather_kernel, n_dp, n_tensor), out_shap...]
    dot_general x32 -> x124, matrix products: 178 us -> 269 us  [mm(): return jnp.einsum(spec, left, right, preferred_element_type=F32)]
    psum x2 -> x0, blocking collectives: 76.7 us -> none  [the longest x1 52.4 us: shards(): lax.psum((gain_one_grad, shift_one_grad, gain_two_grad, shift_two_grad),...]
    reshape x19 -> x6, local copies, waits for them, and re-layouts: 78.2 us -> 7.48 us  [the longest x3 7.39 us: split(): return jnp.transpose(values.reshape(-1, heads, HEAD_DIM), (1, 0, 2))]
    all_to_all x3 -> x0, waiting for transfers between devices: 45.9 us -> none  [the longest x2 45.9 us: reorder(): lax.all_to_all(stacked, 'dp', split_axis=1, concat_axis=2, tiled=True)]
    all_gather x4 -> x1, local copies, waits for them, and re-layouts: 34.1 us -> 0.01 us  [shards(): bias_u = lax.all_gather(up_bias, 'tensor', axis=0)]
  transfers between devices with their start and end apart: 19 -> 4, of which waited for: 16 -> 0; matrix products, arithmetic and copies ran while one was open for 9% -> 4% of each run, Pallas kernels for 0% -> 0%
where the time goes in v1:
time: 844 us; the launch traced here: 831 us
  Pallas kernels  278 us (33%)
  matrix products  269 us (32%)
  local copies, waits for them, and re-layouts  131 us (16%)
  other arithmetic  103 us (12%)
  blocking collectives  45.4 us (5%)
    dot_general x124, matrix products, mm(): return jnp.einsum(spec, left, right, preferred_element_type=F32)  269 us
    pallas_call x1, Pallas kernels, gather(): pl.pallas_call(functools.partial(gather_kernel, n_dp, n_tensor), out_shap...  144 us
    pallas_call x1, Pallas kernels, scatter(): pl.pallas_call(functools.partial(scatter_kernel, n_dp, n_tensor), out_sha...  135 us
    concatenate x2, local copies, waits for them, and re-layouts, shards(): jnp.concatenate([qkv_w_grad.reshape(n_tensor, width, 3 * group), out_grad...  30.7 us
    all_gather x1, blocking collectives, shards(): bias_v = lax.all_gather(value_bias, 'tensor', axis=0)  24.5 us
    dynamic_update_slice x16, local copies, waits for them, and re-layouts, shards(): attended, log_total = lax.map(attend, (q_h, k_h, v_h))  21.5 us
    lt x32, other arithmetic, shards(): visible = jnp.arange(2 * half) < length  20.8 us
    convert_element_type x1, other arithmetic, shards(): activated = gelu_exact(expanded).astype(BF)  20.4 us
  transfers between devices with their start and end apart: 4, of which 0 were waited for; matrix products, arithmetic and copies ran while one was open for 4% of the time, Pallas kernels for 0%

profile of v1, /device:TPU:0, one launch (start us, length us, event | category | flops | bytes accessed | tf_op | source)
XLA Modules:
  0.0 830.7 jit_solution(14481271012299006428)
XLA Ops:
  6.7 3.5 copy_bitcast_fusion
  11.2 143.8 %gather_all.1 = (bf16[2,256,1024]{2,1,0:T(8,128)(2,1)}, bf16[2,8,32,1024]{3,2,1,0:T(8,128)(2,1)}, bf16[3,4,4,2,128,1024]{5,4,3,2,1,0:T(8,128)(2,1)}) custom-call(s32[16]{0:T(128)} %undealing.1, bf16[2,256,1024]{2,1,0:T(8,128)(2,1)} %get-tuple-element.312.x_ref, bf16[2,256,1024]{2,1,0:T(8,128)(2,1)} %get-tuple-element.311.cot_ref, ...), custom_call_target="tpu_custom_call" | custom-call | tf_op jit(solution)/shard_map/gather_all/pallas_call | solution.py:247
  155.0 14.2 %fusion.96 = (bf16[1,4,4,2,128,1024]{5,4,3,2,1,0:T(8,128)(2,1)}, bf16[1,4,4,2,128,1024]{5,4,3,2,1,0:T(8,128)(2,1)}, bf16[1,4,4,2,128,1024]{5,4,3,2,1,0:T(8,128)(2,1)S(1)}) fusion(bf16[3,4,4,2,128,1024]{5,4,3,2,1,0:T(8,128)(2,1)} %get-tuple-element.115), kind=kLoop, calls=%fused_computation.196 | loop fusion | bytes 50331648 | tf_op jit(solution)/shard_map/slice | solution.py:610
  169.2 3.2 copy-done
  172.4 3.3 slice.140
  175.7 8.7 %copy.85 = bf16[4,1024,768]{1,2,0:T(8,128)(2,1)} copy(bf16[4,1024,768]{2,1,0:T(8,128)(2,1)} %slice.140) | data formatting | bytes 12582912 | tf_op jit(solution)/shard_map/slice | solution.py:608
  184.4 24.5 %all-gather.4 = f32[4,1,256]{2,1,0:T(1,128)S(1)} all-gather(f32[1,1,256]{2,1,0:T(1,128)S(1)} %bitcast.313), channel_id=3, replica_groups=mesh['dp'=8,'tensor'=4] {'tensor'}, dimensions={0}, use_global_device_ids=true | all-gather | bytes 5120 | tf_op jit(solution)/shard_map/all_gather | solution.py:613
  209.0 5.6 convolution_bitcast_fusion
  220.7 2.7 copy.86
  223.5 7.6 all-gather.3
  231.2 13.3 %all-gather.2 = f32[4096]{0:T(1024)S(1)} all-gather(f32[1024]{0:T(1024)S(1)} %copy-done.19), channel_id=4, replica_groups=mesh['dp'=8,'tensor'=4] {'tensor'}, dimensions={0}, use_global_device_ids=true | all-gather | bytes 20480 | tf_op jit(solution)/shard_map/all_gather | solution.py:614
  245.1 4.1 fusion.53
  249.2 2.2 broadcast_select_fusion.5
  251.7 3.2 copy.89
  254.8 2.3 broadcast_select_fusion.7
  257.4 3.2 copy.88
  261.7 101.0 %while.28 = (s32[]{:T(128)}, bf16[16,512,64]{1,2,0:T(8,128)(2,1)}, f32[16,512]{1,0:T(8,128)}, bf16[16,512,64]{2,1,0:T(8,128)(2,1)}, bf16[16,1024,64]{2,1,0:T(8,1...) while((s32[]{:T(128)}, bf16[16,512,64]{1,2,0:T(8,128)(2,1)}, ...), condition=%wide.region_3.4_spmd.clone, body=%wide.region_0.3_spmd.clone.sunk | while | flops 138969600 | bytes 7039077 | solution.py:650
  265.8 2.2 fusion.134
  272.1 2.2 fusion.134
  278.4 2.2 fusion.134
  284.7 2.2 fusion.134
  291.0 2.2 fusion.134
  297.3 2.2 fusion.134
  303.6 2.2 fusion.134
  309.9 2.2 fusion.134
  316.2 2.2 fusion.134
  322.5 2.2 fusion.134
  328.9 2.2 fusion.134
  335.2 2.2 fusion.134
  341.5 2.2 fusion.134
  347.8 2.2 fusion.134
  354.1 2.2 fusion.134
  360.4 2.2 fusion.134
  362.7 3.6 fusion.98
  366.6 9.1 %fusion.62 = (u8[512,1024]{1,0:T(8,128)(4,1)S(1)}, u8[512,1024]{1,0:T(8,128)(4,1)S(1)}, f32[512,4,1024]{2,0,1:T(8,128)S(1)}) fusion(f32[4,1024]{1,0:T(4,128)S(1)} %reshape.263, bf16[4,1024,1024]{2,1,0:T(8,128)(2,1)} %bitcast.279, f32[512,1024]{1,0:T(8,128)S(1)} %get-tuple-element.304, f32[1024]{0:T(1024)S(1)} %copy-done.29, f32[1024]{0:T(1024)S(1)} %copy-done.21, ...), kind=kOutput, calls=%fused_computation.125 | convolution fusion | flops 4325900288 | bytes 19951616 | tf_op jit(solution)/shard_map/nm,tmf->ntf/dot_general | solution.py:552
  375.7 20.4 %multiply_convert_fusion.1 = (bf16[512,4,1024]{2,0,1:T(8,128)(2,1)}, f32[512,4,1024]{2,0,1:T(8,128)S(1)}) fusion(f32[512,4,1024]{2,0,1:T(8,128)S(1)} %get-tuple-element.305, f32[4,1024]{1,0:T(4,128)S(1)} %reshape.263, u8[512,1024]{1,0:T(8,128)(4,1)S(1)} %get-tuple-element.218, u8[512,1024]{1,0:T(8,128)(4,1)S(1)} %get-tuple-element.217), kind=kLoop, calls=%fused_computation.67 | loop fusion | flops 148897792 | bytes 22036480 | tf_op jit(solution)/shard_map/convert_element_type | solution.py:657
  396.1 9.9 %fusion.99 = (f32[512]{0:T(512)S(1)}, f32[512,1024]{1,0:T(8,128)S(1)}) fusion(f32[1024]{0:T(1024)S(1)} %copy-done.28, bf16[512,4,1024]{2,0,1:T(8,128)(2,1)} %get-tuple-element.266, bf16[4,1024,1024]{2,1,0:T(8,128)(2,1)} %bitcast.281, f32[1024]{0:T(1024)S(1)} %copy-done.29, f32[1024]{0:T(1024)S(1)} %copy-done.21, f32[512]{0:T(512)S(1)} %fusion.86, ...), kind=kOutput, calls=%fused_computation.199 | convolution fusion | flops 4298636800 | bytes 16795648 | tf_op jit(solution)/shard_map/ntf,tmf->nm/dot_general | solution.py:552
  407.3 2.0 fusion.94
  410.6 13.2 %convert_reduce_fusion = (f32[4,1024]{1,0:T(4,128)}, bf16[512,4,1024]{2,0,1:T(8,128)(2,1)}) fusion(f32[512,4,1024]{2,0,1:T(8,128)S(1)} %get-tuple-element.267, bf16[4,1024,1024]{2,1,0:T(8,128)(2,1)} %bitcast.282, bf16[512,1024]{1,0:T(8,128)(2,1)S(1)} %get-tuple-element.259, f32[512,4,1024]{2,0,1:T(8,128)S(1)} %get-tuple-element.305, f32[4,1024]{1,0:T(4,128)S(1)} %reshape.263), kind=kOutput, calls=%fused_computation.65 | convolution fusion | flops 4330614784 | bytes 30441472 | tf_op jit(solution)/shard_map/nm,tmf->ntf/dot_general | solution.py:552
  423.8 10.4 %multiply_reduce_fusion.3 = (f32[1024]{0:T(1024)S(1)}, f32[512]{0:T(512)S(1)}, f32[1024]{0:T(1024)S(1)}, f32[512,1024]{1,0:T(8,128)S(1)}) fusion(f32[512,1024]{1,0:T(8,128)S(1)} %copy-done.6, f32[512]{0:T(512)S(1)} %fusion.86, f32[512]{0:T(512)S(1)} %broadcast_multiply_fusion.2, f32[1024]{0:T(1024)} %param.39, ...), kind=kOutput, calls=%fused_computation.113 | convolution fusion | flops 4300207616 | bytes 18894848 | tf_op jit(solution)/shard_map/ntf,tmf->nm/dot_general | solution.py:552
  435.2 3.4 fusion.71
  438.7 2.6 convert_bitcast_fusion.1
  441.3 8.1 convolution_convert_fusion.5
  450.5 146.1 %while.29 = (s32[]{:T(128)}, bf16[16,512,64]{1,2,0:T(8,128)(2,1)S(1)}, bf16[16,1024,64]{1,2,0:T(8,128)(2,1)}, bf16[16,1024,64]{1,2,0:T(8,128)(2,1)}, bf16[16,512...) while((s32[]{:T(128)}, ...), condition=%wide.region_14.15_spmd.clone, body=%wide.region_12.14_spmd.clone.sunk | while | flops 339902976 | bytes 17384564 | solution.py:689
  473.8 1.9 fusion.145
  482.9 1.9 fusion.145
  492.0 1.9 fusion.145
  501.1 1.9 fusion.145
  519.4 1.9 fusion.145
  546.7 1.9 fusion.145
  564.9 1.9 fusion.145
  583.2 1.9 fusion.145
  596.6 3.1 broadcast_select_fusion.3
  602.1 2.9 copy.94
  605.1 10.7 %convolution_convert_fusion.4 = bf16[4,1024,1024]{1,2,0:T(8,128)(2,1)} fusion(bf16[512,4,1024]{2,0,1:T(8,128)(2,1)} %get-tuple-element.266, bf16[512,1024]{1,0:T(8,128)(2,1)} %copy-done.13), kind=kOutput, calls=%fused_computation.80 | convolution fusion | flops 4299161600 | bytes 13631488 | tf_op jit(solution)/shard_map/nm,ntf->tmf/dot_general | solution.py:552
  619.2 7.3 fusion.56
  626.5 5.6 convert_bitcast_fusion
  632.9 13.2 %copy.112 = bf16[4,1024,3,256]{3,2,1,0:T(4,128)(2,1)} copy(bf16[4,1024,3,256]{1,3,0,2:T(8,128)(2,1)} %convert_bitcast_fusion) | data formatting | bytes 12582912 | tf_op jit(solution)/shard_map/concatenate | solution.py:706
  646.1 17.5 %reshape.281 = bf16[1,4,4,2,128,768]{5,4,3,2,1,0:T(8,128)(2,1)} reshape(bf16[4,1024,3,256]{3,2,1,0:T(4,128)(2,1)} %copy.112) | data formatting | bytes 12582912 | tf_op jit(solution)/shard_map/concatenate | solution.py:706
  663.6 2.7 pad_maximum_fusion.4.y_ref
  666.4 16.6 %pad_maximum_fusion.grad_ref = bf16[3,4,4,2,128,1024]{5,4,3,2,1,0:T(8,128)(2,1)} fusion(bf16[1,4,4,2,128,1024]{5,4,3,2,1,0:T(8,128)(2,1)} %bitcast.284, bf16[1,4,4,2,128,1024]{5,4,3,2,1,0:T(8,128)(2,1)} %bitcast.283, bf16[1,4,4,2,128,256]{5,4,3,2,1,0:T(8,128)(2,1)S(1)} %bitcast.276, bf16[1,4,4,2,128,768]{5,4,3,2,1,0:T(8,128)(2,1)} %reshape.281), kind=kLoop, calls=%fused_computation.57 | loop fusion | flops 100663296 | bytes 50331648 | tf_op jit(solution)/shard_map/stack | solution.py:704
  683.0 134.6 %scatter_all.1 = (f32[3,128,1024]{2,1,0:T(8,128)}, f32[32,8,128]{2,1,0:T(8,128)}, bf16[2,2,256,1024]{3,2,1,0:T(8,128)(2,1)}) custom-call(bf16[3,4,4,2,128,1024]{5,4,3,2,1,0:T(8,128)(2,1)} %pad_maximum_fusion.grad_ref, f32[32,8,128]{2,1,0:T(8,128)} %bitcast.302, bf16[2,2,256,1024]{3,2,1,0:T(8,128)(2,1)} %pad_maximum_fusion.4.y_ref), custom_call_target="tpu_custom_call" | custom-call | tf_op jit(solution)/shard_map/scatter_all/pallas_call | solution.py:504
  820.9 2.0 copy.100
  823.0 2.0 copy.101
  (348 shorter events, 230.7 us)
Async XLA Ops:
  169.2 3.2 copy-start
  175.7 8.7 %copy-start.23 = (f32[256]{0:T(256)S(1)}, f32[256]{0:T(256)}, u32[]{:S(2)}) copy-start(f32[256]{0:T(256)} %param.35) | copy-start | bytes 3076
  175.7 33.2 %copy-start.25 = (bf16[2,256,1024]{2,1,0:T(8,128)(2,1)S(1)}, bf16[2,256,1024]{2,1,0:T(8,128)(2,1)}, u32[]{:S(2)}) copy-start(bf16[2,256,1024]{2,1,0:T(8,128)(2,1)} %get-tuple-element.116) | copy-start | bytes 3145732
  214.6 2.9 copy-start.1
  214.6 4.0 copy-start.31
  214.6 5.3 copy-start.2
  215.8 33.4 %collective-permute-start.1 = (bf16[512,4,256]{0,2,1:T(8,128)(2,1)}, bf16[512,4,256]{0,2,1:T(8,128)(2,1)}, u32[]{:S(2)}, u32[]{:S(2)}) collective-permute-start(bf16[512,4,256]{0,2,1:T(8,128)(2,1)} %fusion.55), channel_id=1, source_target_pairs={{0,4},{4,0},{8,12},{12,8},{16,20},{20,16},{24,28},{28,24},{1,5},{5... | collective-permute-start | bytes 3145736 | tf_op jit(solution)/shard_map/ppermute | solution.py:617
  218.6 2.2 slice-start
  218.6 36.3 %collective-permute-start = (bf16[512,4,256]{0,2,1:T(8,128)(2,1)}, bf16[512,4,256]{0,2,1:T(8,128)(2,1)}, u32[]{:S(2)}, u32[]{:S(2)}) collective-permute-start(bf16[512,4,256]{0,2,1:T(8,128)(2,1)} %fusion.78), channel_id=1, source_target_pairs={{0,4},{4,0},{8,12},{12,8},{16,20},{20,16},{24,28},{28,24},{1,5},{5... | collective-permute-start | bytes 3145736 | tf_op jit(solution)/shard_map/ppermute | solution.py:617
  220.7 2.7 copy-start.24
  220.7 10.4 %copy-start.19 = (f32[1024]{0:T(1024)S(1)}, f32[1024]{0:T(1024)}, u32[]{:S(2)}) copy-start(f32[1024]{0:T(1024)} %param.37) | copy-start | bytes 12292
  261.7 101.0 %copy-start.27 = (f32[1024]{0:T(1024)S(1)}, f32[1024]{0:T(1024)}, u32[]{:S(2)}) copy-start(f32[1024]{0:T(1024)} %param.36) | copy-start | bytes 12292
  362.6 4.0 copy-start.21
  362.6 4.0 copy-start.29
  366.2 9.5 %copy-start.5 = (f32[512,1024]{1,0:T(8,128)}, f32[512,1024]{1,0:T(8,128)S(1)}, u32[]{:S(2)}) copy-start(f32[512,1024]{1,0:T(8,128)S(1)} %get-tuple-element.304) | copy-start | bytes 6291460
  375.7 20.4 %copy-start.28 = (f32[1024]{0:T(1024)S(1)}, f32[1024]{0:T(1024)}, u32[]{:S(2)}) copy-start(f32[1024]{0:T(1024)} %param.38) | copy-start | bytes 12292
  396.1 10.3 %copy-start.18 = (f32[1024]{0:T(1024)S(1)}, f32[1024]{0:T(1024)}, u32[]{:S(2)}) copy-start(f32[1024]{0:T(1024)} %param.41) | copy-start | bytes 12292
  406.0 1.3 copy-start.20
  409.3 1.3 copy-start.7
  409.6 14.2 %copy-start.13 = (bf16[512,1024]{1,0:T(8,128)(2,1)}, bf16[512,1024]{1,0:T(8,128)(2,1)S(1)}, u32[]{:S(2)}) copy-start(bf16[512,1024]{1,0:T(8,128)(2,1)S(1)} %get-tuple-element.259) | copy-start | bytes 3145732
  410.6 13.2 %copy-start.6 = (f32[512,1024]{1,0:T(8,128)S(1)}, f32[512,1024]{1,0:T(8,128)}, u32[]{:S(2)}) copy-start(f32[512,1024]{1,0:T(8,128)} %copy-done.5) | copy-start | bytes 6291460
  423.8 10.4 %copy-start.22 = (f32[1024]{0:T(1024)S(1)}, f32[1024]{0:T(1024)}, u32[]{:S(2)}) copy-start(f32[1024]{0:T(1024)} %param.39) | copy-start | bytes 12292
  434.9 3.7 copy-start.3
  435.2 3.4 copy-start.14
  438.6 2.7 copy-start.30
  438.6 2.6 copy-start.32
  596.6 3.1 copy-start.11
  599.7 16.1 %collective-permute-start.2 = (bf16[512,4,256]{0,2,1:T(8,128)(2,1)}, bf16[512,4,256]{0,2,1:T(8,128)(2,1)}, u32[]{:S(2)}, u32[]{:S(2)}) collective-permute-start(bf16[512,4,256]{0,2,1:T(8,128)(2,1)} %bitcast.41), channel_id=1, source_target_pairs={{0,4},{4,0},{8,12},{12,8},{16,20},{20,16},{24,28},{28,24},{1,5},{5... | collective-permute-start | bytes 3145736 | tf_op jit(solution)/shard_map/ppermute | solution.py:617
  601.2 16.3 %collective-permute-start.3 = (bf16[512,4,256]{0,2,1:T(8,128)(2,1)}, bf16[512,4,256]{0,2,1:T(8,128)(2,1)}, u32[]{:S(2)}, u32[]{:S(2)}) collective-permute-start(bf16[512,4,256]{0,2,1:T(8,128)(2,1)} %bitcast.45), channel_id=1, source_target_pairs={{0,4},{4,0},{8,12},{12,8},{16,20},{20,16},{24,28},{28,24},{1,5},{5... | collective-permute-start | bytes 3145736 | tf_op jit(solution)/shard_map/ppermute | solution.py:617
  605.1 10.7 %copy-start.8 = (bf16[512,16,64]{0,2,1:T(8,128)(2,1)S(1)}, bf16[512,16,64]{0,2,1:T(8,128)(2,1)}, u32[]{:S(2)}) copy-start(bf16[512,16,64]{0,2,1:T(8,128)(2,1)} %get-tuple-element.280) | copy-start | bytes 3145732
  615.8 1.7 copy-start.9
  615.8 3.4 copy-start.4
  619.2 7.3 copy-start.26
  626.5 5.6 copy-start.17
  626.5 5.6 copy-start.16
  646.1 17.5 %copy-start.10 = (bf16[512,1024]{1,0:T(8,128)(2,1)S(1)}, bf16[512,1024]{1,0:T(8,128)(2,1)}, u32[]{:S(2)}) copy-start(bf16[512,1024]{1,0:T(8,128)(2,1)} %get-tuple-element.275) | copy-start | bytes 3145732
  818.6 4.4 copy-start.15
  820.9 4.1 copy-start.12
  825.0 4.7 slice-start.1

commit v2 on v1

--- a/solution.py
+++ b/solution.py
@@ -87,18 +87,49 @@
         landed(src, ssem)
 
 
-def gather_kernel(
+def forward_kernel(
     n_dp,
     n_tensor,
     undealing,
+    lengths,
+    vec_ref,
     x_ref,
     cot_ref,
     shard_ref,
-    xl_ref,
+    bias_ref,
     cl_ref,
     full_ref,
+    q_out,
+    k_out,
+    v_out,
+    mixed_out,
+    act_out,
+    slope_out,
+    xt_out,
+    ht_out,
+    n1_out,
+    n2_out,
+    y_out,
+    lse_out,
+    rstd_out,
     c_one,
     c_two,
+    xv,
+    bias_v,
+    wbuf,
+    q_v,
+    k_v,
+    v_v,
+    mixed_v,
+    act_v,
+    slope_v,
+    turned,
+    low_v,
+    n1_v,
+    n2_v,
+    y_v,
+    acc,
+    lse_v,
     x_s,
     x_r,
     c1_s,
@@ -112,6 +143,12 @@
     xy_r,
     sib_s,
     sib_r,
+    kv_s,
+    kv_r,
+    bz_s,
+    bz_r,
+    w_sem,
+    save_sem,
 ):
     d, t, chip, core = place()
     chips = n_dp // 2
@@ -119,32 +156,60 @@
     half_t = n_tensor // 2
     rows, cols = shard_ref.shape[1:]
     half_cols = cols // 2
+    group = q_v.shape[2]
+    span, width = x_ref.shape[1:]
+    tokens = 2 * span
+    units = cols
     prow, pcol = c_one.shape[2:]
     n_col = cot_ref.shape[2] // pcol
+    pieces = KINDS * n_tensor
+    sibling = (d + 1 - 2 * core, t)
+    length = lengths[4 * chip + t]
     greet(n_dp, n_tensor)
 
     def block(k, tt, who, half):
-        return full_ref.at[k, tt, who, core, :, pl.ds(half * half_cols, half_cols)]
-
+        return full_ref.at[
+            k,
+            tt,
+            pl.ds(pl.multiple_of((2 * who + core) * rows, rows), rows),
+            pl.ds(half * half_cols, half_cols),
+        ]
+
+    def stripe(k, tt):
+        return full_ref.at[k, tt, pl.ds(pl.multiple_of(d * rows, rows), rows)]
+
+    def at(index):
+        return lax.div(index, n_tensor), lax.rem(t + lax.rem(index, n_tensor), n_tensor)
+
+    for s in range(2):
+        send_or_keep(
+            (lax.div(t, half_t) == core) & (2 * core + s == t),
+            x_ref.at[s],
+            xv.at[lax.rem(t, half_t)],
+            x_s.at[s],
+            x_r.at[lax.rem(t, half_t)],
+            (2 * chip + lax.div(t, half_t), 2 * core + s),
+        )
     for k in range(KINDS):
-        pltpu.make_async_copy(shard_ref.at[k], full_ref.at[k, t, chip, core], own_sem.at[k]).start()
+        pltpu.make_async_copy(shard_ref.at[k], stripe(k, t), own_sem.at[k]).start()
         for step in range(1, n_tensor):
             remote(
                 shard_ref.at[k],
-                full_ref.at[k, t, chip, core],
+                stripe(k, t),
                 z_s.at[k, step],
                 z_r.at[k, t],
                 (d, lax.rem(t + step, n_tensor)),
             ).start()
-    for s in range(2):
-        send_or_keep(
-            (lax.div(t, half_t) == core) & (2 * core + s == t),
-            x_ref.at[s],
-            xl_ref.at[lax.rem(t, half_t)],
-            x_s.at[s],
-            x_r.at[lax.rem(t, half_t)],
-            (2 * chip + lax.div(t, half_t), 2 * core + s),
-        )
+        if k == 0:
+            pltpu.make_async_copy(bias_ref, bias_v.at[t], bz_r.at[0]).start()
+            for step in range(1, n_tensor):
+                remote(
+                    bias_ref,
+                    bias_v.at[t],
+                    bz_s.at[step],
+                    bz_r.at[step],
+                    (d, lax.rem(t + step, n_tensor)),
+                ).start()
 
     def piece(who):
         return cot_ref.at[
@@ -157,23 +222,6 @@
     for step in range(1, n_dp):
         who = lax.rem(d + step, n_dp)
         remote(piece(who), c_one.at[d], c1_s.at[step], c1_r.at[step], (who, t)).start()
-
-    def forward(k, tt, half, code):
-        order = orders(bits)[half]
-        chip_here = relative(chip, order, code)
-        ref = block(k, tt, chip_here, half)
-        for s in range(code.bit_length(), bits):
-            target = code | 1 << s
-            remote(
-                ref,
-                ref,
-                xy_s.at[k, tt, half, target],
-                xy_r.at[k, tt, half, target],
-                (2 * flip(chip, order[s]) + core, t),
-            ).start()
-        remote(
-            ref, ref, sib_s.at[k, tt, half, code], sib_r.at[k, tt, half, code], (d + 1 - 2 * core, t)
-        ).start()
 
     def cot_second():
         for step in range(n_dp):
@@ -193,22 +241,252 @@
                 (goal, lax.rem(seq, 4)),
             )
 
-    for k in range(KINDS):
-        landed(shard_ref.at[k], own_sem.at[k])
-        for step in range(n_tensor):
-            tt = lax.rem(t + step, n_tensor)
-            if step:
-                landed(shard_ref.at[k], z_r.at[k, tt])
+    def forward(k, tt, half, code):
+        order = orders(bits)[half]
+        ref = block(k, tt, relative(chip, order, code), half)
+        for s in range(code.bit_length(), bits):
+            target = code | 1 << s
+            remote(
+                ref,
+                ref,
+                xy_s.at[k, tt, half, target],
+                xy_r.at[k, tt, half, target],
+                (2 * flip(chip, order[s]) + core, t),
+            ).start()
+        remote(
+            ref, ref, sib_s.at[k, tt, half, code], sib_r.at[k, tt, half, code], sibling
+        ).start()
+
+    def receive(index, codes):
+        k, tt = at(index)
+        for code in codes:
+            for half in range(2):
+                landed(block(k, tt, chip, half), xy_r.at[k, tt, half, code])
+                forward(k, tt, half, code)
+
+    early, late = range(1, max(chips // 2, 1)), range(max(chips // 2, 1), chips)
+
+    def comm_step(index):
+        @pl.when(index + 1 < pieces)
+        def _():
+            k, tt = at(index + 1)
+
+            @pl.when(tt == t)
+            def _():
+                landed(shard_ref.at[0], own_sem.at[k])
+
+            @pl.when(tt != t)
+            def _():
+                landed(shard_ref.at[0], z_r.at[k, tt])
+
             for half in range(2):
                 forward(k, tt, half, 0)
-        if k == 0:
+
+        @pl.when((index >= 0) & (index < pieces))
+        def _():
+            receive(index, early)
+
+        @pl.when((index >= 1) & (index <= pieces))
+        def _():
+            receive(index - 1, late)
+
+    def load(index):
+        k, tt = at(index)
+        slot = lax.rem(index, 2)
+        for half in range(2):
+            for code in range(chips):
+                landed(block(k, tt, chip, half), sib_r.at[k, tt, half, code])
+        copy = pltpu.make_async_copy(full_ref.at[k, tt], wbuf.at[slot], w_sem.at[slot])
+        copy.start()
+        copy.wait()
+
+    def project(index):
+        _, tt = at(index)
+        slot = lax.rem(index, 2)
+        x = xv[...].reshape(tokens, width)
+        mine = pl.ds(pl.multiple_of(core * tokens, tokens), tokens)
+        for c in range(3):
+            out = jnp.dot(
+                x, wbuf[slot, :, c * group : (c + 1) * group], preferred_element_type=F32
+            )
+            if c == 0:
+                q_v[tt] = ((out + bias_v[tt, 0:1]) * 0.125).astype(BF)
+            elif c == 1:
+                k_v[tt, mine] = out.astype(BF)
+            else:
+                v_v[tt, mine] = (out + bias_v[tt, 1:2]).astype(BF)
+        for j, ref in enumerate((k_v, v_v)):
+            remote(
+                ref.at[tt, mine], ref.at[tt, mine], kv_s.at[tt, j], kv_r.at[tt, j], sibling
+            ).start()
+
+    def attend(index):
+        _, tt = at(index)
+        slot = lax.rem(index, 2)
+        mine = pl.ds(pl.multiple_of(core * tokens, tokens), tokens)
+        for j, ref in enumerate((k_v, v_v)):
+            landed(ref.at[tt, mine], kv_r.at[tt, j])
+        block_rows = min(256, tokens)
+        low = lax.broadcasted_iota(jnp.int32, (block_rows, 2 * HEAD_DIM), 1) < HEAD_DIM
+        lanes = lax.broadcasted_iota(jnp.int32, (block_rows, lse_v.shape[1]), 1)
+        live = lax.broadcasted_iota(jnp.int32, (1, 2 * tokens), 1) < length
+
+        def pair_step(step, carry):
+            pair, part = lax.div(step, tokens // block_rows), lax.rem(step, tokens // block_rows)
+            wide = pl.ds(pl.multiple_of(pair * 2 * HEAD_DIM, 2 * HEAD_DIM), 2 * HEAD_DIM)
+            spot = pl.ds(pl.multiple_of(part * block_rows, block_rows), block_rows)
+            k_pair, v_pair = k_v[tt, :, wide], v_v[tt, :, wide]
+            q_pair = q_v[tt, spot, wide]
+            outs = []
+            for head in range(2):
+                q_one = jnp.where(low if head == 0 else jnp.logical_not(low), q_pair, 0).astype(BF)
+                scores = lax.dot_general(
+                    q_one, k_pair, (((1,), (1,)), ((), ())), preferred_element_type=F32
+                )
+                scores = jnp.where(live, scores, -1000000000.0)
+                summit = jnp.max(scores, axis=-1, keepdims=True)
+                raised = jnp.exp(scores - summit)
+                total = jnp.sum(raised, axis=-1, keepdims=True)
+                out = jnp.dot(raised.astype(BF), v_pair, preferred_element_type=F32)
+                outs.append(out / total)
+                number = tt * (group // HEAD_DIM) + pair * 2 + head
+                lse_v[spot] = jnp.where(lanes == number, summit + jnp.log(total), lse_v[spot])
+            mixed_v[tt, spot, wide] = jnp.where(low, outs[0], outs[1]).astype(BF)
+            return carry
+
+        lax.fori_loop(0, (group // (2 * HEAD_DIM)) * (tokens // block_rows), pair_step, 0)
+        for n in range(width // 256):
+            acc[:, n * 256 : (n + 1) * 256] += lax.dot_general(
+                mixed_v[tt],
+                wbuf[slot, n * 256 : (n + 1) * 256, 3 * group :],
+                (((1,), (1,)), ((), ())),
+                preferred_element_type=F32,
+            )
+
+    chunk = 64
+
+    def norm(which, keep):
+        gain, shift = vec_ref[2 + 2 * which : 3 + 2 * which], vec_ref[3 + 2 * which : 4 + 2 * which]
+
+        def one(step, carry):
+            spot = pl.ds(pl.multiple_of(step * chunk, chunk), chunk)
+            value = acc[spot]
+            center = value - jnp.mean(value, axis=-1, keepdims=True)
+            spread = jnp.mean(center * center, axis=-1, keepdims=True)
+            inverse = lax.rsqrt(spread + 1e-05)
+            unit = center * inverse
+            rstd_out[which, spot] = jnp.broadcast_to(inverse, (chunk, rstd_out.shape[2]))
+            keep(spot, unit, unit * gain + shift)
+            return carry
+
+        lax.fori_loop(0, tokens // chunk, one, 0)
+
+    def keep_one(spot, unit, hidden):
+        n1_v[spot] = unit.astype(BF)
+        low_v[spot] = hidden.astype(BF)
+        acc[spot] = hidden + vec_ref[1:2]
+
+    def keep_two(spot, unit, hidden):
+        n2_v[spot] = unit.astype(BF)
+        y_v[spot] = hidden.astype(BF)
+
+    def turn_rows(source, which):
+        flat = jnp.transpose(source)
+        for dev in range(n_dp):
+            turned[which, dev % 2, (dev // 2) * rows : (dev // 2 + 1) * rows] = flat[
+                dev * rows : (dev + 1) * rows
+            ]
+
+    def expand(index):
+        _, tt = at(index)
+        slot = lax.rem(index, 2)
+
+        def one(n, carry):
+            wide = pl.ds(pl.multiple_of(n * 256, 256), 256)
+            u = jnp.dot(low_v[...], wbuf[slot, :, wide], preferred_element_type=F32)
+            u = u + bias_v[tt, pl.ds(2 + n, 1)]
+            bell, below = gauss(u)
+            act_v[tt, :, wide] = (u * below).astype(BF)
+            slope_v[tt, :, wide] = (below + u * bell).astype(BF)
+            return carry
+
+        lax.fori_loop(0, units // 256, one, 0)
+
+    def contract(index):
+        _, tt = at(index)
+        slot = lax.rem(index, 2)
+
+        def one(n, carry):
+            wide = pl.ds(pl.multiple_of(n * 256, 256), 256)
+            acc[:, wide] += lax.dot_general(
+                act_v[tt], wbuf[slot, wide, :], (((1,), (1,)), ((), ())), preferred_element_type=F32
+            )
+            return carry
+
+        lax.fori_loop(0, width // 256, one, 0)
+
+    comm_step(jnp.int32(-1))
+    comm_step(jnp.int32(0))
+    for s in range(2):
+        landed(x_ref.at[s], x_r.at[s])
+    for step in range(n_tensor):
+        landed(bias_ref, bz_r.at[step])
+    acc[...] = xv[...].reshape(tokens, width).astype(F32) + vec_ref[0:1]
+    turn_rows(xv[...].reshape(tokens, width), 0)
+    lse_v[...] = jnp.zeros_like(lse_v)
+
+    def turn(index, carry):
+        comm_step(index + 1)
+        load(index)
+
+        @pl.when(index < n_tensor)
+        def _():
+            project(index)
+
+        @pl.when((index >= 1) & (index <= n_tensor))
+        def _():
+            attend(index - 1)
+
+        @pl.when(index == n_tensor)
+        def _():
             cot_second()
-        for code in range(1, chips):
-            for step in range(n_tensor):
-                tt = lax.rem(t + step, n_tensor)
-                for half in range(2):
-                    landed(block(k, tt, chip, half), xy_r.at[k, tt, half, code])
-                    forward(k, tt, half, code)
+            norm(0, keep_one)
+            turn_rows(low_v[...], 1)
+
+        @pl.when((index >= n_tensor) & (index < 2 * n_tensor))
+        def _():
+            expand(index)
+
+        @pl.when(index >= 2 * n_tensor)
+        def _():
+            contract(index)
+
+        return carry
+
+    lax.fori_loop(0, pieces, turn, 0)
+    norm(1, keep_two)
+    lse_out[...] = jnp.transpose(lse_v[...])
+
+    saves = [
+        pltpu.make_async_copy(src, dst, save_sem.at[i])
+        for i, (src, dst) in enumerate(
+            (
+                (q_v, q_out),
+                (k_v, k_out),
+                (v_v, v_out),
+                (mixed_v, mixed_out),
+                (act_v, act_out),
+                (slope_v, slope_out),
+                (turned.at[0], xt_out),
+                (turned.at[1], ht_out),
+                (n1_v, n1_out),
+                (n2_v, n2_out),
+                (y_v, y_out),
+            )
+        )
+    ]
+    for copy in saves:
+        copy.start()
 
     for k in range(KINDS):
         for step in range(1, n_tensor):
@@ -218,13 +496,16 @@
             for half in range(2):
                 for code in range(chips):
                     ref = block(k, tt, chip, half)
-                    landed(ref, sib_r.at[k, tt, half, code])
                     landed(ref, sib_s.at[k, tt, half, code])
                     if code:
                         landed(ref, xy_s.at[k, tt, half, code])
     for s in range(2):
         sent((lax.div(t, half_t) == core) & (2 * core + s == t), x_ref.at[s], x_s.at[s])
-        landed(x_ref.at[s], x_r.at[s])
+    for step in range(1, n_tensor):
+        landed(bias_ref, bz_s.at[step])
+    for tt in range(n_tensor):
+        for j in range(2):
+            landed(q_v.at[tt], kv_s.at[tt, j])
     for step in range(1, n_dp):
         landed(c_one.at[0], c1_s.at[step])
     for step in range(2 * n_dp):
@@ -234,28 +515,73 @@
     for q in range(half_t):
         for who in range(n_dp):
             landed(c_two.at[0], c2_r.at[q, who])
-
-
-def gather(n_dp, n_tensor, undealing, x_in, cot_in, shard):
+    for copy in saves:
+        copy.wait()
+
+
+def gauss(u):
+    size = jnp.abs(u)
+    bell = 0.3989422804014327 * jnp.exp(-0.5 * (u * u))
+    s = 1.0 / (1.0 + 0.23164190 * size)
+    tail = bell * s * (
+        0.319381530 + s * (-0.356563782 + s * (1.781477937 + s * (-1.821255978 + s * 1.330274429)))
+    )
+    return bell, jnp.where(u < 0, tail, 1.0 - tail)
+
+
+def run_forward(n_dp, n_tensor, undealing, lengths, vecs, x_in, cot_in, shard, biases):
     slots, span, width = x_in.shape
     rows, cols = shard.shape[1:]
     chips = n_dp // 2
+    tokens = 2 * span
+    group = cols // 4
     n_pos = min(n_dp, span // 16)
     prow, pcol = span // n_pos, width // (n_dp // n_pos)
     dma = pltpu.SemaphoreType.DMA
     any_space = pl.BlockSpec(memory_space=pl.ANY)
+    smem = pl.BlockSpec(memory_space=pltpu.SMEM)
+    vmem = pl.BlockSpec(memory_space=pltpu.VMEM)
+    shapes = (
+        ((2, n_dp, prow, pcol), BF),
+        ((KINDS, n_tensor, width, cols), BF),
+        ((n_tensor, tokens, group), BF),
+        ((n_tensor, 2 * tokens, group), BF),
+        ((n_tensor, 2 * tokens, group), BF),
+        ((n_tensor, tokens, group), BF),
+        ((n_tensor, tokens, cols), BF),
+        ((n_tensor, tokens, cols), BF),
+        ((2, width // 2, tokens), BF),
+        ((2, width // 2, tokens), BF),
+        ((tokens, width), BF),
+        ((tokens, width), BF),
+        ((tokens, width), BF),
+        ((128, tokens), F32),
+        ((2, tokens, 128), F32),
+    )
     return pl.pallas_call(
-        functools.partial(gather_kernel, n_dp, n_tensor),
-        out_shape=(
-            jax.ShapeDtypeStruct((2, span, width), BF),
-            jax.ShapeDtypeStruct((2, n_dp, prow, pcol), BF),
-            jax.ShapeDtypeStruct((KINDS, n_tensor, chips, 2, rows, cols), BF),
-        ),
-        in_specs=[pl.BlockSpec(memory_space=pltpu.SMEM), any_space, any_space, any_space],
-        out_specs=(any_space, any_space, any_space),
+        functools.partial(forward_kernel, n_dp, n_tensor),
+        out_shape=tuple(jax.ShapeDtypeStruct(*shape) for shape in shapes),
+        in_specs=[smem, smem, vmem, any_space, any_space, any_space, any_space],
+        out_specs=(any_space,) * 13 + (vmem, vmem),
         scratch_shapes=[
             pltpu.VMEM((n_dp, slots, prow, pcol), BF),
             pltpu.VMEM((2 * n_dp, prow, pcol), BF),
+            pltpu.VMEM((2, span, width), BF),
+            pltpu.VMEM((n_tensor,) + biases.shape, F32),
+            pltpu.VMEM((2, width, cols), BF),
+            pltpu.VMEM((n_tensor, tokens, group), BF),
+            pltpu.VMEM((n_tensor, 2 * tokens, group), BF),
+            pltpu.VMEM((n_tensor, 2 * tokens, group), BF),
+            pltpu.VMEM((n_tensor, tokens, group), BF),
+            pltpu.VMEM((n_tensor, tokens, cols), BF),
+            pltpu.VMEM((n_tensor, tokens, cols), BF),
+            pltpu.VMEM((2, 2, width // 2, tokens), BF),
+            pltpu.VMEM((tokens, width), BF),
+            pltpu.VMEM((tokens, width), BF),
+            pltpu.VMEM((tokens, width), BF),
+            pltpu.VMEM((tokens, width), BF),
+            pltpu.VMEM((tokens, width), F32),
+            pltpu.VMEM((tokens, 128), F32),
             dma((2,)),
             dma((2,)),
             dma((n_dp,)),
@@ -269,12 +595,18 @@
             dma((KINDS, n_tensor, 2, chips)),
             dma((KINDS, n_tensor, 2, chips)),
             dma((KINDS, n_tensor, 2, chips)),
+            dma((n_tensor, 2)),
+            dma((n_tensor, 2)),
+            dma((n_tensor,)),
+            dma((n_tensor,)),
+            dma((2,)),
+            dma((11,)),
         ],
         compiler_params=pltpu.CompilerParams(
             collective_id=0, has_side_effects=True, vmem_limit_bytes=VMEM_LIMIT
         ),
-        name="gather_all",
-    )(undealing, x_in, cot_in, shard)
+        name="forward_layer",
+    )(undealing, lengths, vecs, x_in, cot_in, shard, biases)
 
 
 def scatter_kernel(
@@ -538,16 +870,6 @@
     )(grads, bias, outs)
 
 
-def normalize(hidden, norm_gain, norm_shift):
-    center = hidden - jnp.mean(hidden, axis=-1, keepdims=True)
-    spread = jnp.mean(center * center, axis=-1, keepdims=True)
-    return center * lax.rsqrt(spread + 1e-05) * norm_gain + norm_shift
-
-
-def gelu_exact(values):
-    return jax.nn.gelu(values, approximate=False)
-
-
 def mm(spec, left, right):
     return jnp.einsum(spec, left, right, preferred_element_type=F32)
 
@@ -592,87 +914,75 @@
             down_weight.T,
         ]
     ).astype(BF)
-    x_loc, cot_loc, full = gather(
+    blank = jnp.zeros((group,), F32)
+    biases = jnp.concatenate([query_bias, value_bias, up_bias, blank, blank]).reshape(8, group)
+    vecs = jnp.stack([output_bias, down_bias, first_gain, first_shift, second_gain, second_shift])
+    (
+        cot_loc, full, query, key, value, mixed, activated, slope, x_t, h_t, n1, n2, y, lse, rstd
+    ) = run_forward(
         n_dp,
         n_tensor,
         undealing,
+        lengths,
+        jnp.pad(vecs, ((0, 2), (0, 0))),
         jnp.transpose(inputs, (1, 0, 2)),
         jnp.transpose(cotangent, (1, 0, 2)),
         shard,
+        biases,
     )
     n_col = width // cot_loc.shape[3]
     cot = cot_loc.reshape(2, n_dp // n_col, n_col, *cot_loc.shape[2:])
     cot = jnp.transpose(cot, (0, 1, 3, 2, 4)).reshape(half, width)
-    x = x_loc.reshape(half, width)
-    full = full.reshape(KINDS, n_tensor, width, 4 * group)
     w_qkv = full[0][:, :, : 3 * group].reshape(n_tensor, width, 3, group)
     w_out = full[0][:, :, 3 * group :]
     w_up, w_down = full[1], full[2]
 
-    bias_q = lax.all_gather(query_bias, "tensor", axis=0)
-    bias_v = lax.all_gather(value_bias, "tensor", axis=0)
-    bias_u = lax.all_gather(up_bias, "tensor", axis=0)
+    def unturn(values):
+        return jnp.transpose(values.reshape(2, n_dp // 2, width // n_dp, half), (3, 1, 0, 2)).reshape(half, width)
+
+    x, hidden_low = unturn(x_t), unturn(h_t)
 
     def swap(values):
-        other = lax.ppermute(values, "dp", [(i, i ^ 1) for i in range(n_dp)])
-        return other
-
-    def whole(values):
-        other = swap(values)
-        return jnp.concatenate(
-            [jnp.where(core == 0, values, other), jnp.where(core == 0, other, values)], axis=0
-        )
-
-    qkv = mm("nm,tmjc->jntc", x, w_qkv)
-    query = ((qkv[0] + bias_q) * 0.125).astype(BF)
-    key = qkv[1].astype(BF)
-    value = (qkv[2] + bias_v).astype(BF)
+        return lax.ppermute(values, "dp", [(i, i ^ 1) for i in range(n_dp)])
+
     heads = n_tensor * group // HEAD_DIM
 
     def split(values):
-        return jnp.transpose(values.reshape(-1, heads, HEAD_DIM), (1, 0, 2))
+        values = values.reshape(n_tensor, -1, group // HEAD_DIM, HEAD_DIM)
+        return jnp.transpose(values, (0, 2, 1, 3)).reshape(heads, -1, HEAD_DIM)
 
     def join(values):
         return jnp.transpose(values, (1, 0, 2)).reshape(-1, n_tensor, group)
 
-    q_h, k_h, v_h = split(query), split(whole(key)), split(whole(value))
+    q_h, k_h, v_h = split(query), split(key), split(value)
+    log_total = lse[:heads]
     visible = jnp.arange(2 * half) < length
-
-    def attend(one):
-        q_one, k_one, v_one = one
-        scores = jnp.where(visible, mm("qe,ke->qk", q_one, k_one), -1000000000.0)
-        summit = jnp.max(scores, axis=-1, keepdims=True)
-        raised = jnp.exp(scores - summit)
-        total = jnp.sum(raised, axis=-1, keepdims=True)
-        out = mm("qk,ke->qe", (raised / total).astype(BF), v_one)
-        return out.astype(BF), (summit + jnp.log(total))[:, 0]
-
-    attended, log_total = lax.map(attend, (q_h, k_h, v_h))
-    mixed = join(attended)
-    branch = mm("ntc,tmc->nm", mixed, w_out) + output_bias
-    residual = x.astype(F32) + branch
-    hidden_one, back_one = jax.vjp(normalize, residual, first_gain, first_shift)
-    hidden_low = hidden_one.astype(BF)
-    expanded = mm("nm,tmf->ntf", hidden_low, w_up) + bias_u
-    activated = gelu_exact(expanded).astype(BF)
-    branch_two = mm("ntf,tmf->nm", activated, w_down) + down_bias
-    result, back_two = jax.vjp(normalize, hidden_one + branch_two, second_gain, second_shift)
+    mixed = jnp.transpose(mixed, (1, 0, 2))
+    activated = jnp.transpose(activated, (1, 0, 2))
+    slope = jnp.transpose(slope, (1, 0, 2))
+    result = y
+
+    def norm_back(e, unit, gain, inverse):
+        unit = unit.astype(F32)
+        ge = e * gain
+        grad = ge - jnp.mean(ge, -1, keepdims=True) - unit * jnp.mean(ge * unit, -1, keepdims=True)
+        return grad * inverse[:, :1], jnp.sum(e * unit, 0), jnp.sum(e, 0)
 
     seed = cot.astype(F32) * valid[:, None]
-    grad_two, gain_two, shift_two = back_two(seed)
+    grad_two, gain_two, shift_two = norm_back(seed, n2, second_gain, rstd[1])
     mlp_grad = grad_two.astype(BF)
     down_bias_grad = jnp.sum(mlp_grad, axis=0, dtype=F32)
     down_grad = mm("nm,ntf->tmf", mlp_grad, activated).astype(BF)
     act_grad = mm("nm,tmf->ntf", mlp_grad, w_down)
-    expand_grad = jax.vjp(gelu_exact, expanded)[1](act_grad)[0].astype(BF)
+    expand_grad = (slope.astype(F32) * act_grad).astype(BF)
     up_bias_grad = jnp.sum(expand_grad, axis=0, dtype=F32)
     up_grad = mm("nm,ntf->tmf", hidden_low, expand_grad).astype(BF)
     hidden_grad = grad_two + mm("ntf,tmf->nm", expand_grad, w_up)
-    grad_one, gain_one, shift_one = back_one(hidden_grad)
+    grad_one, gain_one, shift_one = norm_back(hidden_grad, n1, first_gain, rstd[0])
     attn_grad = grad_one.astype(BF)
     output_bias_grad = jnp.sum(attn_grad, axis=0, dtype=F32)
     out_grad = mm("nm,ntc->tmc", attn_grad, mixed).astype(BF)
-    mixed_grad = split(mm("nm,tmc->ntc", attn_grad, w_out).astype(BF))
+    mixed_grad = split(mm("nm,tmc->tnc", attn_grad, w_out).astype(BF))
 
     def attend_back(one):
         q_one, k_one, v_one, total, o_one = one

time: 844 us -> 703 us (0.83)
  matrix products: 269 us -> 177 us
  Pallas kernels: 278 us -> 357 us
  blocking collectives: 45.4 us -> 0 us
  other arithmetic: 103 us -> 62.2 us
  local copies, waits for them, and re-layouts: 131 us -> 90.2 us
    dot_general x124 -> x88, matrix products: 269 us -> 177 us  [mm(): return jnp.einsum(spec, left, right, preferred_element_type=F32)]
    pallas_call x1, Pallas kernels: 144 us -> 219 us  [run_forward(): pl.pallas_call(functools.partial(forward_kernel, n_dp, n_tensor), out_sha...]
    all_gather x3 -> x0, blocking collectives: 45.4 us -> none  [the longest x1 24.5 us: shards(): bias_v = lax.all_gather(value_bias, 'tensor', axis=0)]
    dynamic_update_slice x16 -> x0, local copies, waits for them, and re-layouts: 21.5 us -> none  [shards(): attended, log_total = lax.map(attend, (q_h, k_h, v_h))]
    convert_element_type x2 -> x0, other arithmetic: 21.5 us -> none  [the longest x1 20.4 us: shards(): activated = gelu_exact(expanded).astype(BF)]
    dynamic_slice x16, local copies, waits for them, and re-layouts: 11.7 us -> 0.2 us  [shards(): lax.map(attend_back, (q_h, k_h, v_h, log_total, mixed_grad))]
    slice x3, local copies, waits for them, and re-layouts: 14.2 us -> 3.05 us  [the longest x1 14.2 us: shards(): w_up, w_down = (full[1], full[2])]
    reduce_sum x22 -> x2, other arithmetic: 13.4 us -> 2.97 us  [norm_back(): return (grad * inverse[:, :1], jnp.sum(e * unit, 0), jnp.sum(e, 0))]
  transfers between devices with their start and end apart: 4 -> 2, of which waited for: 0 -> 0; matrix products, arithmetic and copies ran while one was open for 4% -> 8% of each run, Pallas kernels for 0% -> 0%
where the time goes in v2:
time: 703 us; the launch traced here: 689 us
  Pallas kernels  357 us (51%)
  matrix products  177 us (25%)
  local copies, waits for them, and re-layouts  90.2 us (13%)
  other arithmetic  62.2 us (9%)
    pallas_call x1, Pallas kernels, run_forward(): pl.pallas_call(functools.partial(forward_kernel, n_dp, n_tensor), out_sha...  219 us
    dot_general x88, matrix products, mm(): return jnp.einsum(spec, left, right, preferred_element_type=F32)  177 us
    pallas_call x1, Pallas kernels, scatter(): pl.pallas_call(functools.partial(scatter_kernel, n_dp, n_tensor), out_sha...  138 us
    concatenate x2, local copies, waits for them, and re-layouts, shards(): jnp.concatenate([qkv_w_grad.reshape(n_tensor, width, 3 * group), out_grad...  30.9 us
    another operation x1, other arithmetic, shards(): jnp.stack([jnp.concatenate([qkv_w_grad.reshape(n_tensor, width, 3 * group...  16.7 us
    unnamed x93, local copies, waits for them, and re-layouts  16.2 us
    slice x2, local copies, waits for them, and re-layouts, shards(): w_qkv = full[0][:, :, :3 * group].reshape(n_tensor, width, 3, group)  14.6 us
  transfers between devices with their start and end apart: 2, of which 0 were waited for; matrix products, arithmetic and copies ran while one was open for 8% of the time, Pallas kernels for 0%

profile of v2, /device:TPU:0, one launch (start us, length us, event | category | flops | bytes accessed | tf_op | source)
XLA Modules:
  0.0 689.3 jit_solution(5650726372038855283)
XLA Ops:
  14.4 218.9 %forward_layer.1 = (bf16[2,8,32,1024]{3,2,1,0:T(8,128)(2,1)}, bf16[3,4,1024,1024]{3,2,1,0:T(8,128)(2,1)}, bf16[4,512,256]{2,1,0:T(8,128)(2,1)}, bf16[4,1024,256]...) custom-call(s32[16]{0:T(128)} %undealing.1, ...), custom_call_target="tpu_custom_call" | custom-call | tf_op jit(solution)/shard_map/forward_layer/pallas_call | solution.py:561
  233.4 2.5 fusion.44
  236.5 7.7 %slice_bitcast_fusion = bf16[4,1024,1024]{2,1,0:T(8,128)(2,1)} fusion(bf16[3,4,1024,1024]{3,2,1,0:T(8,128)(2,1)} %get-tuple-element.92), kind=kLoop, calls=%fused_computation.46 | loop fusion | bytes 16777216 | tf_op jit(solution)/shard_map/squeeze | solution.py:937
  245.2 1.8 copy-done.33
  247.0 8.8 %convert_reduce_fusion = (f32[4,1024]{1,0:T(4,128)S(1)}, bf16[512,4,1024]{2,0,1:T(8,128)(2,1)S(1)}) fusion(bf16[3,4,1024,1024]{3,2,1,0:T(8,128)(2,1)} %get-tuple-element.92, bf16[512,1024]{1,0:T(8,128)(2,1)S(1)} %get-tuple-element.206, bf16[4,512,1024]{2,1,0:T(8,128)(2,1)S(1)} %copy-done.33), kind=kOutput, calls=%fused_computation.43 | convolution fusion | flops 4305448960 | bytes 17842176 | tf_op jit(solution)/shard_map/nm,tmf->ntf/dot_general | solution.py:874
  255.8 9.1 %fusion.48 = (f32[1024]{0:T(1024)S(1)}, f32[512]{0:T(512)S(1)}, f32[512]{0:T(512)S(1)}, f32[1024]{0:T(1024)S(1)}, f32[512,1024]{1,0:T(8,128)S(1)}) fusion(bf16[512,1024]{1,0:T(8,128)(2,1)S(1)} %copy-done.21, f32[1024]{0:T(1024)S(1)} %copy-done.25, f32[512,1024]{1,0:T(8,128)S(1)} %get-tuple-element.211, bf16[512,4,1024]{2,0,1:T(8,128)(2,1)S(1)} %get-tuple-element.255, ...), kind=kOutput, calls=%fused_computation.69 | convolution fusion | flops 4299682816 | bytes 17842176 | tf_op jit(solution)/shard_map/ntf,tmf->nm/dot_general | solution.py:874
  265.6 3.7 fusion.63
  270.5 2.1 fusion.86
  273.4 2.0 fusion.83
  275.4 2.4 pad_maximum_fusion.2
  277.8 2.4 pad_maximum_fusion.1
  280.1 1.7 pad_maximum_fusion.4
  281.9 134.6 %while.15 = (s32[]{:T(128)}, bf16[16,512,64]{1,2,0:T(8,128)(2,1)S(1)}, bf16[16,1024,64]{1,2,0:T(8,128)(2,1)}, bf16[16,1024,64]{1,2,0:T(8,128)(2,1)}, bf16[16,512...) while((s32[]{:T(128)}, ...), condition=%wide.region_6.7_spmd.clone, body=%wide.region_4.0_spmd.clone.sunk | while | flops 339902976 | bytes 17384564 | solution.py:999
  283.9 1.8 multiply_reduce_fusion.4
  286.0 1.9 fusion.115
  292.3 1.8 multiply_reduce_fusion.4
  294.4 1.9 fusion.115
  300.8 1.8 multiply_reduce_fusion.4
  302.8 1.9 fusion.115
  309.2 1.8 multiply_reduce_fusion.4
  311.2 1.9 fusion.115
  317.6 1.8 multiply_reduce_fusion.4
  319.6 1.9 fusion.115
  326.0 1.8 multiply_reduce_fusion.4
  328.0 1.9 fusion.115
  334.5 1.8 multiply_reduce_fusion.4
  336.5 1.9 fusion.115
  342.9 1.8 multiply_reduce_fusion.4
  344.9 1.9 fusion.115
  351.3 1.8 multiply_reduce_fusion.4
  353.3 1.9 fusion.115
  359.7 1.8 multiply_reduce_fusion.4
  361.7 1.9 fusion.115
  368.1 1.8 multiply_reduce_fusion.4
  370.2 1.9 fusion.115
  376.6 1.8 multiply_reduce_fusion.4
  378.6 1.9 fusion.115
  385.0 1.8 multiply_reduce_fusion.4
  387.0 1.9 fusion.115
  393.4 1.8 multiply_reduce_fusion.4
  395.4 1.9 fusion.115
  401.8 1.8 multiply_reduce_fusion.4
  403.8 1.9 fusion.115
  410.2 1.8 multiply_reduce_fusion.4
  412.2 1.9 fusion.115
  417.5 2.8 broadcast_select_fusion.3
  422.3 5.8 slice.219
  428.2 8.8 %copy.67 = bf16[4,1024,768]{1,2,0:T(8,128)(2,1)} copy(bf16[4,1024,768]{2,1,0:T(8,128)(2,1)} %slice.219) | data formatting | bytes 12582912 | tf_op jit(solution)/shard_map/slice | solution.py:936
  440.0 4.2 convert_bitcast_fusion.1
  444.2 2.8 copy.63
  448.4 8.9 %convolution_convert_fusion.3 = bf16[4,1024,1024]{1,2,0:T(8,128)(2,1)} fusion(bf16[512,1024,1]{0,1,2:T(8,128)(2,1)S(1)} %bitcast.256, bf16[512,4,1024]{2,0,1:T(8,128)(2,1)} %copy-done.35), kind=kOutput, calls=%fused_computation.47 | convolution fusion | flops 4299161600 | bytes 13631488 | tf_op jit(solution)/shard_map/nm,ntf->tmf/dot_general | solution.py:874
  457.3 2.4 broadcast_multiply_fusion
  459.7 9.9 %convolution_convert_fusion.4 = bf16[4,1024,1024]{1,2,0:T(8,128)(2,1)} fusion(bf16[4,512,1024]{2,1,0:T(8,128)(2,1)} %get-tuple-element.105, bf16[512,1024]{1,0:T(8,128)(2,1)S(1)} %copy-done.13), kind=kOutput, calls=%fused_computation.48 | convolution fusion | flops 4299161600 | bytes 13631488 | tf_op jit(solution)/shard_map/nm,ntf->tmf/dot_general | solution.py:874
  469.6 2.5 convert_reduce_fusion.3
  472.9 1.8 fusion.67
  474.7 7.7 %fusion.51 = bf16[512,1024]{1,0:T(8,128)(2,1)} fusion(f32[512,1024]{1,0:T(8,128)S(1)} %copy-done.9, bf16[4,1024,3,256]{1,3,2,0:T(8,128)(2,1)} %bitcast.242, bf16[1,512,4,256]{1,3,2,0:T(8,128)(2,1)} %get-tuple-element.215, bf16[1,512,4,256]{1,3,2,0:T(8,128)(2,1)S(1)} %fusion.67, bf16[1,512,4,256]{1,3,2,0:T(8,128)(2,1)S(1)} %bitcast.254), kind=kOutput, calls=%fused_computation.75 | convolution fusion | flops 3225419776 | bytes 12582912 | tf_op jit(solution)/shard_map/jntc,tmjc->nm/dot_general | solution.py:874
  482.4 5.3 convert_bitcast_fusion
  487.7 13.3 %copy.82 = bf16[4,1024,3,256]{3,2,1,0:T(4,128)(2,1)} copy(bf16[4,1024,3,256]{1,3,0,2:T(8,128)(2,1)} %convert_bitcast_fusion) | data formatting | bytes 12582912 | tf_op jit(solution)/shard_map/concatenate | solution.py:1016
  501.0 17.7 %reshape.218 = bf16[1,4,4,2,128,768]{5,4,3,2,1,0:T(8,128)(2,1)} reshape(bf16[4,1024,3,256]{3,2,1,0:T(4,128)(2,1)} %copy.82) | data formatting | bytes 12582912 | tf_op jit(solution)/shard_map/concatenate | solution.py:1016
  518.7 2.7 pad_maximum_fusion.5.y_ref
  521.4 16.7 %pad_maximum_fusion.grad_ref = bf16[3,4,4,2,128,1024]{5,4,3,2,1,0:T(8,128)(2,1)} fusion(bf16[1,4,4,2,128,1024]{5,4,3,2,1,0:T(8,128)(2,1)} %bitcast.240, bf16[1,4,4,2,128,1024]{5,4,3,2,1,0:T(8,128)(2,1)} %bitcast.239, bf16[1,4,4,2,128,256]{5,4,3,2,1,0:T(8,128)(2,1)S(1)} %bitcast.238, bf16[1,4,4,2,128,768]{5,4,3,2,1,0:T(8,128)(2,1)} %reshape.218), kind=kLoop, calls=%fused_computation.36 | loop fusion | flops 100663296 | bytes 50331648 | tf_op jit(solution)/shard_map/stack | solution.py:1014
  538.0 138.3 %scatter_all.1 = (f32[3,128,1024]{2,1,0:T(8,128)}, f32[32,8,128]{2,1,0:T(8,128)}, bf16[2,2,256,1024]{3,2,1,0:T(8,128)(2,1)}) custom-call(bf16[3,4,4,2,128,1024]{5,4,3,2,1,0:T(8,128)(2,1)} %pad_maximum_fusion.grad_ref, f32[32,8,128]{2,1,0:T(8,128)} %bitcast.260, bf16[2,2,256,1024]{3,2,1,0:T(8,128)(2,1)} %pad_maximum_fusion.5.y_ref), custom_call_target="tpu_custom_call" | custom-call | tf_op jit(solution)/shard_map/scatter_all/pallas_call | solution.py:836
  679.7 2.0 copy.70
  681.7 2.0 copy.71
  (239 shorter events, 109.6 us)
Async XLA Ops:
  0.7 8.8 %copy-start.14 = (bf16[256,2,1024]{2,1,0:T(2,128)(2,1)S(1)}, bf16[256,2,1024]{2,1,0:T(2,128)(2,1)}, u32[]{:S(2)}) copy-start(bf16[256,2,1024]{2,1,0:T(2,128)(2,1)} %param.23) | copy-start | bytes 3145732
  4.4 6.5 copy-start.15
  9.5 2.6 copy-start.24
  9.5 2.6 copy-start.25
  9.5 2.6 copy-start.26
  9.5 2.6 copy-start.27
  9.5 2.6 copy-start.28
  9.5 2.6 copy-start.29
  9.5 3.2 copy-start.30
  9.6 3.2 copy-start.31
  9.6 3.2 copy-start.32
  233.4 2.5 copy-start
  233.4 3.1 copy-start.22
  236.5 7.9 %copy-start.4 = (bf16[512,1024]{1,0:T(8,128)(2,1)S(1)}, bf16[512,1024]{1,0:T(8,128)(2,1)}, u32[]{:S(2)}) copy-start(bf16[512,1024]{1,0:T(8,128)(2,1)} %get-tuple-element.94) | copy-start | bytes 3145732
  244.4 2.6 copy-start.33
  245.2 10.6 %copy-start.12 = (bf16[512,1024]{1,0:T(8,128)(2,1)}, bf16[512,1024]{1,0:T(8,128)(2,1)S(1)}, u32[]{:S(2)}) copy-start(bf16[512,1024]{1,0:T(8,128)(2,1)S(1)} %get-tuple-element.206) | copy-start | bytes 3145732
  247.0 8.8 %copy-start.21 = (bf16[512,1024]{1,0:T(8,128)(2,1)S(1)}, bf16[512,1024]{1,0:T(8,128)(2,1)}, u32[]{:S(2)}) copy-start(bf16[512,1024]{1,0:T(8,128)(2,1)} %get-tuple-element.97) | copy-start | bytes 3145732
  255.8 9.2 %copy-start.35 = (bf16[512,4,1024]{2,0,1:T(8,128)(2,1)}, bf16[512,4,1024]{2,0,1:T(8,128)(2,1)S(1)}, u32[]{:S(2)}) copy-start(bf16[512,4,1024]{2,0,1:T(8,128)(2,1)S(1)} %get-tuple-element.255) | copy-start | bytes 12582916
  265.6 3.7 copy-start.8
  270.5 2.9 copy-start.1
  270.5 2.9 copy-start.2
  280.1 1.7 copy-start.5
  416.5 1.0 copy-start.6
  417.5 2.8 copy-start.10
  420.3 52.6 %collective-permute-start = (bf16[512,4,256]{0,2,1:T(8,128)(2,1)}, bf16[512,4,256]{0,2,1:T(8,128)(2,1)}, u32[]{:S(2)}, u32[]{:S(2)}) collective-permute-start(bf16[512,4,256]{0,2,1:T(8,128)(2,1)} %bitcast.33), channel_id=1, source_target_pairs={{0,4},{4,0},{8,12},{12,8},{16,20},{20,16},{24,28},{28,24},{1,5},{5... | collective-permute-start | bytes 3145736 | tf_op jit(solution)/shard_map/ppermute | solution.py:946
  421.8 47.7 %collective-permute-start.1 = (bf16[512,4,256]{0,2,1:T(8,128)(2,1)}, bf16[512,4,256]{0,2,1:T(8,128)(2,1)}, u32[]{:S(2)}, u32[]{:S(2)}) collective-permute-start(bf16[512,4,256]{0,2,1:T(8,128)(2,1)} %bitcast.37), channel_id=1, source_target_pairs={{0,4},{4,0},{8,12},{12,8},{16,20},{20,16},{24,28},{28,24},{1,5},{5... | collective-permute-start | bytes 3145736 | tf_op jit(solution)/shard_map/ppermute | solution.py:946
  428.2 8.8 %copy-start.7 = (bf16[16,512,64]{1,2,0:T(8,128)(2,1)S(1)}, bf16[16,512,64]{1,2,0:T(8,128)(2,1)}, u32[]{:S(2)}) copy-start(bf16[16,512,64]{1,2,0:T(8,128)(2,1)} %copy-done.6) | copy-start | bytes 3145732
  428.2 9.2 %copy-start.16 = (bf16[2,512,512]{2,1,0:T(8,128)(2,1)S(1)}, bf16[2,512,512]{2,1,0:T(8,128)(2,1)}, u32[]{:S(2)}) copy-start(bf16[2,512,512]{2,1,0:T(8,128)(2,1)} %get-tuple-element.102) | copy-start | bytes 3145732
  438.3 1.7 copy-start.34
  457.3 2.4 copy-start.13
  459.7 9.9 %copy-start.3 = (bf16[512,16,64]{0,2,1:T(8,128)(2,1)S(1)}, bf16[512,16,64]{0,2,1:T(8,128)(2,1)}, u32[]{:S(2)}) copy-start(bf16[512,16,64]{0,2,1:T(8,128)(2,1)} %get-tuple-element.218) | copy-start | bytes 3145732
  472.2 2.5 copy-start.9
  472.2 2.5 copy-start.18
  474.7 7.7 %copy-start.17 = (bf16[512,1024,1,1]{1,0,2,3:T(8,128)(2,1)S(1)}, bf16[512,1024,1,1]{1,0,2,3:T(8,128)(2,1)}, u32[]{:S(2)}) copy-start(bf16[512,1024,1,1]{1,0,2,3:T(8,128)(2,1)} %reshape.213) | copy-start | bytes 3145732
  474.7 7.7 %copy-start.19 = (bf16[1,512,4,256]{1,3,2,0:T(8,128)(2,1)S(1)}, bf16[1,512,4,256]{1,3,2,0:T(8,128)(2,1)}, u32[]{:S(2)}) copy-start(bf16[1,512,4,256]{1,3,2,0:T(8,128)(2,1)} %get-tuple-element.215) | copy-start | bytes 3145732
  501.0 17.7 %copy-start.20 = (bf16[512,1024]{1,0:T(8,128)(2,1)S(1)}, bf16[512,1024]{1,0:T(8,128)(2,1)}, u32[]{:S(2)}) copy-start(bf16[512,1024]{1,0:T(8,128)(2,1)} %get-tuple-element.106) | copy-start | bytes 3145732
  677.3 2.4 copy-start.23
  679.7 4.1 copy-start.11
  683.8 4.7 slice-start

commit v3 on v2

--- a/solution.py
+++ b/solution.py
@@ -609,34 +609,71 @@
     )(undealing, lengths, vecs, x_in, cot_in, shard, biases)
 
 
-def scatter_kernel(
+SMALL = 12
+
+
+def backward_kernel(
     n_dp,
     n_tensor,
-    grad_ref,
-    bias_ref,
+    lengths,
+    vec_ref,
+    lse_ref,
+    rstd_ref,
+    cot_ref,
+    full_ref,
+    q_ref,
+    k_ref,
+    v_ref,
+    mixed_ref,
+    act_ref,
+    slope_ref,
+    xt_ref,
+    ht_ref,
+    n1_ref,
+    n2_ref,
     y_ref,
     sum_ref,
-    bias_out,
+    small_out,
     y_out,
+    lts,
+    rms,
+    q_v,
+    k_v,
+    v_v,
+    n1_v,
+    n2_v,
+    cot_v,
+    acc,
+    wbuf,
+    mix_grad,
+    delta_v,
+    dqt_v,
+    kt_v,
+    dkv_v,
+    dkv_in,
+    outbox,
     from_core,
     held,
     from_chip,
     from_z,
-    bias_in,
+    small_v,
+    small_in,
+    load_sem,
+    w_sem,
+    dkv_s,
+    dkv_r,
     y_s,
     y_r,
     b_s,
     b_r,
     bo_s,
     bo_r,
-    own_sem,
     core_s,
     core_r,
     xy_s,
     xy_r,
     z_s,
     z_r,
-    out_sem,
 ):
     d, t, chip, core = place()
     chips = n_dp // 2
@@ -644,234 +681,578 @@
     half_t = n_tensor // 2
     count = n_dp * n_tensor
     me = d * n_tensor + t
-    rows, cols = grad_ref.shape[4:]
+    tokens, width = acc.shape
+    cols = wbuf.shape[2]
+    group = q_v.shape[2]
+    rows = from_z.shape[2]
     half_cols = cols // 2
+    half_width = width // 2
     pieces = KINDS * n_tensor
+    slots = held.shape[0]
+    sibling = (d + 1 - 2 * core, t)
+    length = lengths[4 * chip + t]
+    mine = pl.ds(pl.multiple_of(core * tokens, tokens), tokens)
+    others = pl.ds(pl.multiple_of((1 - core) * tokens, tokens), tokens)
     greet(n_dp, n_tensor)
 
-    def at(index):
-        k = lax.div(index, n_tensor)
-        return k, lax.rem(t + lax.rem(index, n_tensor), n_tensor)
-
-    def begin(index, carry):
-        k, tt = at(index)
-        remote(
-            grad_ref.at[k, tt, :, 1 - core],
-            from_core.at[index],
-            core_s.at[index],
-            core_r.at[index],
-            (d + 1 - 2 * core, t),
-        ).start()
-        pltpu.make_async_copy(grad_ref.at[k, tt, :, core], held.at[index], own_sem.at[index]).start()
-        return carry
-
-    lax.fori_loop(0, pieces, begin, 0)
-
-    for a in range(y_ref.shape[0]):
+    loads = [
+        pltpu.make_async_copy(src, dst, load_sem.at[i])
+        for i, (src, dst) in enumerate(
+            (
+                (cot_ref, cot_v),
+                (n2_ref, n2_v),
+                (slope_ref, rms.at[1]),
+                (act_ref, rms.at[0]),
+                (ht_ref, lts.at[1]),
+                (n1_ref, n1_v),
+                (q_ref, q_v),
+                (k_ref, k_v),
+                (v_ref, v_v),
+                (mixed_ref, rms.at[2, :, :, pl.ds(3 * group, group)]),
+                (xt_ref, lts.at[2]),
+            )
+        )
+    ]
+
+    def at(step):
+        return lax.rem(t + step, n_tensor)
+
+    def weights(k, step, slot):
+        return pltpu.make_async_copy(full_ref.at[k, at(step)], wbuf.at[slot], w_sem.at[slot])
+
+    for copy in loads[:2]:
+        copy.start()
+    weights(2, 0, 0).start()
+    for copy in loads[2:4]:
+        copy.start()
+    weights(1, 0, 1).start()
+    for copy in loads[4:]:
+        copy.start()
+
+    def send_output(a, source):
         for q in range(2):
             send_or_keep(
                 (lax.div(t, half_t) == core) & (2 * core + q == t),
-                y_ref.at[a, q],
+                source.at[q],
                 y_out.at[a, lax.rem(t, half_t)],
                 y_s.at[a, q],
                 y_r.at[a, lax.rem(t, half_t)],
                 (2 * chip + lax.div(t, half_t), 2 * core + q),
             )
 
-    def device(index):
-        return (lax.div(index, n_tensor), lax.rem(index, n_tensor))
-
-    def bias_begin(step, carry):
-        other = lax.rem(me + step, count)
+    send_output(0, y_ref)
+
+    def kind_of(index):
+        return KINDS - 1 - lax.div(index, n_tensor)
+
+    def emit(index):
+        order = lax.div(index, n_tensor)
+        tt = at(lax.rem(index, n_tensor))
+        slot, box = lax.rem(index, slots), lax.rem(index, 2)
+
+        @pl.when(index >= 2)
+        def _():
+            landed(outbox.at[0], core_s.at[index - 2])
+
+        @pl.when(index >= slots)
+        def _():
+            for half in range(2):
+                for code in range(1, chips):
+                    landed(from_chip.at[0, 0, 0], xy_s.at[index - slots, half, code])
+
+            @pl.when(lax.rem(index - slots, n_tensor) > 0)
+            def _():
+                landed(from_z.at[0, 0], z_s.at[index - slots])
+
+        def one(n, carry):
+            wide = pl.ds(pl.multiple_of(n * group, group), group)
+            left = order + jnp.where((order == 2) & (n == 3), 1, 0)
+            right = rms[order, tt, :, wide]
+            outbox[box, :, wide] = jnp.dot(
+                lts[left, 1 - core], right, preferred_element_type=F32
+            ).astype(BF)
+            held[slot, :, wide] = jnp.dot(
+                lts[left, core], right, preferred_element_type=F32
+            ).astype(BF)
+            return carry
+
+        lax.fori_loop(0, cols // group, one, 0)
         remote(
-            bias_ref.at[other], bias_in.at[step], b_s.at[step], b_r.at[step], device(other)
+            outbox.at[box], from_core.at[slot], core_s.at[index], core_r.at[index], sibling
         ).start()
-        return carry
-
-    lax.fori_loop(1, count, bias_begin, 0)
-    pltpu.make_async_copy(bias_ref.at[me], bias_in.at[0], b_r.at[0]).start()
-
-    def bias_middle():
-        def arrive(step, total):
-            landed(bias_in.at[0], b_r.at[step])
-            return total + bias_in[step]
-
-        total = lax.fori_loop(0, count, arrive, jnp.zeros(bias_in.shape[1:], F32))
-
-        def leave(step, carry):
-            landed(bias_in.at[0], b_s.at[step])
-            return carry
-
-        lax.fori_loop(1, count, leave, 0)
-        bias_in[0] = total
-        pltpu.make_async_copy(bias_in.at[0], bias_out.at[me], bo_r.at[0]).start()
-
-        def spread(step, carry):
-            other = lax.rem(me + step, count)
-            remote(
-                bias_in.at[0], bias_out.at[me], bo_s.at[step], bo_r.at[step], device(other)
-            ).start()
-            return carry
-
-        lax.fori_loop(1, count, spread, 0)
-
-    def bias_end():
-        def last(step, carry):
-            landed(bias_in.at[0], bo_r.at[step])
-            return carry
-
-        lax.fori_loop(0, count, last, 0)
-
-        def gone(step, carry):
-            landed(bias_in.at[0], bo_s.at[step])
-            return carry
-
-        lax.fori_loop(1, count, gone, 0)
+
+    def spot_of(code, order):
+        return pl.ds(pl.multiple_of(relative(chip, order, code) * rows, rows), rows)
 
     def pass_on(index, s):
+        slot = lax.rem(index, slots)
         for half in range(2):
             order = orders(bits)[half]
             for code in range(1 << s, 2 << s):
                 remote(
-                    held.at[index, relative(chip, order, code), :, pl.ds(half * half_cols, half_cols)],
-                    from_chip.at[index, half, code - 1],
+                    held.at[slot, spot_of(code, order), pl.ds(half * half_cols, half_cols)],
+                    from_chip.at[slot, half, code - 1],
                     xy_s.at[index, half, code],
                     xy_r.at[index, half, code],
                     (2 * flip(chip, order[s]) + core, t),
                 ).start()
 
     def take_in(index, s):
+        slot = lax.rem(index, slots)
         for half in range(2):
             order = orders(bits)[half]
             for code in range(1 << s, 2 << s):
                 landed(from_chip.at[0, 0, 0], xy_r.at[index, half, code])
-                spot = held.at[
-                    index,
-                    relative(chip, order, code - (1 << s)),
-                    :,
-                    pl.ds(half * half_cols, half_cols),
-                ]
-                spot[...] = (
-                    spot[...].astype(F32) + from_chip[index, half, code - 1].astype(F32)
+                spot = spot_of(code - (1 << s), order)
+                wide = pl.ds(half * half_cols, half_cols)
+                held[slot, spot, wide] = (
+                    held[slot, spot, wide].astype(F32)
+                    + from_chip[slot, half, code - 1].astype(F32)
                 ).astype(BF)
 
     def first(index):
-        landed(held.at[0], own_sem.at[index])
-        landed(held.at[0], core_r.at[index])
+        slot = lax.rem(index, slots)
+        landed(outbox.at[0], core_r.at[index])
+        part = min(128, half_width)
 
         def add(c, carry):
-            held[index, c] = (held[index, c].astype(F32) + from_core[index, c].astype(F32)).astype(BF)
+            spot = pl.ds(pl.multiple_of(c * part, part), part)
+            held[slot, spot] = (
+                held[slot, spot].astype(F32) + from_core[slot, spot].astype(F32)
+            ).astype(BF)
             return carry
 
-        lax.fori_loop(0, chips, add, 0)
+        lax.fori_loop(0, half_width // part, add, 0)
         if bits:
             pass_on(index, bits - 1)
 
     def finish(index):
-        k, tt = at(index)
-        step = lax.rem(index, n_tensor)
+        slot, step = lax.rem(index, slots), lax.rem(index, n_tensor)
+        source = pl.ds(pl.multiple_of(chip * rows, rows), rows)
+
+        @pl.when(step == 0)
+        def _():
+            from_z[kind_of(index), 0] = held[slot, source]
 
         @pl.when(step > 0)
         def _():
             remote(
-                held.at[index, chip],
-                from_z.at[k, step],
-                z_s.at[k, step],
-                z_r.at[k, step],
-                (d, tt),
+                held.at[slot, source],
+                from_z.at[kind_of(index), step],
+                z_s.at[index],
+                z_r.at[index],
+                (d, at(step)),
             ).start()
 
-    def turn(it, carry):
+    def advance(index):
+        @pl.when(index < pieces)
+        def _():
+            emit(index)
+
         for stage in range(bits + 1):
-            index = it - stage
-
-            @pl.when((index >= 0) & (index < pieces))
-            def _(stage=stage, index=index):
+            earlier = index - 1 - stage
+
+            @pl.when((earlier >= 0) & (earlier < pieces))
+            def _(stage=stage, earlier=earlier):
                 if stage == 0:
-                    first(index)
+                    first(earlier)
                 else:
-                    take_in(index, bits - stage)
+                    take_in(earlier, bits - stage)
                     if stage < bits:
-                        pass_on(index, bits - stage - 1)
+                        pass_on(earlier, bits - stage - 1)
                 if stage == bits:
-                    finish(index)
-
+                    finish(earlier)
+
+    def keep_small(which, row):
+        for r in range(8):
+            small_v[which, r : r + 1] = row[:, r * 128 : (r + 1) * 128]
+
+    chunk = 64
+
+    def norm_back(which, unit_ref, incoming, low_ref):
+        gain = vec_ref[2 + 2 * which : 3 + 2 * which]
+
+        def one(step, carry):
+            spot = pl.ds(pl.multiple_of(step * chunk, chunk), chunk)
+            e = incoming(step, spot)
+            unit = unit_ref[spot].astype(F32)
+            ge = e * gain
+            first_mean = jnp.mean(ge, axis=-1, keepdims=True)
+            second_mean = jnp.mean(ge * unit, axis=-1, keepdims=True)
+            grad = (ge - first_mean - unit * second_mean) * rstd_ref[which, spot, 0:1]
+            acc[spot] = grad
+            low = grad.astype(BF)
+            low_ref[spot] = low
+            return (
+                carry[0] + jnp.sum(e * unit, axis=0, keepdims=True),
+                carry[1] + jnp.sum(e, axis=0, keepdims=True),
+                carry[2] + jnp.sum(low.astype(F32), axis=0, keepdims=True),
+            )
+
+        zero = jnp.zeros((1, width), F32)
+        return lax.fori_loop(0, tokens // chunk, one, (zero, zero, zero))
+
+    def turn_rows(source, which):
+        flat = jnp.transpose(source)
+        for dev in range(n_dp):
+            lts[which, dev % 2, (dev // 2) * rows : (dev // 2 + 1) * rows] = flat[
+                dev * rows : (dev + 1) * rows
+            ]
+
+    loads[0].wait()
+    loads[1].wait()
+
+    def seed(step, spot):
+        number = core * tokens + step * chunk + lax.broadcasted_iota(jnp.int32, (chunk, 1), 0)
+        return jnp.where(number < length, cot_v[spot].astype(F32), 0.0)
+
+    sums = norm_back(1, n2_v, seed, cot_v)
+    keep_small(10, sums[0])
+    keep_small(11, sums[1])
+    keep_small(7, sums[2])
+    turn_rows(cot_v[...], 0)
+    for copy in loads[2:5]:
+        copy.wait()
+
+    def mlp(step, carry):
+        tt = at(step)
+        weights(2, step, 0).wait()
+
+        def one(n, carry):
+            wide = pl.ds(pl.multiple_of(n * 256, 256), 256)
+            grad = jnp.dot(cot_v[...], wbuf[0, :, wide], preferred_element_type=F32)
+            rms[1, tt, :, wide] = (rms[1, tt, :, wide].astype(F32) * grad).astype(BF)
+            return carry
+
+        lax.fori_loop(0, cols // 256, one, 0)
+
+        @pl.when(step < n_tensor - 1)
+        def _():
+            weights(2, step + 1, 0).start()
+
+        @pl.when(step == n_tensor - 1)
+        def _():
+            weights(0, 0, 0).start()
+
+        total = jnp.sum(rms[1, tt].astype(F32), axis=0, keepdims=True)
+        for r in range(8):
+            small_v[3 + tt, r : r + 1] = total[:, r * 128 : (r + 1) * 128]
+        weights(1, step, 1).wait()
+
+        def two(n, carry):
+            wide = pl.ds(pl.multiple_of(n * 256, 256), 256)
+            acc[:, wide] += lax.dot_general(
+                rms[1, tt], wbuf[1, wide, :], (((1,), (1,)), ((), ())), preferred_element_type=F32
+            )
+            return carry
+
+        lax.fori_loop(0, width // 256, two, 0)
+
+        @pl.when(step < n_tensor - 1)
+        def _():
+            weights(1, step + 1, 1).start()
+
+        @pl.when(step == n_tensor - 1)
+        def _():
+            weights(0, 1, 1).start()
+
+        advance(step)
         return carry
 
-    lax.fori_loop(0, pieces + bits, turn, 0)
-    bias_middle()
+    lax.fori_loop(0, n_tensor, mlp, 0)
+
+    loads[5].wait()
+    sums = norm_back(0, n1_v, lambda step, spot: acc[spot], n2_v)
+    keep_small(8, sums[0])
+    keep_small(9, sums[1])
+    keep_small(2, sums[2])
+    turn_rows(n2_v[...], 3)
+    for copy in loads[6:]:
+        copy.wait()
+
+    key_rows = min(256, 2 * tokens)
+    low_lanes = lax.broadcasted_iota(jnp.int32, (tokens, 2 * HEAD_DIM), 1) < HEAD_DIM
+
+    def prepare(step):
+        tt, slot = at(step), lax.rem(step, 2)
+        weights(0, step, slot).wait()
+        grad = jnp.dot(
+            n2_v[...], wbuf[slot, :, 3 * group :], preferred_element_type=F32
+        ).astype(BF)
+        mix_grad[...] = grad
+        both = grad.astype(F32) * rms[2, tt, :, 3 * group :].astype(F32)
+        high = both.astype(BF)
+        rest = (both - high.astype(F32)).astype(BF)
+        heads = lax.broadcasted_iota(jnp.int32, (8, group), 0)
+        lanes = lax.broadcasted_iota(jnp.int32, (8, group), 1)
+        picks = jnp.where(lax.div(lanes, HEAD_DIM) == heads, 1.0, 0.0).astype(BF)
+        dims = (((1,), (1,)), ((), ()))
+        delta_v[...] = lax.dot_general(
+            picks, high, dims, preferred_element_type=F32
+        ) + lax.dot_general(picks, rest, dims, preferred_element_type=F32)
+
+        @pl.when(step >= 2)
+        def _():
+            for j in range(2):
+                landed(dkv_in.at[0, 0], dkv_s.at[step - 2, j])
+
+    def pair_back(step, pair):
+        tt, slot = at(step), lax.rem(step, 2)
+        wide = pl.ds(pl.multiple_of(pair * 2 * HEAD_DIM, 2 * HEAD_DIM), 2 * HEAD_DIM)
+        q_pair, o_pair = q_v[tt, :, wide], mix_grad[:, wide]
+        q_ones = [jnp.where(low_lanes, q_pair, 0).astype(BF), jnp.where(low_lanes, 0, q_pair).astype(BF)]
+        o_ones = [jnp.where(low_lanes, o_pair, 0).astype(BF), jnp.where(low_lanes, 0, o_pair).astype(BF)]
+        kt_v[...] = jnp.transpose(k_v[tt, :, wide])
+        dqt_v[...] = jnp.zeros_like(dqt_v)
+        dims = (((1,), (1,)), ((), ()))
+
+        def block(b, carry):
+            spot = pl.ds(pl.multiple_of(b * key_rows, key_rows), key_rows)
+            k_part, v_part = k_v[tt, spot, wide], v_v[tt, spot, wide]
+            number = b * key_rows + lax.broadcasted_iota(jnp.int32, (key_rows, 1), 0)
+            live = number < length
+            dv, dk = None, None
+            for head in range(2):
+                which = tt * (group // HEAD_DIM) + pair * 2 + head
+                scores = lax.dot_general(k_part, q_ones[head], dims, preferred_element_type=F32)
+                probs = jnp.where(live, jnp.exp(scores - lse_ref[pl.ds(which, 1)]), 0.0)
+                prob_grad = lax.dot_general(v_part, o_ones[head], dims, preferred_element_type=F32)
+                score_grad = (probs * (prob_grad - delta_v[pl.ds(pair * 2 + head, 1)])).astype(BF)
+                one_v = jnp.dot(probs.astype(BF), o_ones[head], preferred_element_type=F32)
+                one_k = jnp.dot(score_grad, q_ones[head], preferred_element_type=F32)
+                dv = one_v if dv is None else dv + one_v
+                dk = one_k if dk is None else dk + one_k
+                rows_here = slice(head * HEAD_DIM, (head + 1) * HEAD_DIM)
+                dqt_v[rows_here] += jnp.dot(
+                    kt_v[rows_here, spot], score_grad, preferred_element_type=F32
+                )
+            dkv_v[slot, 0, spot, wide] = dk.astype(BF)
+            dkv_v[slot, 1, spot, wide] = dv.astype(BF)
+            return carry
+
+        lax.fori_loop(0, 2 * tokens // key_rows, block, 0)
+        dq = jnp.transpose(dqt_v[...].astype(BF).astype(F32)) * 0.125
+        rms[2, tt, :, wide] = dq.astype(BF)
+        total = jnp.sum(dq, axis=0, keepdims=True)
+        small_v[0, pl.ds(tt * (group // 128) + pair, 1)] = total
+
+    def exchange(step):
+        slot = lax.rem(step, 2)
+        for j in range(2):
+            remote(
+                dkv_v.at[slot, j, others],
+                dkv_in.at[step, j],
+                dkv_s.at[step, j],
+                dkv_r.at[step, j],
+                sibling,
+            ).start()
+
+    def collect(step):
+        tt, slot = at(step), lax.rem(step, 2)
+        for j in range(2):
+            landed(dkv_in.at[0, 0], dkv_r.at[step, j])
+            value = (
+                dkv_v[slot, j, mine].astype(F32) + dkv_in[step, j].astype(F32)
+            ).astype(BF)
+            rms[2, tt, :, (1 + j) * group : (2 + j) * group] = value
+            if j:
+                total = jnp.sum(value.astype(F32), axis=0, keepdims=True)
+                for r in range(group // 128):
+                    small_v[1, pl.ds(tt * (group // 128) + r, 1)] = total[:, r * 128 : (r + 1) * 128]
+
+        def one(n, carry):
+            wide = pl.ds(pl.multiple_of(n * 256, 256), 256)
+            acc[:, wide] += lax.dot_general(
+                rms[2, tt, :, : 3 * group],
+                wbuf[slot, wide, : 3 * group],
+                (((1,), (1,)), ((), ())),
+                preferred_element_type=F32,
+            )
+            return carry
+
+        lax.fori_loop(0, width // 256, one, 0)
+
+    def attention(step, carry):
+        @pl.when(step < n_tensor)
+        def _():
+            prepare(step)
+            for pair in range(group // (2 * HEAD_DIM)):
+                pair_back(step, pair)
+
+                @pl.when(step < 2)
+                def _(pair=pair):
+                    advance(n_tensor + 2 * step + pair)
+
+            exchange(step)
+
+        @pl.when(step >= 1)
+        def _():
+            collect(step - 1)
+
+            @pl.when(step < n_tensor - 1)
+            def _():
+                weights(0, step + 1, lax.rem(step + 1, 2)).start()
+
+            advance(2 * n_tensor + step - 1)
+
+        return carry
+
+    lax.fori_loop(0, n_tensor + 1, attention, 0)
+
+    for q in range(2):
+        cot_v[pl.ds(q * (tokens // 2), tokens // 2)] = acc[
+            pl.ds(q * (tokens // 2), tokens // 2)
+        ].astype(BF)
+    for q in range(2):
+        send_or_keep(
+            (lax.div(t, half_t) == core) & (2 * core + q == t),
+            cot_v.at[pl.ds(q * (tokens // 2), tokens // 2)],
+            y_out.at[1, lax.rem(t, half_t)],
+            y_s.at[1, q],
+            y_r.at[1, lax.rem(t, half_t)],
+            (2 * chip + lax.div(t, half_t), 2 * core + q),
+        )
+    for j in range(SMALL):
+        send_or_keep(
+            me == j,
+            small_v.at[j],
+            small_in.at[me],
+            b_s.at[j],
+            b_r.at[me],
+            (j // n_tensor, j % n_tensor),
+        )
+    advance(jnp.int32(pieces))
+
+    @pl.when(me < SMALL)
+    def _():
+        def arrive(step, total):
+            landed(small_in.at[0], b_r.at[step])
+            return total + small_in[step]
+
+        total = lax.fori_loop(0, count, arrive, jnp.zeros(small_in.shape[1:], F32))
+        small_in[0] = total
+        pltpu.make_async_copy(small_in.at[0], small_out.at[me], bo_r.at[me]).start()
+
+        def spread(step, carry):
+            other = lax.rem(me + step, count)
+            remote(
+                small_in.at[0],
+                small_out.at[me],
+                bo_s.at[step],
+                bo_r.at[me],
+                (lax.div(other, n_tensor), lax.rem(other, n_tensor)),
+            ).start()
+            return carry
+
+        lax.fori_loop(1, count, spread, 0)
+
+    for index in range(pieces + 1, pieces + 1 + bits):
+        advance(jnp.int32(index))
 
     for k in range(KINDS):
-        total = held[k * n_tensor, chip].astype(F32)
+        total = from_z[k, 0].astype(F32)
         for step in range(1, n_tensor):
-            landed(from_z.at[0, 0], z_r.at[k, step])
+            landed(from_z.at[0, 0], z_r.at[(KINDS - 1 - k) * n_tensor + step])
             total = total + from_z[k, step].astype(F32)
         sum_ref[k] = total
 
-    def close(index, carry):
-        landed(held.at[0], core_s.at[index])
+    for j in range(SMALL):
+        landed(small_v.at[0], bo_r.at[j])
+        sent(me == j, small_v.at[0], b_s.at[j])
+
+    @pl.when(me < SMALL)
+    def _():
+        def gone(step, carry):
+            landed(small_v.at[0], bo_s.at[step])
+            return carry
+
+        lax.fori_loop(1, count, gone, 0)
+
+    for a in range(2):
+        for q in range(2):
+            sent((lax.div(t, half_t) == core) & (2 * core + q == t), y_ref.at[q], y_s.at[a, q])
+            landed(y_ref.at[q], y_r.at[a, q])
+    for step in range(n_tensor - 2, n_tensor):
+        for j in range(2):
+            landed(dkv_in.at[0, 0], dkv_s.at[step, j])
+    for index in range(pieces - 2, pieces):
+        landed(outbox.at[0], core_s.at[index])
+    for index in range(pieces - slots, pieces):
         for half in range(2):
             for code in range(1, chips):
                 landed(from_chip.at[0, 0, 0], xy_s.at[index, half, code])
-        return carry
-
-    lax.fori_loop(0, pieces, close, 0)
-    for k in range(KINDS):
-        for step in range(1, n_tensor):
-            landed(from_z.at[0, 0], z_s.at[k, step])
-    for a in range(y_ref.shape[0]):
-        for q in range(2):
-            sent((lax.div(t, half_t) == core) & (2 * core + q == t), y_ref.at[a, q], y_s.at[a, q])
-            landed(y_ref.at[a, q], y_r.at[a, q])
-    bias_end()
-
-
-def scatter(n_dp, n_tensor, grads, bias, outs):
-    rows, cols = grads.shape[4:]
+        if index % n_tensor:
+            landed(from_z.at[0, 0], z_s.at[index])
+
+
+def run_backward(n_dp, n_tensor, lengths, vecs, lse, rstd, cot, full, saved):
+    tokens, width = cot.shape
+    cols = full.shape[3]
+    group = cols // 4
+    rows = width // n_dp
     chips = n_dp // 2
     pieces = KINDS * n_tensor
     count = n_dp * n_tensor
+    slots = 4
     dma = pltpu.SemaphoreType.DMA
     any_space = pl.BlockSpec(memory_space=pl.ANY)
+    smem = pl.BlockSpec(memory_space=pltpu.SMEM)
+    vmem = pl.BlockSpec(memory_space=pltpu.VMEM)
     return pl.pallas_call(
-        functools.partial(scatter_kernel, n_dp, n_tensor),
+        functools.partial(backward_kernel, n_dp, n_tensor),
         out_shape=(
             jax.ShapeDtypeStruct((KINDS, rows, cols), F32),
-            jax.ShapeDtypeStruct(bias.shape, F32),
-            jax.ShapeDtypeStruct(outs.shape, BF),
+            jax.ShapeDtypeStruct((SMALL, 8, 128), F32),
+            jax.ShapeDtypeStruct((2, 2, tokens // 2, width), BF),
         ),
-        in_specs=[any_space] * 3,
-        out_specs=(pl.BlockSpec(memory_space=pltpu.VMEM), any_space, any_space),
+        in_specs=[smem, vmem, vmem, vmem] + [any_space] * (2 + len(saved)),
+        out_specs=(vmem, any_space, any_space),
         scratch_shapes=[
-            pltpu.VMEM((pieces, chips, rows, cols), BF),
-            pltpu.VMEM((pieces, chips, rows, cols), BF),
-            pltpu.VMEM((pieces, 2, chips - 1, rows, cols // 2), BF),
+            pltpu.VMEM((4, 2, width // 2, tokens), BF),
+            pltpu.VMEM((KINDS, n_tensor, tokens, cols), BF),
+            pltpu.VMEM((n_tensor, tokens, group), BF),
+            pltpu.VMEM((n_tensor, 2 * tokens, group), BF),
+            pltpu.VMEM((n_tensor, 2 * tokens, group), BF),
+            pltpu.VMEM((tokens, width), BF),
+            pltpu.VMEM((tokens, width), BF),
+            pltpu.VMEM((tokens, width), BF),
+            pltpu.VMEM((tokens, width), F32),
+            pltpu.VMEM((2, width, cols), BF),
+            pltpu.VMEM((tokens, group), BF),
+            pltpu.VMEM((8, tokens), F32),
+            pltpu.VMEM((2 * HEAD_DIM, tokens), F32),
+            pltpu.VMEM((2 * HEAD_DIM, 2 * tokens), BF),
+            pltpu.VMEM((2, 2, 2 * tokens, group), BF),
+            pltpu.VMEM((n_tensor, 2, tokens, group), BF),
+            pltpu.VMEM((2, width // 2, cols), BF),
+            pltpu.VMEM((slots, width // 2, cols), BF),
+            pltpu.VMEM((slots, width // 2, cols), BF),
+            pltpu.VMEM((slots, 2, max(chips - 1, 1), rows, cols // 2), BF),
             pltpu.VMEM((KINDS, n_tensor, rows, cols), BF),
-            pltpu.VMEM(bias.shape, F32),
-            dma((outs.shape[0], 2)),
-            dma((outs.shape[0], 2)),
+            pltpu.VMEM((SMALL, 8, 128), F32),
+            pltpu.VMEM((count, 8, 128), F32),
+            dma((11,)),
+            dma((2,)),
+            dma((n_tensor, 2)),
+            dma((n_tensor, 2)),
+            dma((2, 2)),
+            dma((2, 2)),
+            dma((SMALL,)),
             dma((count,)),
             dma((count,)),
-            dma((count,)),
-            dma((count,)),
-            dma((pieces,)),
+            dma((SMALL,)),
             dma((pieces,)),
             dma((pieces,)),
             dma((pieces, 2, chips)),
             dma((pieces, 2, chips)),
-            dma((KINDS, n_tensor)),
-            dma((KINDS, n_tensor)),
-            dma((1,)),
+            dma((pieces,)),
+            dma((pieces,)),
         ],
         compiler_params=pltpu.CompilerParams(
             collective_id=1, has_side_effects=True, vmem_limit_bytes=VMEM_LIMIT
         ),
-        name="scatter_all",
-    )(grads, bias, outs)
-
-
-def mm(spec, left, right):
-    return jnp.einsum(spec, left, right, preferred_element_type=F32)
+        name="backward_layer",
+    )(lengths, vecs, lse, rstd, cot, full, *saved)
 
 
 def shards(
@@ -900,13 +1281,6 @@
 ):
     span, slots, width = inputs.shape
     group = query_weight.shape[1]
-    units = up_weight.shape[1]
-    half = span * n_tensor // 2
-    d, t, chip, core = place()
-    length = lengths[2 * slots * chip + t]
-    positions = core * half + jnp.arange(half)
-    valid = (positions < length).astype(F32)
-
     shard = jnp.stack(
         [
             jnp.concatenate([query_weight, key_weight, value_weight, output_weight.T], axis=1),
@@ -917,6 +1291,7 @@
     blank = jnp.zeros((group,), F32)
     biases = jnp.concatenate([query_bias, value_bias, up_bias, blank, blank]).reshape(8, group)
     vecs = jnp.stack([output_bias, down_bias, first_gain, first_shift, second_gain, second_shift])
+    vecs = jnp.pad(vecs, ((0, 2), (0, 0)))
     (
         cot_loc, full, query, key, value, mixed, activated, slope, x_t, h_t, n1, n2, y, lse, rstd
     ) = run_forward(
@@ -924,7 +1299,7 @@
         n_tensor,
         undealing,
         lengths,
-        jnp.pad(vecs, ((0, 2), (0, 0))),
+        vecs,
         jnp.transpose(inputs, (1, 0, 2)),
         jnp.transpose(cotangent, (1, 0, 2)),
         shard,
@@ -932,118 +1307,24 @@
     )
     n_col = width // cot_loc.shape[3]
     cot = cot_loc.reshape(2, n_dp // n_col, n_col, *cot_loc.shape[2:])
-    cot = jnp.transpose(cot, (0, 1, 3, 2, 4)).reshape(half, width)
-    w_qkv = full[0][:, :, : 3 * group].reshape(n_tensor, width, 3, group)
-    w_out = full[0][:, :, 3 * group :]
-    w_up, w_down = full[1], full[2]
-
-    def unturn(values):
-        return jnp.transpose(values.reshape(2, n_dp // 2, width // n_dp, half), (3, 1, 0, 2)).reshape(half, width)
-
-    x, hidden_low = unturn(x_t), unturn(h_t)
-
-    def swap(values):
-        return lax.ppermute(values, "dp", [(i, i ^ 1) for i in range(n_dp)])
-
-    heads = n_tensor * group // HEAD_DIM
-
-    def split(values):
-        values = values.reshape(n_tensor, -1, group // HEAD_DIM, HEAD_DIM)
-        return jnp.transpose(values, (0, 2, 1, 3)).reshape(heads, -1, HEAD_DIM)
-
-    def join(values):
-        return jnp.transpose(values, (1, 0, 2)).reshape(-1, n_tensor, group)
-
-    q_h, k_h, v_h = split(query), split(key), split(value)
-    log_total = lse[:heads]
-    visible = jnp.arange(2 * half) < length
-    mixed = jnp.transpose(mixed, (1, 0, 2))
-    activated = jnp.transpose(activated, (1, 0, 2))
-    slope = jnp.transpose(slope, (1, 0, 2))
-    result = y
-
-    def norm_back(e, unit, gain, inverse):
-        unit = unit.astype(F32)
-        ge = e * gain
-        grad = ge - jnp.mean(ge, -1, keepdims=True) - unit * jnp.mean(ge * unit, -1, keepdims=True)
-        return grad * inverse[:, :1], jnp.sum(e * unit, 0), jnp.sum(e, 0)
-
-    seed = cot.astype(F32) * valid[:, None]
-    grad_two, gain_two, shift_two = norm_back(seed, n2, second_gain, rstd[1])
-    mlp_grad = grad_two.astype(BF)
-    down_bias_grad = jnp.sum(mlp_grad, axis=0, dtype=F32)
-    down_grad = mm("nm,ntf->tmf", mlp_grad, activated).astype(BF)
-    act_grad = mm("nm,tmf->ntf", mlp_grad, w_down)
-    expand_grad = (slope.astype(F32) * act_grad).astype(BF)
-    up_bias_grad = jnp.sum(expand_grad, axis=0, dtype=F32)
-    up_grad = mm("nm,ntf->tmf", hidden_low, expand_grad).astype(BF)
-    hidden_grad = grad_two + mm("ntf,tmf->nm", expand_grad, w_up)
-    grad_one, gain_one, shift_one = norm_back(hidden_grad, n1, first_gain, rstd[0])
-    attn_grad = grad_one.astype(BF)
-    output_bias_grad = jnp.sum(attn_grad, axis=0, dtype=F32)
-    out_grad = mm("nm,ntc->tmc", attn_grad, mixed).astype(BF)
-    mixed_grad = split(mm("nm,tmc->tnc", attn_grad, w_out).astype(BF))
-
-    def attend_back(one):
-        q_one, k_one, v_one, total, o_one = one
-        scores = jnp.where(visible, mm("qe,ke->qk", q_one, k_one), -1000000000.0)
-        probs = jnp.exp(scores - total[:, None])
-        prob_grad = mm("qe,ke->qk", o_one, v_one)
-        value_g = mm("qk,qe->ke", probs.astype(BF), o_one)
-        inner = jnp.sum(probs * prob_grad, axis=-1, keepdims=True)
-        score_grad = (probs * (prob_grad - inner)).astype(BF)
-        query_g = mm("qk,ke->qe", score_grad, k_one)
-        key_g = mm("qk,qe->ke", score_grad, q_one)
-        return query_g.astype(BF), key_g.astype(BF), value_g.astype(BF)
-
-    query_g, key_g, value_g = lax.map(attend_back, (q_h, k_h, v_h, log_total, mixed_grad))
-
-    def collect(values):
-        parts = join(values).reshape(2, half, n_tensor, group)
-        own = jnp.where(core == 0, parts[0], parts[1])
-        other = jnp.where(core == 0, parts[1], parts[0])
-        return (own.astype(F32) + swap(other).astype(F32)).astype(BF)
-
-    query_grad = join(query_g) * jnp.asarray(0.125, BF)
-    qkv_grad = jnp.stack([query_grad, collect(key_g), collect(value_g)])
-    query_bias_grad = jnp.sum(qkv_grad[0], axis=0, dtype=F32)
-    value_bias_grad = jnp.sum(qkv_grad[2], axis=0, dtype=F32)
-    qkv_w_grad = mm("nm,jntc->tmjc", x, qkv_grad).astype(BF)
-    dealt = grad_one + mm("jntc,tmjc->nm", qkv_grad, w_qkv)
-
-    grads = jnp.stack(
-        [
-            jnp.concatenate([qkv_w_grad.reshape(n_tensor, width, 3 * group), out_grad], axis=2),
-            up_grad,
-            down_grad,
-        ]
-    ).reshape(KINDS, n_tensor, n_dp // 2, 2, width // n_dp, 4 * group)
-    parts = (
-        query_bias_grad,
-        value_bias_grad,
-        output_bias_grad,
-        up_bias_grad,
-        down_bias_grad,
-        gain_one,
-        shift_one,
-        gain_two,
-        shift_two,
+    cot = jnp.transpose(cot, (0, 1, 3, 2, 4)).reshape(2 * span, width)
+    sums, small, returned = run_backward(
+        n_dp,
+        n_tensor,
+        lengths,
+        vecs,
+        lse,
+        rstd,
+        cot,
+        full,
+        (query, key, value, mixed, activated, slope, x_t, h_t, n1, n2, y.reshape(2, span, width)),
     )
-    count = n_dp * n_tensor
-    flat = jnp.concatenate([part.reshape(-1) for part in parts])
-    flat = jnp.pad(flat.reshape(count, -1), ((0, 0), (0, 1024 - flat.shape[0] // count)))
-    outs = jnp.stack([result.astype(BF), dealt.astype(BF)]).reshape(2, 2, span, width)
-    sums, bias_sum, returned = scatter(n_dp, n_tensor, grads, flat.reshape(count, 8, 128), outs)
-
     returned = jnp.transpose(returned, (0, 2, 1, 3))
-    used = sum(part.size for part in parts) // count
-    bias_sum = bias_sum.reshape(count, 1024)[:, :used].reshape(-1)
-    sizes = [part.size for part in parts]
-    ends = [sum(sizes[: i + 1]) for i in range(len(sizes))]
-    pieces = [bias_sum[end - size : end] for end, size in zip(ends, sizes)]
-
-    def mine(values, size):
-        return lax.dynamic_slice(values, (t * size,), (size,))
+    small = small.reshape(SMALL, width)
+    t = lax.axis_index("tensor")
+
+    def mine(row):
+        return lax.dynamic_slice(small[row], (t * group,), (group,))
 
     return (
         returned[0],
@@ -1054,15 +1335,15 @@
         sums[0][:, 3 * group :].T,
         sums[1],
         sums[2].T,
-        mine(pieces[0], group),
-        mine(pieces[1], group),
-        pieces[2],
-        mine(pieces[3], units),
-        pieces[4],
-        pieces[5],
-        pieces[6],
-        pieces[7],
-        pieces[8],
+        mine(0),
+        mine(1),
+        small[2],
+        lax.dynamic_index_in_dim(small, 3 + t, 0, keepdims=False),
+        small[7],
+        small[8],
+        small[9],
+        small[10],
+        small[11],
     )
 
 

time: 703 us -> 431 us (0.61); the launches traced: 689 us -> 426 us
  matrix products: 177 us -> 0 us
  local copies, waits for them, and re-layouts: 90.2 us -> 16.9 us
  other arithmetic: 62.2 us -> 1.08 us
  Pallas kernels: 357 us -> 407 us
    dot_general x88 -> x0, matrix products: 177 us -> none  [mm(): return jnp.einsum(spec, left, right, preferred_element_type=F32)]
    pallas_call x1, Pallas kernels: 138 us -> 188 us  [run_backward(): pl.pallas_call(functools.partial(backward_kernel, n_dp, n_tensor), out_sh...]
    concatenate x3 -> x0, local copies, waits for them, and re-layouts: 30.9 us -> none  [the longest x2 30.9 us: shards(): jnp.concatenate([qkv_w_grad.reshape(n_tensor, width, 3 * group), out_grad...]
    another operation x11 -> x3, other arithmetic: 28.8 us -> 0.03 us  [the longest x1 16.7 us: shards(): jnp.stack([jnp.concatenate([qkv_w_grad.reshape(n_tensor, width, 3 * group...]
    slice x9 -> x0, local copies, waits for them, and re-layouts: 18.3 us -> none  [the longest x2 14.6 us: shards(): w_qkv = full[0][:, :, :3 * group].reshape(n_tensor, width, 3, group)]
    lt x16 -> x0, other arithmetic: 10.4 us -> none  [shards(): visible = jnp.arange(2 * half) < length]
    unnamed x93 -> x42, local copies, waits for them, and re-layouts: 16.2 us -> 6.17 us
    squeeze x2 -> x1, local copies, waits for them, and re-layouts: 7.71 us -> 0.61 us  [shards(): small[11]]
  transfers between devices with their start and end apart: 2 -> 0, of which waited for: 0 -> 0; matrix products, arithmetic and copies ran while one was open for 8% -> 0% of each run, Pallas kernels for 0% -> 0%
where the time goes in v3:
time: 431 us; the launch traced here: 426 us
  Pallas kernels  407 us (94%)
  local copies, waits for them, and re-layouts  16.9 us (4%)
    pallas_call x1, Pallas kernels, run_forward(): pl.pallas_call(functools.partial(forward_kernel, n_dp, n_tensor), out_sha...  219 us
    pallas_call x1, Pallas kernels, run_backward(): pl.pallas_call(functools.partial(backward_kernel, n_dp, n_tensor), out_sh...  188 us

profile of v3, /device:TPU:0, one launch (start us, length us, event | category | flops | bytes accessed | tf_op | source)
XLA Modules:
  0.0 425.6 jit_solution(14133836566546548117)
XLA Ops:
  0.7 0.0 copy-start.8
  0.7 0.0 copy-start.9
  0.7 0.0 copy-start.10
  0.7 0.0 copy-start.11
  0.7 0.0 copy-start.12
  0.7 0.0 copy-start.13
  0.7 0.0 copy-start.4
  0.7 0.0 copy-start.5
  0.7 0.0 copy-start.6
  0.8 0.0 copy-start.7
  0.8 0.0 copy-start.1
  0.8 3.6 copy_bitcast_fusion
  4.4 0.0 copy-start.2
  4.4 0.0 copy-done.8
  4.4 0.0 copy-done.9
  4.4 0.0 copy-done.10
  4.4 0.0 copy-done.11
  4.4 0.0 copy-done.12
  4.4 0.0 copy-done.13
  4.4 0.1 stack.43
  4.5 0.6 pad.4.vec_ref
  5.1 0.0 copy-done.4
  5.1 0.1 copy.38
  5.2 0.0 copy-done.5
  5.2 0.0 copy-start.14
  5.2 0.0 copy-start.15
  5.2 0.0 copy-start.16
  5.3 0.0 copy-done.6
  5.3 0.0 copy-done.7
  5.4 0.0 copy-done.1
  5.4 0.1 copy.39
  5.5 0.0 copy-done.2
  5.6 1.0 pad_maximum_fusion.shard_ref
  6.5 0.0 copy-done.14
  6.5 0.0 copy-done.15
  6.5 0.0 copy-done.16
  6.6 0.6 reshape.59.bias_ref
  7.2 219.0 %forward_layer.1 = (bf16[2,8,32,1024]{3,2,1,0:T(8,128)(2,1)}, bf16[3,4,1024,1024]{3,2,1,0:T(8,128)(2,1)}, bf16[4,512,256]{2,1,0:T(8,128)(2,1)}, bf16[4,1024,256]...) custom-call(s32[16]{0:T(128)} %undealing.1, ...), custom_call_target="tpu_custom_call" | custom-call | tf_op jit(solution)/shard_map/forward_layer/pallas_call | solution.py:561
  226.2 187.7 %backward_layer.1 = (f32[3,128,1024]{2,1,0:T(8,128)}, f32[12,8,128]{2,1,0:T(8,128)}, bf16[2,2,256,1024]{3,2,1,0:T(8,128)(2,1)}) custom-call(s32[16]{0:T(128)} %lengths.3, f32[8,1024]{1,0:T(8,128)} %pad.4.vec_ref, f32[128,512]{1,0:T(8,128)} %get-tuple-element.35.lse_ref, f32[2,512,128]{2,1,0:T(8,128)} %get-tuple-element.36.rstd_ref, ...), custom_call_target="tpu_custom_call" | custom-call | tf_op jit(solution)/shard_map/backward_layer/pallas_call | solution.py:1201
  413.9 1.7 slice_bitcast_fusion
  415.6 0.0 copy-start
  415.6 2.0 copy.40
  417.6 2.0 copy.41
  419.7 0.0 copy-done
  419.7 0.0 copy-start.3
  419.7 0.9 slice_bitcast_fusion.2
  420.6 0.8 slice_bitcast_fusion.5
  421.3 0.8 copy.42
  422.1 1.0 copy.43
  423.1 0.0 copy-done.3
  423.1 0.6 constant_dynamic-slice_fusion
  423.7 0.6 slice_bitcast_fusion.6
  424.4 0.6 dynamic_slice.10
  425.0 0.6 dynamic_slice.11
  (9 shorter events, 0.1 us)
Async XLA Ops:
  0.7 3.7 copy-start.8
  0.7 3.7 copy-start.9
  0.7 3.7 copy-start.10
  0.7 3.7 copy-start.11
  0.7 3.7 copy-start.12
  0.7 3.7 copy-start.13
  0.7 4.4 %copy-start.4 = (f32[256,128]{1,0:T(8,128)S(1)}, f32[256,128]{1,0:T(8,128)}, u32[]{:S(2)}) copy-start(f32[256,128]{1,0:T(8,128)} %param.27) | copy-start | bytes 393220
  0.7 4.5 %copy-start.5 = (f32[128,256]{1,0:T(8,128)S(1)}, f32[128,256]{1,0:T(8,128)}, u32[]{:S(2)}) copy-start(f32[128,256]{1,0:T(8,128)} %param.24) | copy-start | bytes 393220
  0.7 4.5 %copy-start.6 = (f32[128,256]{1,0:T(8,128)S(1)}, f32[128,256]{1,0:T(8,128)}, u32[]{:S(2)}) copy-start(f32[128,256]{1,0:T(8,128)} %param.25) | copy-start | bytes 393220
  0.8 4.5 %copy-start.7 = (f32[128,256]{1,0:T(8,128)S(1)}, f32[128,256]{1,0:T(8,128)}, u32[]{:S(2)}) copy-start(f32[128,256]{1,0:T(8,128)} %param.26) | copy-start | bytes 393220
  0.8 4.6 %copy-start.1 = (f32[1024,128]{1,0:T(8,128)S(1)}, f32[1024,128]{1,0:T(8,128)}, u32[]{:S(2)}) copy-start(f32[1024,128]{1,0:T(8,128)} %param.29) | copy-start | bytes 1572868
  4.4 1.1 copy-start.2
  5.2 1.3 copy-start.14
  5.2 1.3 copy-start.15
  5.2 1.3 copy-start.16
  415.6 4.1 copy-start
  419.7 3.4 copy-start.3

commit v4 on v3

v4 whole, which is shorter than its diff:
```python
import functools

import jax
import jax.numpy as jnp
from jax import lax
from jax.experimental import pallas as pl
from jax.experimental.pallas import tpu as pltpu
from jax.sharding import PartitionSpec as P

HEAD_DIM = 64
KINDS = 3
MESH = pl.DeviceIdType.MESH
VMEM_LIMIT = 63 << 20
BF = jnp.bfloat16
F32 = jnp.float32


def flip(index, bit):
    unit = 1 << bit
    return index + unit * (1 - 2 * lax.rem(lax.div(index, unit), 2))


def orders(bits):
    return (tuple(range(bits)), tuple(reversed(range(bits))))


def relative(chip, order, code):
    for place, bit in enumerate(order):
        if code >> place & 1:
            chip = flip(chip, bit)
    return chip


def place():
    d, t = lax.axis_index("dp"), lax.axis_index("tensor")
    return d, t, lax.div(d, 2), lax.rem(d, 2)


def greet(n_dp, n_tensor):
    d, t, _, _ = place()
    barrier = pltpu.get_barrier_semaphore()
    me = d * n_tensor + t
    count = n_dp * n_tensor

    def one(step, carry):
        other = lax.rem(me + step, count)
        pl.semaphore_signal(
            barrier,
            inc=1,
            device_id=(lax.div(other, n_tensor), lax.rem(other, n_tensor)),
            device_id_type=MESH,
        )
        return carry

    lax.fori_loop(1, count, one, 0)
    pl.semaphore_wait(barrier, count - 1)


def remote(src, dst, ssem, rsem, device):
    return pltpu.make_async_remote_copy(
        src_ref=src,
        dst_ref=dst,
        send_sem=ssem,
        recv_sem=rsem,
        device_id=device,
        device_id_type=MESH,
    )


def landed(ref, sem):
    pltpu.make_async_copy(ref, ref, sem).wait()


def send_or_keep(mine, src, dst, ssem, rsem, device):
    @pl.when(mine)
    def _():
        pltpu.make_async_copy(src, dst, rsem).start()

    @pl.when(jnp.logical_not(mine))
    def _():
        remote(src, dst, ssem, rsem, device).start()


def sent(mine, src, ssem):
    @pl.when(jnp.logical_not(mine))
    def _():
        landed(src, ssem)


LAG = 2
SMALL = 12
SLOTS = 4
COT_ONE, COT_TWO = 3, 8


def layer_kernel(
    n_dp,
    n_tensor,
    undealing,
    lengths,
    vec_ref,
    x_ref,
    cot_ref,
    shard_ref,
    bias_ref,
    full_ref,
    sum_ref,
    small_out,
    y_out,
    c_one,
    c_two,
    bias_v,
    wbuf,
    q_v,
    k_v,
    v_v,
    lts,
    rms,
    n1_v,
    n2_v,
    cot_v,
    y_v,
    acc,
    lse_v,
    lse_rows,
    rstd_v,
    mix_grad,
    delta_v,
    dqt_v,
    kt_v,
    dkv_v,
    dkv_in,
    outbox,
    from_core,
    held,
    from_chip,
    from_z,
    small_v,
    small_in,
    x_s,
    x_r,
    c1_s,
    c1_r,
    c2_s,
    c2_r,
    own_sem,
    gz_s,
    gz_r,
    gxy_s,
    gxy_r,
    sib_s,
    sib_r,
    kv_s,
    kv_r,
    bz_s,
    bz_r,
    w_sem,
    dkv_s,
    dkv_r,
    y_s,
    y_r,
    b_s,
    b_r,
    bo_s,
    bo_r,
    core_s,
    core_r,
    xy_s,
    xy_r,
    z_s,
    z_r,
):
    d, t, chip, core = place()
    chips = n_dp // 2
    bits = chips.bit_length() - 1
    half_t = n_tensor // 2
    count = n_dp * n_tensor
    me = d * n_tensor + t
    rows, cols = shard_ref.shape[1:]
    half_cols = cols // 2
    group = q_v.shape[2]
    span, width = x_ref.shape[1:]
    half_width = width // 2
    tokens = 2 * span
    units = cols
    prow, pcol = c_one.shape[2:]
    n_col = width // pcol
    pieces = KINDS * n_tensor
    sibling = (d + 1 - 2 * core, t)
    length = lengths[4 * chip + t]
    mine = pl.ds(pl.multiple_of(core * tokens, tokens), tokens)
    others = pl.ds(pl.multiple_of((1 - core) * tokens, tokens), tokens)
    greet(n_dp, n_tensor)

    def block(k, tt, who, half):
        return full_ref.at[
            k,
            tt,
            pl.ds(pl.multiple_of((2 * who + core) * rows, rows), rows),
            pl.ds(half * half_cols, half_cols),
        ]

    def arriving(index):
        rest, others = index - KINDS, n_tensor - 1
        return jnp.where(
            index < KINDS,
            index * n_tensor,
            lax.div(rest, others) * n_tensor + 1 + lax.rem(rest, others),
        )

    def stripe(k, tt):
        return full_ref.at[k, tt, pl.ds(pl.multiple_of(d * rows, rows), rows)]

    def at(index):
        step = lax.rem(index, n_tensor)
        near = jnp.where(t < half_t, t, n_tensor - 1 - t)
        spot = jnp.where(step <= near, near - step, step)
        return lax.div(index, n_tensor), jnp.where(t < half_t, spot, n_tensor - 1 - spot)

    for k in range(KINDS):
        pltpu.make_async_copy(shard_ref.at[k], stripe(k, t), own_sem.at[k]).start()

    def relay(index):
        k, tt = at(index)

        @pl.when(tt != t)
        def _():
            landed(shard_ref.at[0], gz_r.at[k, tt])

        for way, wanted in ((1, (tt <= t) & (t < n_tensor - 1)), (0, (tt >= t) & (t > 0))):

            @pl.when(wanted)
            def _(way=way):
                remote(
                    stripe(k, tt),
                    stripe(k, tt),
                    gz_s.at[k, tt, way],
                    gz_r.at[k, tt],
                    (d, t + 2 * way - 1),
                ).start()

    def relayed(k, tt):
        for way, wanted in ((1, (tt <= t) & (t < n_tensor - 1)), (0, (tt >= t) & (t > 0))):

            @pl.when(wanted)
            def _(way=way):
                landed(shard_ref.at[0], gz_s.at[k, tt, way])

    def start_tokens():
        for s in range(2):
            send_or_keep(
                (lax.div(t, half_t) == core) & (2 * core + s == t),
                x_ref.at[s],
                outbox.at[0, pl.ds(pl.multiple_of(lax.rem(t, half_t) * span, span), span)],
                x_s.at[s],
                x_r.at[lax.rem(t, half_t)],
                (2 * chip + lax.div(t, half_t), 2 * core + s),
            )
        pltpu.make_async_copy(bias_ref, bias_v.at[t], bz_r.at[0]).start()
        for step in range(1, n_tensor):
            remote(
                bias_ref,
                bias_v.at[t],
                bz_s.at[step],
                bz_r.at[step],
                (d, lax.rem(t + step, n_tensor)),
            ).start()

    def piece(who):
        return cot_ref.at[
            :,
            pl.ds(pl.multiple_of(lax.div(who, n_col) * prow, prow), prow),
            pl.ds(pl.multiple_of(lax.rem(who, n_col) * pcol, pcol), pcol),
        ]

    def cot_first():
        pltpu.make_async_copy(piece(d), c_one.at[d], c1_r.at[0]).start()
        for step in range(1, n_dp):
            who = lax.rem(d + step, n_dp)
            remote(piece(who), c_one.at[d], c1_s.at[step], c1_r.at[step], (who, t)).start()

    def cot_second():
        for step in range(n_dp):
            landed(c_one.at[0], c1_r.at[step])
        count = 2 * n_dp
        for step in range(count):
            seq = lax.rem(4 * chip + step, count)
            slot = undealing[seq]
            c_two[seq] = c_one[lax.div(slot, 2), lax.rem(slot, 2)]
            goal = 2 * lax.div(seq, 4) + lax.div(t, half_t)
            send_or_keep(
                (goal == d) & (lax.rem(seq, 4) == t),
                c_two.at[seq],
                cot_v.at[
                    pl.ds(
                        pl.multiple_of(lax.rem(t, half_t) * span + lax.div(d, n_col) * prow, prow),
                        prow,
                    ),
                    pl.ds(pl.multiple_of(lax.rem(d, n_col) * pcol, pcol), pcol),
                ],
                c2_s.at[step],
                c2_r.at[lax.rem(t, half_t), d],
                (goal, lax.rem(seq, 4)),
            )

    def forward(k, tt, half, code):
        order = orders(bits)[half]
        ref = block(k, tt, relative(chip, order, code), half)
        for s in range(code.bit_length(), bits):
            target = code | 1 << s
            remote(
                ref,
                ref,
                gxy_s.at[k, tt, half],
                gxy_r.at[k, tt, half, target],
                (2 * flip(chip, order[s]) + core, t),
            ).start()
        remote(
            ref, ref, sib_s.at[k, tt, half], sib_r.at[k, tt, half, code], sibling
        ).start()

    def receive(index, codes):
        k, tt = at(arriving(index))
        for code in codes:
            for half in range(2):
                landed(block(k, tt, chip, half), gxy_r.at[k, tt, half, code])
                forward(k, tt, half, code)

    early, late = range(1, max(chips // 2, 1)), range(max(chips // 2, 1), chips)

    def comm_step(index):
        follow = index + KINDS
        others = n_tensor - 1

        @pl.when(follow < pieces)
        def _():
            relay(arriving(follow))

            @pl.when((lax.rem(index, others) == others - 1) & (follow + 1 < pieces))
            def _():
                relay(lax.div(index, others) * n_tensor + n_tensor)

        @pl.when((index + 2 >= KINDS) & (index + 2 < pieces))
        def _():
            k, tt = at(arriving(index + 2))
            for half in range(2):
                forward(k, tt, half, 0)

        @pl.when(index < pieces)
        def _():
            receive(index, early)

        @pl.when(index >= LAG)
        def _():
            receive(index - LAG, late)

    def load(index):
        k, tt = at(index)
        slot = lax.rem(index, 2)
        for half in range(2):
            for code in range(chips):
                landed(block(k, tt, chip, half), sib_r.at[k, tt, half, code])
        copy = pltpu.make_async_copy(full_ref.at[k, tt], wbuf.at[slot], w_sem.at[slot])
        copy.start()
        copy.wait()

    def project(index):
        _, tt = at(index)
        slot = lax.rem(index, 2)
        x = outbox[0]
        for c in range(3):
            out = jnp.dot(
                x, wbuf[slot, :, c * group : (c + 1) * group], preferred_element_type=F32
            )
            if c == 0:
                q_v[tt] = ((out + bias_v[tt, 0:1]) * 0.125).astype(BF)
            elif c == 1:
                k_v[tt, mine] = out.astype(BF)
            else:
                v_v[tt, mine] = (out + bias_v[tt, 1:2]).astype(BF)
        for j, ref in enumerate((k_v, v_v)):
            remote(
                ref.at[tt, mine], ref.at[tt, mine], kv_s.at[tt, j], kv_r.at[tt, j], sibling
            ).start()

    def attend(index):
        _, tt = at(index)
        slot = lax.rem(index, 2)
        for j, ref in enumerate((k_v, v_v)):
            landed(ref.at[tt, mine], kv_r.at[tt, j])
        block_rows = min(256, tokens)
        low = lax.broadcasted_iota(jnp.int32, (block_rows, 2 * HEAD_DIM), 1) < HEAD_DIM
        lanes = lax.broadcasted_iota(jnp.int32, (block_rows, lse_v.shape[1]), 1)
        live = lax.broadcasted_iota(jnp.int32, (1, 2 * tokens), 1) < length

        def pair_step(step, carry):
            pair, part = lax.div(step, tokens // block_rows), lax.rem(step, tokens // block_rows)
            wide = pl.ds(pl.multiple_of(pair * 2 * HEAD_DIM, 2 * HEAD_DIM), 2 * HEAD_DIM)
            spot = pl.ds(pl.multiple_of(part * block_rows, block_rows), block_rows)
            k_pair, v_pair = k_v[tt, :, wide], v_v[tt, :, wide]
            q_pair = q_v[tt, spot, wide]
            outs = []
            for head in range(2):
                q_one = jnp.where(low if head == 0 else jnp.logical_not(low), q_pair, 0).astype(BF)
                scores = lax.dot_general(
                    q_one, k_pair, (((1,), (1,)), ((), ())), preferred_element_type=F32
                )
                scores = jnp.where(live, scores, -1000000000.0)
                summit = jnp.max(scores, axis=-1, keepdims=True)
                raised = jnp.exp(scores - summit)
                total = jnp.sum(raised, axis=-1, keepdims=True)
                out = jnp.dot(raised.astype(BF), v_pair, preferred_element_type=F32)
                outs.append(out / total)
                number = tt * (group // HEAD_DIM) + pair * 2 + head
                lse_v[spot] = jnp.where(lanes == number, summit + jnp.log(total), lse_v[spot])
            rms[2, tt, spot, pl.ds(pl.multiple_of(3 * group + pair * 2 * HEAD_DIM, 2 * HEAD_DIM), 2 * HEAD_DIM)] = jnp.where(low, outs[0], outs[1]).astype(BF)
            return carry

        lax.fori_loop(0, (group // (2 * HEAD_DIM)) * (tokens // block_rows), pair_step, 0)
        for n in range(width // 256):
            acc[:, n * 256 : (n + 1) * 256] += lax.dot_general(
                rms[2, tt, :, 3 * group :],
                wbuf[slot, n * 256 : (n + 1) * 256, 3 * group :],
                (((1,), (1,)), ((), ())),
                preferred_element_type=F32,
            )

    chunk = 64

    def norm(which, keep):
        gain, shift = vec_ref[2 + 2 * which : 3 + 2 * which], vec_ref[3 + 2 * which : 4 + 2 * which]

        def one(step, carry):
            spot = pl.ds(pl.multiple_of(step * chunk, chunk), chunk)
            value = acc[spot]
            center = value - jnp.mean(value, axis=-1, keepdims=True)
            spread = jnp.mean(center * center, axis=-1, keepdims=True)
            inverse = lax.rsqrt(spread + 1e-05)
            unit = center * inverse
            rstd_v[which, spot] = jnp.broadcast_to(inverse, (chunk, rstd_v.shape[2]))
            keep(spot, unit, unit * gain + shift)
            return carry

        lax.fori_loop(0, tokens // chunk, one, 0)

    def keep_one(spot, unit, hidden):
        n1_v[spot] = unit.astype(BF)
        outbox[1, spot] = hidden.astype(BF)
        acc[spot] = hidden + vec_ref[1:2]

    def keep_two(spot, unit, hidden):
        n2_v[spot] = unit.astype(BF)
        y_v[spot] = hidden.astype(BF)

    def turn_rows(source, which):
        flat = jnp.transpose(source)
        for dev in range(n_dp):
            lts[which, dev % 2, (dev // 2) * rows : (dev // 2 + 1) * rows] = flat[
                dev * rows : (dev + 1) * rows
            ]

    def expand(index):
        _, tt = at(index)
        slot = lax.rem(index, 2)

        def one(n, carry):
            wide = pl.ds(pl.multiple_of(n * 256, 256), 256)
            u = jnp.dot(outbox[1], wbuf[slot, :, wide], preferred_element_type=F32)
            u = u + bias_v[tt, pl.ds(2 + n, 1)]
            bell, below = gauss(u)
            rms[0, tt, :, wide] = (u * below).astype(BF)
            rms[1, tt, :, wide] = (below + u * bell).astype(BF)
            return carry

        lax.fori_loop(0, units // 256, one, 0)

    def contract(index):
        _, tt = at(index)
        slot = lax.rem(index, 2)

        def one(n, carry):
            wide = pl.ds(pl.multiple_of(n * 256, 256), 256)
            acc[:, wide] += lax.dot_general(
                rms[0, tt], wbuf[slot, wide, :], (((1,), (1,)), ((), ())), preferred_element_type=F32
            )
            return carry

        lax.fori_loop(0, width // 256, one, 0)

    landed(shard_ref.at[0], own_sem.at[0])
    relay(jnp.int32(0))
    start_tokens()
    for k in range(KINDS):
        if k:
            landed(shard_ref.at[0], own_sem.at[k])
        for half in range(2):
            forward(k, t, half, 0)
    for s in range(2):
        landed(x_ref.at[s], x_r.at[s])
    for step in range(n_tensor):
        landed(bias_ref, bz_r.at[step])
    acc[...] = outbox[0].astype(F32) + vec_ref[0:1]
    turn_rows(outbox[0], 2)
    lse_v[...] = jnp.zeros_like(lse_v)

    def turn(index, carry):
        comm_step(index)
        done = index - LAG

        @pl.when((done == 1) | ((done >= 4) & (done <= 6)))
        def _():
            attend(jnp.where(done == 1, 0, done - 3))

        @pl.when((done == 0) | ((done >= 3) & (done <= 5)))
        def _():
            group_index = jnp.where(done == 0, 0, done - 2)
            load(group_index)
            project(group_index)

        @pl.when(index == COT_ONE)
        def _():
            cot_first()

        @pl.when(index == COT_TWO)
        def _():
            cot_second()

        @pl.when(done == 6)
        def _():
            norm(0, keep_one)
            turn_rows(outbox[1], 1)
            lse_rows[...] = jnp.transpose(lse_v[...])

        def up(step, carry):
            load(step)
            expand(step)
            return carry

        def down(step, carry):
            load(step)
            contract(step)
            return carry

        lax.fori_loop(
            jnp.where(done == 8, 6, 4), jnp.where(done == 7, 6, jnp.where(done == 8, 8, 4)), up, 0
        )
        lax.fori_loop(
            jnp.where(done == 9, 8, jnp.where(done > 9, done, 8)),
            jnp.where(done == 9, 10, jnp.where(done > 9, done + 1, 8)),
            down,
            0,
        )
        return carry

    lax.fori_loop(0, pieces + LAG, turn, 0)
    norm(1, keep_two)

    def rat(step):
        return lax.rem(t + 1 + step, n_tensor)

    def weights(k, step, slot):
        return pltpu.make_async_copy(full_ref.at[k, rat(step)], wbuf.at[slot], w_sem.at[slot])

    def send_output(a, source):
        for q in range(2):
            send_or_keep(
                (lax.div(t, half_t) == core) & (2 * core + q == t),
                source.at[pl.ds(q * span, span)],
                y_out.at[a, lax.rem(t, half_t)],
                y_s.at[a, q],
                y_r.at[a, lax.rem(t, half_t)],
                (2 * chip + lax.div(t, half_t), 2 * core + q),
            )


    def kind_of(index):
        return KINDS - 1 - lax.div(index, n_tensor)

    def emit(index):
        order = lax.div(index, n_tensor)
        tt = rat(lax.rem(index, n_tensor))
        slot, box = lax.rem(index, SLOTS), lax.rem(index, 2)

        @pl.when(index >= 2)
        def _():
            landed(outbox.at[0], core_s.at[index - 2])

        @pl.when(index >= SLOTS)
        def _():
            for half in range(2):
                landed(from_chip.at[0, 0], xy_s.at[index - SLOTS, half])

            @pl.when(lax.rem(index - SLOTS, n_tensor) < n_tensor - 1)
            def _():
                landed(from_z.at[0, 0], z_s.at[index - SLOTS])

        def one(n, carry):
            wide = pl.ds(pl.multiple_of(n * group, group), group)
            left = order + jnp.where((order == 2) & (n == 3), 1, 0)
            right = rms[order, tt, :, wide]
            outbox[box, :, wide] = jnp.dot(
                lts[left, 1 - core], right, preferred_element_type=F32
            ).astype(BF)
            held[slot, :, wide] = jnp.dot(
                lts[left, core], right, preferred_element_type=F32
            ).astype(BF)
            return carry

        lax.fori_loop(0, cols // group, one, 0)
        remote(
            outbox.at[box], from_core.at[slot], core_s.at[index], core_r.at[index], sibling
        ).start()

    def spot_of(code, order):
        return pl.ds(pl.multiple_of(relative(chip, order, code) * rows, rows), rows)

    def pass_on(index, s):
        slot = lax.rem(index, SLOTS)
        for half in range(2):
            order = orders(bits)[half]
            for code in range(1 << s, 2 << s):
                remote(
                    held.at[slot, spot_of(code, order), pl.ds(half * half_cols, half_cols)],
                    from_chip.at[slot, half, code - 1],
                    xy_s.at[index, half],
                    xy_r.at[index, half, code],
                    (2 * flip(chip, order[s]) + core, t),
                ).start()

    def take_in(index, s):
        slot = lax.rem(index, SLOTS)
        for half in range(2):
            order = orders(bits)[half]
            for code in range(1 << s, 2 << s):
                landed(from_chip.at[0, 0, 0], xy_r.at[index, half, code])
                spot = spot_of(code - (1 << s), order)
                wide = pl.ds(half * half_cols, half_cols)
                held[slot, spot, wide] = (
                    held[slot, spot, wide].astype(F32)
                    + from_chip[slot, half, code - 1].astype(F32)
                ).astype(BF)

    def first(index):
        slot = lax.rem(index, SLOTS)
        landed(outbox.at[0], core_r.at[index])
        part = min(128, half_width)

        def add(c, carry):
            spot = pl.ds(pl.multiple_of(c * part, part), part)
            held[slot, spot] = (
                held[slot, spot].astype(F32) + from_core[slot, spot].astype(F32)
            ).astype(BF)
            return carry

        lax.fori_loop(0, half_width // part, add, 0)
        if bits:
            pass_on(index, bits - 1)

    def finish(index):
        slot, step = lax.rem(index, SLOTS), lax.rem(index, n_tensor)
        source = pl.ds(pl.multiple_of(chip * rows, rows), rows)

        @pl.when(step == n_tensor - 1)
        def _():
            from_z[kind_of(index), step] = held[slot, source]

        @pl.when(step < n_tensor - 1)
        def _():
            remote(
                held.at[slot, source],
                from_z.at[kind_of(index), step],
                z_s.at[index],
                z_r.at[index],
                (d, rat(step)),
            ).start()

    def advance(index):
        @pl.when(index < pieces)
        def _():
            emit(index)

        for stage in range(bits + 1):
            earlier = index - 1 - stage

            @pl.when((earlier >= 0) & (earlier < pieces))
            def _(stage=stage, earlier=earlier):
                if stage == 0:
                    first(earlier)
                else:
                    take_in(earlier, bits - stage)
                    if stage < bits:
                        pass_on(earlier, bits - stage - 1)
                if stage == bits:
                    finish(earlier)

    def keep_small(which, row):
        for r in range(8):
            small_v[which, r : r + 1] = row[:, r * 128 : (r + 1) * 128]

    def norm_back(which, unit_ref, incoming, low_ref):
        gain = vec_ref[2 + 2 * which : 3 + 2 * which]

        def one(step, carry):
            spot = pl.ds(pl.multiple_of(step * chunk, chunk), chunk)
            e = incoming(step, spot)
            unit = unit_ref[spot].astype(F32)
            ge = e * gain
            first_mean = jnp.mean(ge, axis=-1, keepdims=True)
            second_mean = jnp.mean(ge * unit, axis=-1, keepdims=True)
            grad = (ge - first_mean - unit * second_mean) * rstd_v[which, spot, 0:1]
            acc[spot] = grad
            low = grad.astype(BF)
            low_ref[spot] = low
            return (
                carry[0] + jnp.sum(e * unit, axis=0, keepdims=True),
                carry[1] + jnp.sum(e, axis=0, keepdims=True),
                carry[2] + jnp.sum(low.astype(F32), axis=0, keepdims=True),
            )

        zero = jnp.zeros((1, width), F32)
        return lax.fori_loop(0, tokens // chunk, one, (zero, zero, zero))

    for q in range(half_t):
        for who in range(n_dp):
            landed(c_two.at[0], c2_r.at[q, who])
    weights(2, 0, 0).start()
    weights(1, 0, 1).start()
    send_output(0, y_v)

    def seed(step, spot):
        number = core * tokens + step * chunk + lax.broadcasted_iota(jnp.int32, (chunk, 1), 0)
        return jnp.where(number < length, cot_v[spot].astype(F32), 0.0)

    sums = norm_back(1, n2_v, seed, cot_v)
    keep_small(10, sums[0])
    keep_small(11, sums[1])
    keep_small(7, sums[2])
    turn_rows(cot_v[...], 0)
    advance(jnp.int32(0))

    def mlp(step, carry):
        tt = rat(step)
        weights(2, step, 0).wait()

        def one(n, carry):
            wide = pl.ds(pl.multiple_of(n * 256, 256), 256)
            grad = jnp.dot(cot_v[...], wbuf[0, :, wide], preferred_element_type=F32)
            rms[1, tt, :, wide] = (rms[1, tt, :, wide].astype(F32) * grad).astype(BF)
            return carry

        lax.fori_loop(0, cols // 256, one, 0)

        @pl.when(step < n_tensor - 1)
        def _():
            weights(2, step + 1, 0).start()

        @pl.when(step == n_tensor - 1)
        def _():
            weights(0, 0, 0).start()

        total = jnp.sum(rms[1, tt].astype(F32), axis=0, keepdims=True)
        for r in range(8):
            small_v[3 + tt, r : r + 1] = total[:, r * 128 : (r + 1) * 128]
        weights(1, step, 1).wait()

        def two(n, carry):
            wide = pl.ds(pl.multiple_of(n * 256, 256), 256)
            acc[:, wide] += lax.dot_general(
                rms[1, tt], wbuf[1, wide, :], (((1,), (1,)), ((), ())), preferred_element_type=F32
            )
            return carry

        lax.fori_loop(0, width // 256, two, 0)

        @pl.when(step < n_tensor - 1)
        def _():
            weights(1, step + 1, 1).start()

        @pl.when(step == n_tensor - 1)
        def _():
            weights(0, 1, 1).start()

        @pl.when(lax.rem(step, 2) == 1)
        def _():
            advance(1 + lax.div(step, 2))

        return carry

    lax.fori_loop(0, n_tensor, mlp, 0)

    sums = norm_back(0, n1_v, lambda step, spot: acc[spot], n2_v)
    keep_small(8, sums[0])
    keep_small(9, sums[1])
    keep_small(2, sums[2])
    turn_rows(n2_v[...], 3)

    key_rows = min(256, 2 * tokens)
    low_lanes = lax.broadcasted_iota(jnp.int32, (tokens, 2 * HEAD_DIM), 1) < HEAD_DIM

    def prepare(step):
        tt, slot = rat(step), lax.rem(step, 2)
        weights(0, step, slot).wait()
        grad = jnp.dot(
            n2_v[...], wbuf[slot, :, 3 * group :], preferred_element_type=F32
        ).astype(BF)
        mix_grad[...] = grad
        both = grad.astype(F32) * rms[2, tt, :, 3 * group :].astype(F32)
        high = both.astype(BF)
        rest = (both - high.astype(F32)).astype(BF)
        heads = lax.broadcasted_iota(jnp.int32, (8, group), 0)
        lanes = lax.broadcasted_iota(jnp.int32, (8, group), 1)
        picks = jnp.where(lax.div(lanes, HEAD_DIM) == heads, 1.0, 0.0).astype(BF)
        dims = (((1,), (1,)), ((), ()))
        delta_v[...] = lax.dot_general(
            picks, high, dims, preferred_element_type=F32
        ) + lax.dot_general(picks, rest, dims, preferred_element_type=F32)

        @pl.when(step >= 2)
        def _():
            for j in range(2):
                landed(dkv_in.at[0, 0], dkv_s.at[step - 2, j])

    def pair_back(step, pair):
        tt, slot = rat(step), lax.rem(step, 2)
        wide = pl.ds(pl.multiple_of(pair * 2 * HEAD_DIM, 2 * HEAD_DIM), 2 * HEAD_DIM)
        q_pair, o_pair = q_v[tt, :, wide], mix_grad[:, wide]
        q_ones = [jnp.where(low_lanes, q_pair, 0).astype(BF), jnp.where(low_lanes, 0, q_pair).astype(BF)]
        o_ones = [jnp.where(low_lanes, o_pair, 0).astype(BF), jnp.where(low_lanes, 0, o_pair).astype(BF)]
        kt_v[...] = jnp.transpose(k_v[tt, :, wide])
        dqt_v[...] = jnp.zeros_like(dqt_v)
        dims = (((1,), (1,)), ((), ()))

        def block(b, carry):
            spot = pl.ds(pl.multiple_of(b * key_rows, key_rows), key_rows)
            k_part, v_part = k_v[tt, spot, wide], v_v[tt, spot, wide]
            number = b * key_rows + lax.broadcasted_iota(jnp.int32, (key_rows, 1), 0)
            live = number < length
            dv, dk = None, None
            for head in range(2):
                which = tt * (group // HEAD_DIM) + pair * 2 + head
                scores = lax.dot_general(k_part, q_ones[head], dims, preferred_element_type=F32)
                probs = jnp.where(live, jnp.exp(scores - lse_rows[pl.ds(which, 1)]), 0.0)
                prob_grad = lax.dot_general(v_part, o_ones[head], dims, preferred_element_type=F32)
                score_grad = (probs * (prob_grad - delta_v[pl.ds(pair * 2 + head, 1)])).astype(BF)
                one_v = jnp.dot(probs.astype(BF), o_ones[head], preferred_element_type=F32)
                one_k = jnp.dot(score_grad, q_ones[head], preferred_element_type=F32)
                dv = one_v if dv is None else dv + one_v
                dk = one_k if dk is None else dk + one_k
                rows_here = slice(head * HEAD_DIM, (head + 1) * HEAD_DIM)
                dqt_v[rows_here] += jnp.dot(
                    kt_v[rows_here, spot], score_grad, preferred_element_type=F32
                )
            dkv_v[slot, 0, spot, wide] = dk.astype(BF)
            dkv_v[slot, 1, spot, wide] = dv.astype(BF)
            return carry

        lax.fori_loop(0, 2 * tokens // key_rows, block, 0)
        dq = jnp.transpose(dqt_v[...].astype(BF).astype(F32)) * 0.125
        rms[2, tt, :, wide] = dq.astype(BF)
        total = jnp.sum(dq, axis=0, keepdims=True)
        small_v[0, pl.ds(tt * (group // 128) + pair, 1)] = total

    def exchange(step):
        slot = lax.rem(step, 2)
        for j in range(2):
            remote(
                dkv_v.at[slot, j, others],
                dkv_in.at[step, j],
                dkv_s.at[step, j],
                dkv_r.at[step, j],
                sibling,
            ).start()

    def collect(step):
        tt, slot = rat(step), lax.rem(step, 2)
        for j in range(2):
            landed(dkv_in.at[0, 0], dkv_r.at[step, j])
            value = (
                dkv_v[slot, j, mine].astype(F32) + dkv_in[step, j].astype(F32)
            ).astype(BF)
            rms[2, tt, :, (1 + j) * group : (2 + j) * group] = value
            if j:
                total = jnp.sum(value.astype(F32), axis=0, keepdims=True)
                for r in range(group // 128):
                    small_v[1, pl.ds(tt * (group // 128) + r, 1)] = total[:, r * 128 : (r + 1) * 128]

        def one(n, carry):
            wide = pl.ds(pl.multiple_of(n * 256, 256), 256)
            acc[:, wide] += lax.dot_general(
                rms[2, tt, :, : 3 * group],
                wbuf[slot, wide, : 3 * group],
                (((1,), (1,)), ((), ())),
                preferred_element_type=F32,
            )
            return carry

        lax.fori_loop(0, width // 256, one, 0)

    def attention(step, carry):
        @pl.when(step < n_tensor)
        def _():
            prepare(step)
            for pair in range(group // (2 * HEAD_DIM)):
                pair_back(step, pair)

                @pl.when(step < 2)
                def _(pair=pair):
                    advance(3 + 2 * step + pair)

            @pl.when(step == 2)
            def _():
                advance(7)

            exchange(step)

        @pl.when(step >= 1)
        def _():
            collect(step - 1)

            @pl.when(step < n_tensor - 1)
            def _():
                weights(0, step + 1, lax.rem(step + 1, 2)).start()

        return carry

    lax.fori_loop(0, n_tensor + 1, attention, 0)

    cot_v[...] = acc[...].astype(BF)
    send_output(1, cot_v)
    for j in range(SMALL):
        send_or_keep(
            me == j,
            small_v.at[j],
            small_in.at[me],
            b_s.at[j],
            b_r.at[me],
            (j // n_tensor, j % n_tensor),
        )
    def drain(index, carry):
        advance(index)
        return carry

    lax.fori_loop(2 * n_tensor, pieces + 1, drain, 0)

    @pl.when(me < SMALL)
    def _():
        def arrive(step, total):
            landed(small_in.at[0], b_r.at[step])
            return total + small_in[step]

        total = lax.fori_loop(0, count, arrive, jnp.zeros(small_in.shape[1:], F32))
        small_in[0] = total
        pltpu.make_async_copy(small_in.at[0], small_out.at[me], bo_r.at[me]).start()

        def spread(step, carry):
            other = lax.rem(me + step, count)
            remote(
                small_in.at[0],
                small_out.at[me],
                bo_s.at[step],
                bo_r.at[me],
                (lax.div(other, n_tensor), lax.rem(other, n_tensor)),
            ).start()
            return carry

        lax.fori_loop(1, count, spread, 0)

    for index in range(pieces + 1, pieces + 1 + bits):
        advance(jnp.int32(index))

    for k in range(KINDS):
        total = from_z[k, n_tensor - 1].astype(F32)
        for step in range(n_tensor - 1):
            landed(from_z.at[0, 0], z_r.at[(KINDS - 1 - k) * n_tensor + step])
            total = total + from_z[k, step].astype(F32)
        sum_ref[k] = total

    for k in range(KINDS):
        for tt in range(n_tensor):
            relayed(k, tt)
            for half in range(2):
                half_rows = full_ref.at[k, tt, pl.ds(0, width // 2), pl.ds(0, half_cols)]
                landed(half_rows, sib_s.at[k, tt, half])
                if chips > 1:
                    most = full_ref.at[k, tt, pl.ds(0, width // 2 - rows), pl.ds(0, half_cols)]
                    landed(most, gxy_s.at[k, tt, half])
    for s in range(2):
        sent((lax.div(t, half_t) == core) & (2 * core + s == t), x_ref.at[s], x_s.at[s])
    for step in range(1, n_tensor):
        landed(bias_ref, bz_s.at[step])
    for tt in range(n_tensor):
        for j in range(2):
            landed(q_v.at[tt], kv_s.at[tt, j])
    for step in range(1, n_dp):
        landed(c_one.at[0], c1_s.at[step])
    for step in range(2 * n_dp):
        seq = lax.rem(4 * chip + step, 2 * n_dp)
        goal = 2 * lax.div(seq, 4) + lax.div(t, half_t)
        sent((goal == d) & (lax.rem(seq, 4) == t), c_two.at[0], c2_s.at[step])
    for j in range(SMALL):
        landed(small_v.at[0], bo_r.at[j])
        sent(me == j, small_v.at[0], b_s.at[j])

    @pl.when(me < SMALL)
    def _():
        def gone(step, carry):
            landed(small_v.at[0], bo_s.at[step])
            return carry

        lax.fori_loop(1, count, gone, 0)

    for a in range(2):
        for q in range(2):
            sent((lax.div(t, half_t) == core) & (2 * core + q == t), x_ref.at[q], y_s.at[a, q])
            landed(x_ref.at[q], y_r.at[a, q])
    for step in range(n_tensor - 2, n_tensor):
        for j in range(2):
            landed(dkv_in.at[0, 0], dkv_s.at[step, j])
    for index in range(pieces - 2, pieces):
        landed(outbox.at[0], core_s.at[index])
    for index in range(pieces - SLOTS, pieces):
        for half in range(2):
            landed(from_chip.at[0, 0], xy_s.at[index, half])
        if index % n_tensor < n_tensor - 1:
            landed(from_z.at[0, 0], z_s.at[index])


def gauss(u):
    size = jnp.abs(u)
    bell = 0.3989422804014327 * jnp.exp(-0.5 * (u * u))
    s = 1.0 / (1.0 + 0.23164190 * size)
    tail = bell * s * (
        0.319381530 + s * (-0.356563782 + s * (1.781477937 + s * (-1.821255978 + s * 1.330274429)))
    )
    return bell, jnp.where(u < 0, tail, 1.0 - tail)


def run_layer(n_dp, n_tensor, undealing, lengths, vecs, x_in, cot_in, shard, biases):
    slots, span, width = x_in.shape
    rows, cols = shard.shape[1:]
    chips = n_dp // 2
    tokens = 2 * span
    group = cols // 4
    n_pos = min(n_dp, span // 16)
    prow, pcol = span // n_pos, width // (n_dp // n_pos)
    pieces = KINDS * n_tensor
    count = n_dp * n_tensor
    dma = pltpu.SemaphoreType.DMA
    any_space = pl.BlockSpec(memory_space=pl.ANY)
    smem = pl.BlockSpec(memory_space=pltpu.SMEM)
    vmem = pl.BlockSpec(memory_space=pltpu.VMEM)
    shapes = (
        ((KINDS, n_tensor, width, cols), BF),
        ((KINDS, rows, cols), F32),
        ((SMALL, 8, 128), F32),
        ((2, 2, span, width), BF),
    )
    return pl.pallas_call(
        functools.partial(layer_kernel, n_dp, n_tensor),
        out_shape=tuple(jax.ShapeDtypeStruct(*shape) for shape in shapes),
        in_specs=[smem, smem, vmem, any_space, any_space, any_space, any_space],
        out_specs=(any_space, vmem, any_space, any_space),
        scratch_shapes=[
            pltpu.VMEM((n_dp, slots, prow, pcol), BF),
            pltpu.VMEM((2 * n_dp, prow, pcol), BF),
            pltpu.VMEM((n_tensor,) + biases.shape, F32),
            pltpu.VMEM((2, width, cols), BF),
            pltpu.VMEM((n_tensor, tokens, group), BF),
            pltpu.VMEM((n_tensor, 2 * tokens, group), BF),
            pltpu.VMEM((n_tensor, 2 * tokens, group), BF),
            pltpu.VMEM((4, 2, width // 2, tokens), BF),
            pltpu.VMEM((KINDS, n_tensor, tokens, cols), BF),
            pltpu.VMEM((tokens, width), BF),
            pltpu.VMEM((tokens, width), BF),
            pltpu.VMEM((tokens, width), BF),
            pltpu.VMEM((tokens, width), BF),
            pltpu.VMEM((tokens, width), F32),
            pltpu.VMEM((tokens, 128), F32),
            pltpu.VMEM((128, tokens), F32),
            pltpu.VMEM((2, tokens, 128), F32),
            pltpu.VMEM((tokens, group), BF),
            pltpu.VMEM((8, tokens), F32),
            pltpu.VMEM((2 * HEAD_DIM, tokens), F32),
            pltpu.VMEM((2 * HEAD_DIM, 2 * tokens), BF),
            pltpu.VMEM((2, 2, 2 * tokens, group), BF),
            pltpu.VMEM((n_tensor, 2, tokens, group), BF),
            pltpu.VMEM((2, width // 2, cols), BF),
            pltpu.VMEM((SLOTS, width // 2, cols), BF),
            pltpu.VMEM((SLOTS, width // 2, cols), BF),
            pltpu.VMEM((SLOTS, 2, max(chips - 1, 1), rows, cols // 2), BF),
            pltpu.VMEM((KINDS, n_tensor, rows, cols), BF),
            pltpu.VMEM((SMALL, 8, 128), F32),
            pltpu.VMEM((count, 8, 128), F32),
            dma((2,)),
            dma((2,)),
            dma((n_dp,)),
            dma((n_dp,)),
            dma((2 * n_dp,)),
            dma((n_tensor // 2, n_dp)),
            dma((KINDS,)),
            dma((KINDS, n_tensor, 2)),
            dma((KINDS, n_tensor)),
            dma((KINDS, n_tensor, 2)),
            dma((KINDS, n_tensor, 2, chips)),
            dma((KINDS, n_tensor, 2)),
            dma((KINDS, n_tensor, 2, chips)),
            dma((n_tensor, 2)),
            dma((n_tensor, 2)),
            dma((n_tensor,)),
            dma((n_tensor,)),
            dma((2,)),
            dma((n_tensor, 2)),
            dma((n_tensor, 2)),
            dma((2, 2)),
            dma((2, 2)),
            dma((SMALL,)),
            dma((count,)),
            dma((count,)),
            dma((SMALL,)),
            dma((pieces,)),
            dma((pieces,)),
            dma((pieces, 2)),
            dma((pieces, 2, chips)),
            dma((pieces,)),
            dma((pieces,)),
        ],
        compiler_params=pltpu.CompilerParams(
            collective_id=0, has_side_effects=True, vmem_limit_bytes=VMEM_LIMIT
        ),
        name="encoder_layer",
    )(undealing, lengths, vecs, x_in, cot_in, shard, biases)


def shards(
    n_dp,
    n_tensor,
    inputs,
    cotangent,
    lengths,
    dealing,
    undealing,
    query_weight,
    key_weight,
    value_weight,
    output_weight,
    up_weight,
    down_weight,
    query_bias,
    value_bias,
    output_bias,
    up_bias,
    down_bias,
    first_gain,
    first_shift,
    second_gain,
    second_shift,
):
    span, slots, width = inputs.shape
    group = query_weight.shape[1]
    shard = jnp.stack(
        [
            jnp.concatenate([query_weight, key_weight, value_weight, output_weight.T], axis=1),
            up_weight,
            down_weight.T,
        ]
    ).astype(BF)
    blank = jnp.zeros((group,), F32)
    biases = jnp.concatenate([query_bias, value_bias, up_bias, blank, blank]).reshape(8, group)
    vecs = jnp.stack([output_bias, down_bias, first_gain, first_shift, second_gain, second_shift])
    vecs = jnp.pad(vecs, ((0, 2), (0, 0)))
    _, sums, small, returned = run_layer(
        n_dp,
        n_tensor,
        undealing,
        lengths,
        vecs,
        jnp.transpose(inputs, (1, 0, 2)),
        jnp.transpose(cotangent, (1, 0, 2)),
        shard,
        biases,
    )
    returned = jnp.transpose(returned, (0, 2, 1, 3))
    small = small.reshape(SMALL, width)
    t = lax.axis_index("tensor")

    def mine(row):
        return lax.dynamic_slice(small[row], (t * group,), (group,))

    return (
        returned[0],
        returned[1],
        sums[0][:, :group],
        sums[0][:, group : 2 * group],
        sums[0][:, 2 * group : 3 * group],
        sums[0][:, 3 * group :].T,
        sums[1],
        sums[2].T,
        mine(0),
        mine(1),
        small[2],
        lax.dynamic_index_in_dim(small, 3 + t, 0, keepdims=False),
        small[7],
        small[8],
        small[9],
        small[10],
        small[11],
    )


def solution(mesh):
    tokens = P("tensor", "dp", None)
    rows, columns = P("dp", "tensor"), P("tensor", "dp")
    split, copied = P("tensor"), P()
    return jax.shard_map(
        functools.partial(shards, mesh.shape["dp"], mesh.shape["tensor"]),
        mesh=mesh,
        in_specs=(
            (tokens, tokens, copied, copied, copied)
            + (rows, rows, rows, columns, rows, columns)
            + (split, split, copied, split, copied, copied, copied, copied, copied)
        ),
        out_specs=(
            (tokens, tokens, rows, rows, rows, columns, rows, columns)
            + (split, split, copied, split, copied, copied, copied, copied, copied)
        ),
        check_vma=False,
    )
```

time: 431 us -> 380 us (0.88)
  Pallas kernels: 407 us -> 357 us
    pallas_call x2 -> x1, Pallas kernels: 407 us -> 357 us  [run_layer(): pl.pallas_call(functools.partial(layer_kernel, n_dp, n_tensor), out_shape...]
where the time goes in v4:
time: 380 us; the launch traced here: 377 us
  Pallas kernels  357 us (94%)
  local copies, waits for them, and re-layouts  18.1 us (5%)
    pallas_call x1, Pallas kernels, run_layer(): pl.pallas_call(functools.partial(layer_kernel, n_dp, n_tensor), out_shape...  357 us

profile of v4, /device:TPU:0, one launch (start us, length us, event | category | flops | bytes accessed | tf_op | source)
XLA Modules:
  0.0 377.5 jit_solution(17962630422950052050)
XLA Ops:
  0.7 0.8 stack.43
  1.5 0.6 pad.4.vec_ref
  2.1 0.0 copy-start.1
  2.1 0.0 copy-start.2
  2.1 0.0 copy-start.4
  2.1 0.0 copy-start.5
  2.1 0.0 copy-start.6
  2.1 3.6 copy_bitcast_fusion
  5.7 0.0 copy-start.7
  5.7 0.0 copy-done.1
  5.7 0.0 copy-start.8
  5.7 0.0 copy-start.9
  5.7 0.0 copy-start.10
  5.8 0.1 copy.39
  5.9 0.0 copy-done.2
  5.9 0.0 copy-done.4
  6.0 0.1 copy.38
  6.1 0.0 copy-done.5
  6.1 0.0 copy-done.6
  6.1 0.5 copy-done.7
  6.7 1.0 pad_maximum_fusion.shard_ref
  7.7 0.0 copy-done.8
  7.7 0.0 copy-done.9
  7.7 0.0 copy-done.10
  7.7 0.6 reshape.56.bias_ref
  8.3 357.4 %encoder_layer.1 = (bf16[3,4,1024,1024]{3,2,1,0:T(8,128)(2,1)}, f32[3,128,1024]{2,1,0:T(8,128)}, f32[12,8,128]{2,1,0:T(8,128)}, bf16[2,2,256,1024]{3,2,1,0:T(8,128)(2,1)}) custom-call(s32[16]{0:T(128)} %undealing.1, s32[16]{0:T(128)} %lengths.1, f32[8,1024]{1,0:T(8,128)} %pad.4.vec_ref, bf16[2,256,1024]{2,1,0:T(8,128)(2,1)} %get-tuple-element.58.x_ref, ...), custom_call_target="tpu_custom_call" | custom-call | tf_op jit(solution)/shard_map/encoder_layer/pallas_call | solution.py:1058
  365.7 1.7 slice_bitcast_fusion
  367.5 0.0 copy-start
  367.5 2.0 copy.40
  369.5 2.0 copy.41
  371.6 0.0 copy-done
  371.6 0.0 copy-start.3
  371.6 0.9 slice_bitcast_fusion.2
  372.5 0.8 slice_bitcast_fusion.5
  373.2 0.8 copy.42
  374.0 1.0 copy.43
  375.0 0.0 copy-done.3
  375.0 0.6 slice_bitcast_fusion.6
  375.6 0.6 dynamic_slice.10
  376.2 0.6 dynamic_slice.11
  376.9 0.6 constant_dynamic-slice_fusion
  (9 shorter events, 0.1 us)
Async XLA Ops:
  2.1 3.6 copy-start.1
  2.1 3.8 %copy-start.2 = (f32[128,1024]{1,0:T(8,128)S(1)}, f32[128,1024]{1,0:T(8,128)}, u32[]{:S(2)}) copy-start(f32[128,1024]{1,0:T(8,128)} %param.28) | copy-start | bytes 1572868
  2.1 3.9 %copy-start.4 = (f32[256,128]{1,0:T(8,128)S(1)}, f32[256,128]{1,0:T(8,128)}, u32[]{:S(2)}) copy-start(f32[256,128]{1,0:T(8,128)} %param.27) | copy-start | bytes 393220
  2.1 4.0 %copy-start.5 = (f32[128,256]{1,0:T(8,128)S(1)}, f32[128,256]{1,0:T(8,128)}, u32[]{:S(2)}) copy-start(f32[128,256]{1,0:T(8,128)} %param.26) | copy-start | bytes 393220
  2.1 4.0 %copy-start.6 = (f32[128,256]{1,0:T(8,128)S(1)}, f32[128,256]{1,0:T(8,128)}, u32[]{:S(2)}) copy-start(f32[128,256]{1,0:T(8,128)} %param.25) | copy-start | bytes 393220
  5.7 0.9 copy-start.7
  5.7 1.9 copy-start.8
  5.7 1.9 copy-start.9
  5.7 1.9 copy-start.10
  367.5 4.1 %copy-start = (f32[3,128,1024]{2,1,0:T(8,128)S(1)}, f32[3,128,1024]{2,1,0:T(8,128)}, u32[]{:S(2)}) copy-start(f32[3,128,1024]{2,1,0:T(8,128)} %get-tuple-element.21) | copy-start | bytes 4718596
  371.6 3.4 copy-start.3

commit v5 on v4

--- a/solution.py
+++ b/solution.py
@@ -90,7 +90,10 @@
 LAG = 2
 SMALL = 12
 SLOTS = 4
-COT_ONE, COT_TWO = 3, 8
+DEEP = 0
+PLAN = (((3, 3), (4, 4), (5, 6), (7, 8)), ((3, 4), (4, 5), (6, 7), (8, 9)))
+LAST = 9
+COT_ONE, COT_TWO, X_START = 4, 9, 1
 
 
 def layer_kernel(
@@ -169,6 +172,7 @@
     xy_r,
     z_s,
     z_r,
+    out_sem,
 ):
     d, t, chip, core = place()
     chips = n_dp // 2
@@ -256,6 +260,8 @@
                 x_r.at[lax.rem(t, half_t)],
                 (2 * chip + lax.div(t, half_t), 2 * core + s),
             )
+
+    def start_biases():
         pltpu.make_async_copy(bias_ref, bias_v.at[t], bz_r.at[0]).start()
         for step in range(1, n_tensor):
             remote(
@@ -329,6 +335,20 @@
     early, late = range(1, max(chips // 2, 1)), range(max(chips // 2, 1), chips)
 
     def comm_step(index):
+        @pl.when((index + 2 >= KINDS) & (index + 2 < pieces))
+        def _():
+            k, tt = at(arriving(index + 2))
+            for half in range(2):
+                forward(k, tt, half, 0)
+
+        @pl.when(index < pieces)
+        def _():
+            receive(index, early)
+
+        @pl.when(index >= LAG)
+        def _():
+            receive(index - LAG, late)
+
         follow = index + KINDS
         others = n_tensor - 1
 
@@ -339,20 +359,6 @@
             @pl.when((lax.rem(index, others) == others - 1) & (follow + 1 < pieces))
             def _():
                 relay(lax.div(index, others) * n_tensor + n_tensor)
-
-        @pl.when((index + 2 >= KINDS) & (index + 2 < pieces))
-        def _():
-            k, tt = at(arriving(index + 2))
-            for half in range(2):
-                forward(k, tt, half, 0)
-
-        @pl.when(index < pieces)
-        def _():
-            receive(index, early)
-
-        @pl.when(index >= LAG)
-        def _():
-            receive(index - LAG, late)
 
     def load(index):
         k, tt = at(index)
@@ -485,37 +491,45 @@
             )
             return carry
 
-        lax.fori_loop(0, width // 256, one, 0)
+        lax.fori_loop(0, width // 256, one, 0, unroll=True)
 
     landed(shard_ref.at[0], own_sem.at[0])
     relay(jnp.int32(0))
-    start_tokens()
+    start_biases()
     for k in range(KINDS):
         if k:
             landed(shard_ref.at[0], own_sem.at[k])
         for half in range(2):
             forward(k, t, half, 0)
-    for s in range(2):
-        landed(x_ref.at[s], x_r.at[s])
-    for step in range(n_tensor):
-        landed(bias_ref, bz_r.at[step])
-    acc[...] = outbox[0].astype(F32) + vec_ref[0:1]
-    turn_rows(outbox[0], 2)
-    lse_v[...] = jnp.zeros_like(lse_v)
+    def tokens_here():
+        for s in range(2):
+            landed(x_ref.at[s], x_r.at[s])
+        for step in range(n_tensor):
+            landed(bias_ref, bz_r.at[step])
+        acc[...] = outbox[0].astype(F32) + vec_ref[0:1]
+        turn_rows(outbox[0], 2)
+        lse_v[...] = jnp.zeros_like(lse_v)
 
     def turn(index, carry):
         comm_step(index)
         done = index - LAG
 
-        @pl.when((done == 1) | ((done >= 4) & (done <= 6)))
-        def _():
-            attend(jnp.where(done == 1, 0, done - 3))
-
-        @pl.when((done == 0) | ((done >= 3) & (done <= 5)))
-        def _():
-            group_index = jnp.where(done == 0, 0, done - 2)
-            load(group_index)
-            project(group_index)
+        @pl.when(index == X_START)
+        def _():
+            start_tokens()
+
+        @pl.when(done == 2)
+        def _():
+            tokens_here()
+
+        @pl.when((done >= 3) & (done <= 6))
+        def _():
+            attend(done - 3)
+
+        @pl.when((done >= 2) & (done <= 5))
+        def _():
+            load(done - 2)
+            project(done - 2)
 
         @pl.when(index == COT_ONE)
         def _():
@@ -606,9 +620,9 @@
             ).astype(BF)
             return carry
 
-        lax.fori_loop(0, cols // group, one, 0)
+        lax.fori_loop(0, cols // group, one, 0, unroll=True)
         remote(
-            outbox.at[box], from_core.at[slot], core_s.at[index], core_r.at[index], sibling
+            outbox.at[box], from_core.at[lax.rem(index, 4)], core_s.at[index], core_r.at[index], sibling
         ).start()
 
     def spot_of(code, order):
@@ -648,7 +662,7 @@
         def add(c, carry):
             spot = pl.ds(pl.multiple_of(c * part, part), part)
             held[slot, spot] = (
-                held[slot, spot].astype(F32) + from_core[slot, spot].astype(F32)
+                held[slot, spot].astype(F32) + from_core[lax.rem(index, 4), spot].astype(F32)
             ).astype(BF)
             return carry
 
@@ -680,7 +694,7 @@
             emit(index)
 
         for stage in range(bits + 1):
-            earlier = index - 1 - stage
+            earlier = index - 1 - stage - (DEEP if stage else 0)
 
             @pl.when((earlier >= 0) & (earlier < pieces))
             def _(stage=stage, earlier=earlier):
@@ -748,7 +762,7 @@
             rms[1, tt, :, wide] = (rms[1, tt, :, wide].astype(F32) * grad).astype(BF)
             return carry
 
-        lax.fori_loop(0, cols // 256, one, 0)
+        lax.fori_loop(0, cols // 256, one, 0, unroll=True)
 
         @pl.when(step < n_tensor - 1)
         def _():
@@ -770,7 +784,7 @@
             )
             return carry
 
-        lax.fori_loop(0, width // 256, two, 0)
+        lax.fori_loop(0, width // 256, two, 0, unroll=True)
 
         @pl.when(step < n_tensor - 1)
         def _():
@@ -894,7 +908,11 @@
             )
             return carry
 
-        lax.fori_loop(0, width // 256, one, 0)
+        lax.fori_loop(0, width // 256, one, 0, unroll=True)
+
+    def run(index, carry):
+        advance(index)
+        return carry
 
     def attention(step, carry):
         @pl.when(step < n_tensor)
@@ -902,14 +920,10 @@
             prepare(step)
             for pair in range(group // (2 * HEAD_DIM)):
                 pair_back(step, pair)
-
-                @pl.when(step < 2)
-                def _(pair=pair):
-                    advance(3 + 2 * step + pair)
-
-            @pl.when(step == 2)
-            def _():
-                advance(7)
+                low, high = jnp.int32(0), jnp.int32(0)
+                for s, (begin, end) in enumerate(PLAN[pair]):
+                    low, high = jnp.where(step == s, begin, low), jnp.where(step == s, end, high)
+                lax.fori_loop(low, high, run, 0)
 
             exchange(step)
 
@@ -940,7 +954,7 @@
         advance(index)
         return carry
 
-    lax.fori_loop(2 * n_tensor, pieces + 1, drain, 0)
+    lax.fori_loop(LAST, pieces, drain, 0)
 
     @pl.when(me < SMALL)
     def _():
@@ -965,15 +979,17 @@
 
         lax.fori_loop(1, count, spread, 0)
 
-    for index in range(pieces + 1, pieces + 1 + bits):
-        advance(jnp.int32(index))
+    lax.fori_loop(pieces, pieces + 1 + bits + DEEP, drain, 0)
 
     for k in range(KINDS):
         total = from_z[k, n_tensor - 1].astype(F32)
         for step in range(n_tensor - 1):
             landed(from_z.at[0, 0], z_r.at[(KINDS - 1 - k) * n_tensor + step])
             total = total + from_z[k, step].astype(F32)
-        sum_ref[k] = total
+        acc[k * rows : (k + 1) * rows] = total
+        pltpu.make_async_copy(acc.at[pl.ds(k * rows, rows)], sum_ref.at[k], out_sem.at[k]).start()
+    for k in range(KINDS):
+        landed(acc.at[pl.ds(0, rows)], out_sem.at[k])
 
     for k in range(KINDS):
         for tt in range(n_tensor):
@@ -1058,8 +1074,8 @@
     return pl.pallas_call(
         functools.partial(layer_kernel, n_dp, n_tensor),
         out_shape=tuple(jax.ShapeDtypeStruct(*shape) for shape in shapes),
-        in_specs=[smem, smem, vmem, any_space, any_space, any_space, any_space],
-        out_specs=(any_space, vmem, any_space, any_space),
+        in_specs=[smem, smem, vmem, any_space, any_space, vmem, vmem],
+        out_specs=(any_space, any_space, any_space, any_space),
         scratch_shapes=[
             pltpu.VMEM((n_dp, slots, prow, pcol), BF),
             pltpu.VMEM((2 * n_dp, prow, pcol), BF),
@@ -1085,7 +1101,7 @@
             pltpu.VMEM((2, 2, 2 * tokens, group), BF),
             pltpu.VMEM((n_tensor, 2, tokens, group), BF),
             pltpu.VMEM((2, width // 2, cols), BF),
-            pltpu.VMEM((SLOTS, width // 2, cols), BF),
+            pltpu.VMEM((4, width // 2, cols), BF),
             pltpu.VMEM((SLOTS, width // 2, cols), BF),
             pltpu.VMEM((SLOTS, 2, max(chips - 1, 1), rows, cols // 2), BF),
             pltpu.VMEM((KINDS, n_tensor, rows, cols), BF),
@@ -1123,6 +1139,7 @@
             dma((pieces, 2, chips)),
             dma((pieces,)),
             dma((pieces,)),
+            dma((KINDS,)),
         ],
         compiler_params=pltpu.CompilerParams(
             collective_id=0, has_side_effects=True, vmem_limit_bytes=VMEM_LIMIT

time: 380 us -> 329 us (0.87)
  Pallas kernels: 357 us -> 303 us
    pallas_call x1, Pallas kernels: 357 us -> 303 us  [run_layer(): pl.pallas_call(functools.partial(layer_kernel, n_dp, n_tensor), out_shape...]
where the time goes in v5:
time: 329 us; the launch traced here: 323 us
  Pallas kernels  303 us (92%)
  local copies, waits for them, and re-layouts  18.1 us (6%)
    pallas_call x1, Pallas kernels, run_layer(): pl.pallas_call(functools.partial(layer_kernel, n_dp, n_tensor), out_shape...  303 us
    unnamed x30, local copies, waits for them, and re-layouts  6.66 us

profile of v5, /device:TPU:0, one launch (start us, length us, event | category | flops | bytes accessed | tf_op | source)
XLA Modules:
  0.0 322.7 jit_solution(12895271142532929314)
XLA Ops:
  0.7 0.8 stack.43
  1.5 0.6 pad.4.vec_ref
  2.1 0.0 copy-start.1
  2.1 0.0 copy-start.2
  2.1 0.0 copy-start.4
  2.1 0.0 copy-start.5
  2.1 0.0 copy-start.6
  2.1 3.6 %copy_bitcast_fusion = (bf16[2,256,1024]{2,1,0:T(8,128)(2,1)}, bf16[2,256,1024]{2,1,0:T(8,128)(2,1)}) fusion(bf16[256,2,1024]{2,1,0:T(2,128)(2,1)} %param.21, bf16[256,2,1024]{2,1,0:T(2,128)(2,1)} %param.20), kind=kLoop, calls=%fused_computation.2 | loop fusion | bytes 4194304 | tf_op jit(solution)/shard_map/transpose | solution.py:1195
  5.7 0.0 copy-start.7
  5.7 0.0 copy-done.1
  5.7 0.0 copy-start.8
  5.7 0.0 copy-start.9
  5.7 0.0 copy-start.10
  5.8 0.1 copy.39
  5.9 0.0 copy-done.2
  5.9 0.0 copy-done.4
  6.0 0.1 copy.38
  6.1 0.0 copy-done.5
  6.1 0.0 copy-done.6
  6.1 0.5 copy-done.7
  6.7 1.0 pad_maximum_fusion.shard_ref
  7.7 0.0 copy-done.8
  7.7 0.0 copy-done.9
  7.7 0.0 copy-done.10
  7.7 0.6 reshape.56.bias_ref
  8.3 302.7 %encoder_layer.1 = (bf16[3,4,1024,1024]{3,2,1,0:T(8,128)(2,1)}, f32[3,128,1024]{2,1,0:T(8,128)}, f32[12,8,128]{2,1,0:T(8,128)}, bf16[2,2,256,1024]{3,2,1,0:T(8,128)(2,1)}) custom-call(s32[16]{0:T(128)} %undealing.1, s32[16]{0:T(128)} %lengths.1, f32[8,1024]{1,0:T(8,128)} %pad.4.vec_ref, bf16[2,256,1024]{2,1,0:T(8,128)(2,1)} %get-tuple-element.58.x_ref, ...), custom_call_target="tpu_custom_call" | custom-call | tf_op jit(solution)/shard_map/encoder_layer/pallas_call | solution.py:1074
  311.0 1.7 slice_bitcast_fusion
  312.7 0.0 copy-start
  312.7 2.0 copy.40
  314.8 2.0 copy.41
  316.8 0.0 copy-done
  316.8 0.0 copy-start.3
  316.8 0.9 slice_bitcast_fusion.2
  317.7 0.8 slice_bitcast_fusion.5
  318.5 0.8 copy.42
  319.2 1.0 copy.43
  320.2 0.0 copy-done.3
  320.2 0.6 slice_bitcast_fusion.6
  320.8 0.6 dynamic_slice.10
  321.5 0.6 dynamic_slice.11
  322.1 0.6 constant_dynamic-slice_fusion
  (9 shorter events, 0.1 us)
Async XLA Ops:
  2.1 3.6 %copy-start.1 = (f32[1024,128]{1,0:T(8,128)S(1)}, f32[1024,128]{1,0:T(8,128)}, u32[]{:S(2)}) copy-start(f32[1024,128]{1,0:T(8,128)} %param.29) | copy-start | bytes 1572868
  2.1 3.8 %copy-start.2 = (f32[128,1024]{1,0:T(8,128)S(1)}, f32[128,1024]{1,0:T(8,128)}, u32[]{:S(2)}) copy-start(f32[128,1024]{1,0:T(8,128)} %param.28) | copy-start | bytes 1572868
  2.1 3.9 %copy-start.4 = (f32[256,128]{1,0:T(8,128)S(1)}, f32[256,128]{1,0:T(8,128)}, u32[]{:S(2)}) copy-start(f32[256,128]{1,0:T(8,128)} %param.27) | copy-start | bytes 393220
  2.1 4.0 %copy-start.5 = (f32[128,256]{1,0:T(8,128)S(1)}, f32[128,256]{1,0:T(8,128)}, u32[]{:S(2)}) copy-start(f32[128,256]{1,0:T(8,128)} %param.26) | copy-start | bytes 393220
  2.1 4.0 %copy-start.6 = (f32[128,256]{1,0:T(8,128)S(1)}, f32[128,256]{1,0:T(8,128)}, u32[]{:S(2)}) copy-start(f32[128,256]{1,0:T(8,128)} %param.25) | copy-start | bytes 393220
  5.7 0.9 copy-start.7
  5.7 1.9 copy-start.8
  5.7 1.9 copy-start.9
  5.7 1.9 copy-start.10
  312.7 4.1 %copy-start = (f32[3,128,1024]{2,1,0:T(8,128)S(1)}, f32[3,128,1024]{2,1,0:T(8,128)}, u32[]{:S(2)}) copy-start(f32[3,128,1024]{2,1,0:T(8,128)} %get-tuple-element.21) | copy-start | bytes 4718596
  316.8 3.4 %copy-start.3 = (f32[12,8,128]{2,1,0:T(8,128)S(1)}, f32[12,8,128]{2,1,0:T(8,128)}, u32[]{:S(2)}) copy-start(f32[12,8,128]{2,1,0:T(8,128)} %get-tuple-element.22) | copy-start | bytes 147460

commit v6 on v5

--- a/solution.py
+++ b/solution.py
@@ -89,7 +89,7 @@
 
 LAG = 2
 SMALL = 12
-SLOTS = 4
+SLOTS = 6
 DEEP = 0
 PLAN = (((3, 3), (4, 4), (5, 6), (7, 8)), ((3, 4), (4, 5), (6, 7), (8, 9)))
 LAST = 9
@@ -570,7 +570,8 @@
     norm(1, keep_two)
 
     def rat(step):
-        return lax.rem(t + 1 + step, n_tensor)
+        near = jnp.where(step < 2, flip(t, 0), t)
+        return jnp.where((step == 1) | (step == 2), flip(near, 1), near)
 
     def weights(k, step, slot):
         return pltpu.make_async_copy(full_ref.at[k, rat(step)], wbuf.at[slot], w_sem.at[slot])
@@ -674,18 +675,28 @@
         slot, step = lax.rem(index, SLOTS), lax.rem(index, n_tensor)
         source = pl.ds(pl.multiple_of(chip * rows, rows), rows)
 
+        k = kind_of(index)
+
+        @pl.when(step >= 2)
+        def _():
+            given = 3 - step
+            landed(from_z.at[0, 0], z_r.at[index - step + given])
+            held[slot, source] = (
+                held[slot, source].astype(F32) + from_z[k, given].astype(F32)
+            ).astype(BF)
+
         @pl.when(step == n_tensor - 1)
         def _():
-            from_z[kind_of(index), step] = held[slot, source]
+            from_z[k, step] = held[slot, source]
 
         @pl.when(step < n_tensor - 1)
         def _():
             remote(
                 held.at[slot, source],
-                from_z.at[kind_of(index), step],
+                from_z.at[k, step],
                 z_s.at[index],
                 z_r.at[index],
-                (d, rat(step)),
+                (d, jnp.where(step < 2, flip(t, 0), flip(t, 1))),
             ).start()
 
     def advance(index):
@@ -983,9 +994,8 @@
 
     for k in range(KINDS):
         total = from_z[k, n_tensor - 1].astype(F32)
-        for step in range(n_tensor - 1):
-            landed(from_z.at[0, 0], z_r.at[(KINDS - 1 - k) * n_tensor + step])
-            total = total + from_z[k, step].astype(F32)
+        landed(from_z.at[0, 0], z_r.at[(KINDS - 1 - k) * n_tensor + 2])
+        total = total + from_z[k, 2].astype(F32)
         acc[k * rows : (k + 1) * rows] = total
         pltpu.make_async_copy(acc.at[pl.ds(k * rows, rows)], sum_ref.at[k], out_sem.at[k]).start()
     for k in range(KINDS):

time: 329 us -> 317 us (0.964); the launches traced: 323 us -> 316 us
  Pallas kernels: 303 us -> 296 us
    pallas_call x1, Pallas kernels: 303 us -> 296 us  [run_layer(): pl.pallas_call(functools.partial(layer_kernel, n_dp, n_tensor), out_shape...]
where the time goes in v6:
time: 317 us; the launch traced here: 316 us
  Pallas kernels  296 us (93%)
  local copies, waits for them, and re-layouts  18.1 us (6%)
    pallas_call x1, Pallas kernels, run_layer(): pl.pallas_call(functools.partial(layer_kernel, n_dp, n_tensor), out_shape...  296 us
    unnamed x30, local copies, waits for them, and re-layouts  6.66 us

profile of v6, /device:TPU:0, one launch (start us, length us, event | category | flops | bytes accessed | tf_op | source)
XLA Modules:
  0.0 315.9 jit_solution(16808259071277171338)
XLA Ops:
  0.7 0.8 stack.43
  1.5 0.6 pad.4.vec_ref
  2.1 0.0 copy-start.1
  2.1 0.0 copy-start.2
  2.1 0.0 copy-start.4
  2.1 0.0 copy-start.5
  2.1 0.0 copy-start.6
  2.1 3.6 %copy_bitcast_fusion = (bf16[2,256,1024]{2,1,0:T(8,128)(2,1)}, bf16[2,256,1024]{2,1,0:T(8,128)(2,1)}) fusion(bf16[256,2,1024]{2,1,0:T(2,128)(2,1)} %param.21, bf16[256,2,1024]{2,1,0:T(2,128)(2,1)} %param.20), kind=kLoop, calls=%fused_computation.2 | loop fusion | bytes 4194304 | tf_op jit(solution)/shard_map/transpose | solution.py:1205
  5.7 0.0 copy-start.7
  5.7 0.0 copy-done.1
  5.7 0.0 copy-start.8
  5.7 0.0 copy-start.9
  5.7 0.0 copy-start.10
  5.8 0.1 copy.39
  5.9 0.0 copy-done.2
  5.9 0.0 copy-done.4
  6.0 0.1 copy.38
  6.1 0.0 copy-done.5
  6.1 0.0 copy-done.6
  6.1 0.5 copy-done.7
  6.7 1.0 pad_maximum_fusion.shard_ref
  7.7 0.0 copy-done.8
  7.7 0.0 copy-done.9
  7.7 0.0 copy-done.10
  7.7 0.6 reshape.56.bias_ref
  8.3 295.8 %encoder_layer.1 = (bf16[3,4,1024,1024]{3,2,1,0:T(8,128)(2,1)}, f32[3,128,1024]{2,1,0:T(8,128)}, f32[12,8,128]{2,1,0:T(8,128)}, bf16[2,2,256,1024]{3,2,1,0:T(8,128)(2,1)}) custom-call(s32[16]{0:T(128)} %undealing.1, s32[16]{0:T(128)} %lengths.1, f32[8,1024]{1,0:T(8,128)} %pad.4.vec_ref, bf16[2,256,1024]{2,1,0:T(8,128)(2,1)} %get-tuple-element.58.x_ref, ...), custom_call_target="tpu_custom_call" | custom-call | tf_op jit(solution)/shard_map/encoder_layer/pallas_call | solution.py:1084
  304.2 1.7 slice_bitcast_fusion
  305.9 0.0 copy-start
  305.9 2.0 copy.40
  307.9 2.0 copy.41
  310.0 0.0 copy-done
  310.0 0.0 copy-start.3
  310.0 0.9 slice_bitcast_fusion.2
  310.9 0.8 slice_bitcast_fusion.5
  311.6 0.8 copy.42
  312.4 1.0 copy.43
  313.4 0.0 copy-done.3
  313.4 0.6 slice_bitcast_fusion.6
  314.0 0.6 dynamic_slice.10
  314.6 0.6 dynamic_slice.11
  315.3 0.6 constant_dynamic-slice_fusion
  (9 shorter events, 0.1 us)
Async XLA Ops:
  2.1 3.6 %copy-start.1 = (f32[1024,128]{1,0:T(8,128)S(1)}, f32[1024,128]{1,0:T(8,128)}, u32[]{:S(2)}) copy-start(f32[1024,128]{1,0:T(8,128)} %param.29) | copy-start | bytes 1572868
  2.1 3.8 %copy-start.2 = (f32[128,1024]{1,0:T(8,128)S(1)}, f32[128,1024]{1,0:T(8,128)}, u32[]{:S(2)}) copy-start(f32[128,1024]{1,0:T(8,128)} %param.28) | copy-start | bytes 1572868
  2.1 3.9 %copy-start.4 = (f32[256,128]{1,0:T(8,128)S(1)}, f32[256,128]{1,0:T(8,128)}, u32[]{:S(2)}) copy-start(f32[256,128]{1,0:T(8,128)} %param.27) | copy-start | bytes 393220
  2.1 4.0 %copy-start.5 = (f32[128,256]{1,0:T(8,128)S(1)}, f32[128,256]{1,0:T(8,128)}, u32[]{:S(2)}) copy-start(f32[128,256]{1,0:T(8,128)} %param.26) | copy-start | bytes 393220
  2.1 4.0 %copy-start.6 = (f32[128,256]{1,0:T(8,128)S(1)}, f32[128,256]{1,0:T(8,128)}, u32[]{:S(2)}) copy-start(f32[128,256]{1,0:T(8,128)} %param.25) | copy-start | bytes 393220
  5.7 0.9 copy-start.7
  5.7 1.9 copy-start.8
  5.7 1.9 copy-start.9
  5.7 1.9 copy-start.10
  305.9 4.1 %copy-start = (f32[3,128,1024]{2,1,0:T(8,128)S(1)}, f32[3,128,1024]{2,1,0:T(8,128)}, u32[]{:S(2)}) copy-start(f32[3,128,1024]{2,1,0:T(8,128)} %get-tuple-element.21) | copy-start | bytes 4718596
  310.0 3.4 %copy-start.3 = (f32[12,8,128]{2,1,0:T(8,128)S(1)}, f32[12,8,128]{2,1,0:T(8,128)}, u32[]{:S(2)}) copy-start(f32[12,8,128]{2,1,0:T(8,128)} %get-tuple-element.22) | copy-start | bytes 147460

commit v7 on v6

--- a/solution.py
+++ b/solution.py
@@ -93,7 +93,7 @@
 DEEP = 0
 PLAN = (((3, 3), (4, 4), (5, 6), (7, 8)), ((3, 4), (4, 5), (6, 7), (8, 9)))
 LAST = 9
-COT_ONE, COT_TWO, X_START = 4, 9, 1
+COT_ONE, COT_TWO, X_START = 4, 9, 0
 
 
 def layer_kernel(
@@ -600,24 +600,12 @@
         def _():
             landed(outbox.at[0], core_s.at[index - 2])
 
-        @pl.when(index >= SLOTS)
-        def _():
-            for half in range(2):
-                landed(from_chip.at[0, 0], xy_s.at[index - SLOTS, half])
-
-            @pl.when(lax.rem(index - SLOTS, n_tensor) < n_tensor - 1)
-            def _():
-                landed(from_z.at[0, 0], z_s.at[index - SLOTS])
-
         def one(n, carry):
             wide = pl.ds(pl.multiple_of(n * group, group), group)
             left = order + jnp.where((order == 2) & (n == 3), 1, 0)
             right = rms[order, tt, :, wide]
             outbox[box, :, wide] = jnp.dot(
                 lts[left, 1 - core], right, preferred_element_type=F32
-            ).astype(BF)
-            held[slot, :, wide] = jnp.dot(
-                lts[left, core], right, preferred_element_type=F32
             ).astype(BF)
             return carry
 
@@ -657,17 +645,29 @@
 
     def first(index):
         slot = lax.rem(index, SLOTS)
+        @pl.when(index >= SLOTS)
+        def _():
+            for half in range(2):
+                landed(from_chip.at[0, 0], xy_s.at[index - SLOTS, half])
+
+            @pl.when(lax.rem(index - SLOTS, n_tensor) < n_tensor - 1)
+            def _():
+                landed(from_z.at[0, 0], z_s.at[index - SLOTS])
+
         landed(outbox.at[0], core_r.at[index])
-        part = min(128, half_width)
-
-        def add(c, carry):
-            spot = pl.ds(pl.multiple_of(c * part, part), part)
-            held[slot, spot] = (
-                held[slot, spot].astype(F32) + from_core[lax.rem(index, 4), spot].astype(F32)
+        order = lax.div(index, n_tensor)
+        tt = rat(lax.rem(index, n_tensor))
+
+        def one(n, carry):
+            wide = pl.ds(pl.multiple_of(n * group, group), group)
+            left = order + jnp.where((order == 2) & (n == 3), 1, 0)
+            held[slot, :, wide] = (
+                jnp.dot(lts[left, core], rms[order, tt, :, wide], preferred_element_type=F32)
+                + from_core[lax.rem(index, 4), :, wide].astype(F32)
             ).astype(BF)
             return carry
 
-        lax.fori_loop(0, half_width // part, add, 0)
+        lax.fori_loop(0, cols // group, one, 0, unroll=True)
         if bits:
             pass_on(index, bits - 1)
 

time: 317 us -> 315 us (level)
  no operation moved by 1% of the time
where the time goes in v7:
time: 315 us; the launch traced here: 313 us
  Pallas kernels  293 us (93%)
  local copies, waits for them, and re-layouts  18.1 us (6%)
    pallas_call x1, Pallas kernels, run_layer(): pl.pallas_call(functools.partial(layer_kernel, n_dp, n_tensor), out_shape...  293 us
    unnamed x30, local copies, waits for them, and re-layouts  6.66 us

profile of v7, /device:TPU:0, one launch (start us, length us, event | category | flops | bytes accessed | tf_op | source)
XLA Modules:
  0.0 313.5 jit_solution(2030975303318502246)
XLA Ops:
  0.7 0.8 stack.43
  1.5 0.6 pad.4.vec_ref
  2.1 0.0 copy-start.1
  2.1 0.0 copy-start.2
  2.1 0.0 copy-start.4
  2.1 0.0 copy-start.5
  2.1 0.0 copy-start.6
  2.1 3.6 %copy_bitcast_fusion = (bf16[2,256,1024]{2,1,0:T(8,128)(2,1)}, bf16[2,256,1024]{2,1,0:T(8,128)(2,1)}) fusion(bf16[256,2,1024]{2,1,0:T(2,128)(2,1)} %param.21, bf16[256,2,1024]{2,1,0:T(2,128)(2,1)} %param.20), kind=kLoop, calls=%fused_computation.2 | loop fusion | bytes 4194304 | tf_op jit(solution)/shard_map/transpose | solution.py:1205
  5.7 0.0 copy-start.7
  5.7 0.0 copy-done.1
  5.7 0.0 copy-start.8
  5.7 0.0 copy-start.9
  5.7 0.0 copy-start.10
  5.8 0.1 copy.39
  5.9 0.0 copy-done.2
  5.9 0.0 copy-done.4
  6.0 0.1 copy.38
  6.1 0.0 copy-done.5
  6.1 0.0 copy-done.6
  6.1 0.5 copy-done.7
  6.7 1.0 pad_maximum_fusion.shard_ref
  7.7 0.0 copy-done.8
  7.7 0.0 copy-done.9
  7.7 0.0 copy-done.10
  7.7 0.6 reshape.56.bias_ref
  8.3 293.4 %encoder_layer.1 = (bf16[3,4,1024,1024]{3,2,1,0:T(8,128)(2,1)}, f32[3,128,1024]{2,1,0:T(8,128)}, f32[12,8,128]{2,1,0:T(8,128)}, bf16[2,2,256,1024]{3,2,1,0:T(8,128)(2,1)}) custom-call(s32[16]{0:T(128)} %undealing.1, s32[16]{0:T(128)} %lengths.1, f32[8,1024]{1,0:T(8,128)} %pad.4.vec_ref, bf16[2,256,1024]{2,1,0:T(8,128)(2,1)} %get-tuple-element.58.x_ref, ...), custom_call_target="tpu_custom_call" | custom-call | tf_op jit(solution)/shard_map/encoder_layer/pallas_call | solution.py:1084
  301.7 1.7 slice_bitcast_fusion
  303.5 0.0 copy-start
  303.5 2.0 copy.40
  305.5 2.0 copy.41
  307.6 0.0 copy-done
  307.6 0.0 copy-start.3
  307.6 0.9 slice_bitcast_fusion.2
  308.5 0.8 slice_bitcast_fusion.5
  309.2 0.8 copy.42
  310.0 1.0 copy.43
  311.0 0.0 copy-done.3
  311.0 0.6 slice_bitcast_fusion.6
  311.6 0.6 dynamic_slice.10
  312.2 0.6 dynamic_slice.11
  312.9 0.6 constant_dynamic-slice_fusion
  (9 shorter events, 0.1 us)
Async XLA Ops:
  2.1 3.6 %copy-start.1 = (f32[1024,128]{1,0:T(8,128)S(1)}, f32[1024,128]{1,0:T(8,128)}, u32[]{:S(2)}) copy-start(f32[1024,128]{1,0:T(8,128)} %param.29) | copy-start | bytes 1572868
  2.1 3.8 %copy-start.2 = (f32[128,1024]{1,0:T(8,128)S(1)}, f32[128,1024]{1,0:T(8,128)}, u32[]{:S(2)}) copy-start(f32[128,1024]{1,0:T(8,128)} %param.28) | copy-start | bytes 1572868
  2.1 3.9 %copy-start.4 = (f32[256,128]{1,0:T(8,128)S(1)}, f32[256,128]{1,0:T(8,128)}, u32[]{:S(2)}) copy-start(f32[256,128]{1,0:T(8,128)} %param.27) | copy-start | bytes 393220
  2.1 4.0 %copy-start.5 = (f32[128,256]{1,0:T(8,128)S(1)}, f32[128,256]{1,0:T(8,128)}, u32[]{:S(2)}) copy-start(f32[128,256]{1,0:T(8,128)} %param.26) | copy-start | bytes 393220
  2.1 4.0 %copy-start.6 = (f32[128,256]{1,0:T(8,128)S(1)}, f32[128,256]{1,0:T(8,128)}, u32[]{:S(2)}) copy-start(f32[128,256]{1,0:T(8,128)} %param.25) | copy-start | bytes 393220
  5.7 0.9 copy-start.7
  5.7 1.9 copy-start.8
  5.7 1.9 copy-start.9
  5.7 1.9 copy-start.10
  303.5 4.1 %copy-start = (f32[3,128,1024]{2,1,0:T(8,128)S(1)}, f32[3,128,1024]{2,1,0:T(8,128)}, u32[]{:S(2)}) copy-start(f32[3,128,1024]{2,1,0:T(8,128)} %get-tuple-element.21) | copy-start | bytes 4718596
  307.6 3.4 %copy-start.3 = (f32[12,8,128]{2,1,0:T(8,128)S(1)}, f32[12,8,128]{2,1,0:T(8,128)}, u32[]{:S(2)}) copy-start(f32[12,8,128]{2,1,0:T(8,128)} %get-tuple-element.22) | copy-start | bytes 147460

commit v8 on v7

--- a/solution.py
+++ b/solution.py
@@ -91,8 +91,8 @@
 SMALL = 12
 SLOTS = 6
 DEEP = 0
-PLAN = (((3, 3), (4, 4), (5, 6), (7, 8)), ((3, 4), (4, 5), (6, 7), (8, 9)))
-LAST = 9
+PLAN = (((4, 4), (5, 5), (6, 7), (8, 9)), ((4, 5), (5, 6), (7, 8), (9, 10)))
+LAST = 10
 COT_ONE, COT_TWO, X_START = 4, 9, 0
 
 
@@ -745,6 +745,10 @@
         zero = jnp.zeros((1, width), F32)
         return lax.fori_loop(0, tokens // chunk, one, (zero, zero, zero))
 
+    def run(index, carry):
+        advance(index)
+        return carry
+
     for q in range(half_t):
         for who in range(n_dp):
             landed(c_two.at[0], c2_r.at[q, who])
@@ -761,7 +765,7 @@
     keep_small(11, sums[1])
     keep_small(7, sums[2])
     turn_rows(cot_v[...], 0)
-    advance(jnp.int32(0))
+    lax.fori_loop(0, 2, run, 0)
 
     def mlp(step, carry):
         tt = rat(step)
@@ -807,7 +811,7 @@
 
         @pl.when(lax.rem(step, 2) == 1)
         def _():
-            advance(1 + lax.div(step, 2))
+            advance(2 + lax.div(step, 2))
 
         return carry
 
@@ -920,10 +924,6 @@
             return carry
 
         lax.fori_loop(0, width // 256, one, 0, unroll=True)
-
-    def run(index, carry):
-        advance(index)
-        return carry
 
     def attention(step, carry):
         @pl.when(step < n_tensor)

time: 315 us -> 324 us (1.029)
  Pallas kernels: 293 us -> 302 us
    pallas_call x1, Pallas kernels: 293 us -> 302 us  [run_layer(): pl.pallas_call(functools.partial(layer_kernel, n_dp, n_tensor), out_shape...]
where the time goes in v8:
time: 324 us; the launch traced here: 322 us
  Pallas kernels  302 us (93%)
  local copies, waits for them, and re-layouts  18.1 us (6%)
    pallas_call x1, Pallas kernels, run_layer(): pl.pallas_call(functools.partial(layer_kernel, n_dp, n_tensor), out_shape...  302 us
    unnamed x30, local copies, waits for them, and re-layouts  6.66 us

profile of v8, /device:TPU:0, one launch (start us, length us, event | category | flops | bytes accessed | tf_op | source)
XLA Modules:
  0.0 322.4 jit_solution(15049754170929493666)
XLA Ops:
  0.7 0.8 stack.43
  1.5 0.6 pad.4.vec_ref
  2.1 0.0 copy-start.1
  2.1 0.0 copy-start.2
  2.1 0.0 copy-start.4
  2.1 0.0 copy-start.5
  2.1 0.0 copy-start.6
  2.1 3.6 %copy_bitcast_fusion = (bf16[2,256,1024]{2,1,0:T(8,128)(2,1)}, bf16[2,256,1024]{2,1,0:T(8,128)(2,1)}) fusion(bf16[256,2,1024]{2,1,0:T(2,128)(2,1)} %param.21, bf16[256,2,1024]{2,1,0:T(2,128)(2,1)} %param.20), kind=kLoop, calls=%fused_computation.2 | loop fusion | bytes 4194304 | tf_op jit(solution)/shard_map/transpose | solution.py:1205
  5.7 0.0 copy-start.7
  5.7 0.0 copy-done.1
  5.7 0.0 copy-start.8
  5.7 0.0 copy-start.9
  5.7 0.0 copy-start.10
  5.8 0.1 copy.39
  5.9 0.0 copy-done.2
  5.9 0.0 copy-done.4
  6.0 0.1 copy.38
  6.1 0.0 copy-done.5
  6.1 0.0 copy-done.6
  6.1 0.5 copy-done.7
  6.7 1.0 pad_maximum_fusion.shard_ref
  7.7 0.0 copy-done.8
  7.7 0.0 copy-done.9
  7.7 0.0 copy-done.10
  7.7 0.6 reshape.56.bias_ref
  8.3 302.4 %encoder_layer.1 = (bf16[3,4,1024,1024]{3,2,1,0:T(8,128)(2,1)}, f32[3,128,1024]{2,1,0:T(8,128)}, f32[12,8,128]{2,1,0:T(8,128)}, bf16[2,2,256,1024]{3,2,1,0:T(8,128)(2,1)}) custom-call(s32[16]{0:T(128)} %undealing.1, s32[16]{0:T(128)} %lengths.1, f32[8,1024]{1,0:T(8,128)} %pad.4.vec_ref, bf16[2,256,1024]{2,1,0:T(8,128)(2,1)} %get-tuple-element.58.x_ref, ...), custom_call_target="tpu_custom_call" | custom-call | tf_op jit(solution)/shard_map/encoder_layer/pallas_call | solution.py:1084
  310.7 1.7 slice_bitcast_fusion
  312.4 0.0 copy-start
  312.4 2.0 copy.40
  314.5 2.0 copy.41
  316.5 0.0 copy-done
  316.5 0.0 copy-start.3
  316.5 0.9 slice_bitcast_fusion.2
  317.4 0.8 slice_bitcast_fusion.5
  318.2 0.8 copy.42
  318.9 1.0 copy.43
  319.9 0.0 copy-done.3
  319.9 0.6 slice_bitcast_fusion.6
  320.5 0.6 dynamic_slice.10
  321.2 0.6 dynamic_slice.11
  321.8 0.6 constant_dynamic-slice_fusion
  (9 shorter events, 0.1 us)
Async XLA Ops:
  2.1 3.6 %copy-start.1 = (f32[1024,128]{1,0:T(8,128)S(1)}, f32[1024,128]{1,0:T(8,128)}, u32[]{:S(2)}) copy-start(f32[1024,128]{1,0:T(8,128)} %param.29) | copy-start | bytes 1572868
  2.1 3.8 %copy-start.2 = (f32[128,1024]{1,0:T(8,128)S(1)}, f32[128,1024]{1,0:T(8,128)}, u32[]{:S(2)}) copy-start(f32[128,1024]{1,0:T(8,128)} %param.28) | copy-start | bytes 1572868
  2.1 3.9 %copy-start.4 = (f32[256,128]{1,0:T(8,128)S(1)}, f32[256,128]{1,0:T(8,128)}, u32[]{:S(2)}) copy-start(f32[256,128]{1,0:T(8,128)} %param.27) | copy-start | bytes 393220
  2.1 4.0 %copy-start.5 = (f32[128,256]{1,0:T(8,128)S(1)}, f32[128,256]{1,0:T(8,128)}, u32[]{:S(2)}) copy-start(f32[128,256]{1,0:T(8,128)} %param.26) | copy-start | bytes 393220
  2.1 4.0 %copy-start.6 = (f32[128,256]{1,0:T(8,128)S(1)}, f32[128,256]{1,0:T(8,128)}, u32[]{:S(2)}) copy-start(f32[128,256]{1,0:T(8,128)} %param.25) | copy-start | bytes 393220
  5.7 0.9 copy-start.7
  5.7 1.9 copy-start.8
  5.7 1.9 copy-start.9
  5.7 1.9 copy-start.10
  312.4 4.1 %copy-start = (f32[3,128,1024]{2,1,0:T(8,128)S(1)}, f32[3,128,1024]{2,1,0:T(8,128)}, u32[]{:S(2)}) copy-start(f32[3,128,1024]{2,1,0:T(8,128)} %get-tuple-element.21) | copy-start | bytes 4718596
  316.5 3.4 %copy-start.3 = (f32[12,8,128]{2,1,0:T(8,128)S(1)}, f32[12,8,128]{2,1,0:T(8,128)}, u32[]{:S(2)}) copy-start(f32[12,8,128]{2,1,0:T(8,128)} %get-tuple-element.22) | copy-start | bytes 147460
